TPU v7x, 128 devices: a whole 4x4x4 slice. The times are simulated.
128 devices in a mesh: group: 4 (over z_hi, core), tile: 32 (over x, y, z_lo).
Axes of the slice: x: 4, y: 4, z: 4 (z_hi: 2, z_lo: 2; z = z_hi * 2 + z_lo), core: 2. Of those that a mesh axis runs over, the one named last changes fastest.
Arguments:
- state: float32 [4, 32, 8, 384], P('group', 'tile'), may hold values from -6 to 6
- cotangent: float32 [4, 32, 8, 384], P('group', 'tile'), may hold values from -6 to 6
- neighbours: int32 [4, 32, 9, 384], P('group', 'tile'), may hold values from 0 to 649, as said below
- sea_cells: int32 [3, 32, 128], P(None, 'tile'), may hold values from 0 to 383, as said below
- atm_lift: bfloat16 [64, 10], replicated, may hold values from -2 to 2
- atm_conv: bfloat16 [2, 9, 64, 64], replicated, may hold values from -0.25 to 0.25
- atm_head: bfloat16 [12, 64], replicated, may hold values from -0.75 to 0.75
- ocn_lift: bfloat16 [64, 12], replicated, may hold values from -1.75 to 1.75
- ocn_conv: bfloat16 [2, 9, 64, 64], replicated, may hold values from -0.25 to 0.25
- ocn_head: bfloat16 [8, 64], replicated, may hold values from -0.75 to 0.75
Outputs:
- next_state: float32 [4, 32, 8, 384], P('group', 'tile')
- g_atm_lift: float32 [64, 10], replicated
- g_atm_conv: float32 [2, 9, 64, 64], replicated
- g_atm_head: float32 [12, 64], replicated
- g_ocn_lift: float32 [64, 12], replicated
- g_ocn_conv: float32 [2, 9, 64, 64], replicated
- g_ocn_head: float32 [8, 64], replicated
Inputs may be any that keep to these rules, and one draw needn't show every extreme that they name: For a cycle g < 3, neighbours[g, t, :, c] indexes the block's grid extended by one cell on each side (row-major, 130 columns). Entries 0 to 4 are cell c itself and its north, south, west and east cells. Entries 5 and 6 are the north-west and north-east cells or the north cell; entries 7 and 8 are the south-west and south-east cells or the south cell. neighbours[3, t, :, c] indexes ocean cells of sector t: entry 0 is c itself, every entry within 128 positions of it. sea_cells[g, t] lists 128 distinct cells of block (g, t) in increasing order; ocean cell g*128+j of sector t lies under cell sea_cells[g, t, j].
All inputs are finite; a program needn't handle non-finite values.
Results may differ from a plain program's by a relative error of at most 0.022.
Values may be sent and summed in bfloat16 or wider, within the bound.
No kernel may reach another device: no remote copies, remote signals or barrier semaphores. Data moves between devices by JAX's collectives and lax.ppermute only.
A program may use at most 128 MiB of HBM per device.

v0:
```python
import math

import jax
import jax.numpy as jnp
from jax import lax
from jax.sharding import PartitionSpec as P

STEPS = 8
LON = 128


HIGHEST = lax.Precision.HIGHEST
STENCIL = ((0, 0), (-1, 0), (1, 0), (0, -1), (0, 1), (-1, -1), (-1, 1), (1, -1), (1, 1))
FALLBACK = ((-1, 0), (-1, 0), (1, 0), (1, 0))


def extended_2(block, sides, width):
    for axis, dim in sides:
        count = lax.axis_size(axis)
        forward = [(i, i + 1) for i in range(count - 1)]
        forward.append((count - 1, 0))
        backward = [(target, source) for source, target in forward]
        low = lax.ppermute(
            lax.slice_in_dim(block, block.shape[dim] - width, None, axis=dim), axis, forward
        )
        high = lax.ppermute(lax.slice_in_dim(block, 0, width, axis=dim), axis, backward)
        block = jnp.concatenate([low, block, high], axis=dim)
    return block


def broadcast(block, axis, owner):
    block = jnp.where(lax.axis_index(axis) == owner, block, jnp.zeros_like(block))
    return lax.psum(block, axis)


def silu_slope(pre_value):
    gate_value = jax.nn.sigmoid(pre_value)
    return gate_value * (1.0 + pre_value * (1.0 - gate_value))


def flat_weight(weight):
    return jnp.transpose(weight, (1, 2, 0)).reshape(
        weight.shape[1], weight.shape[2] * weight.shape[0]
    )


def conv_ahead(extended, neighbour, weight):
    matrix = flat_weight(weight)
    block_cells = neighbour.shape[1] // 3
    results = []
    for piece_index in range(3):
        part_table = neighbour[:, piece_index * block_cells : (piece_index + 1) * block_cells]
        picked = jnp.take(extended, part_table, axis=1).reshape(-1, block_cells)
        results.append(jnp.dot(matrix, picked, preferred_element_type=jnp.float32))
    return jnp.concatenate(results, axis=1)


def conv_back(extended, neighbour, weight, slope_grad):
    matrix = flat_weight(weight)
    block_cells = neighbour.shape[1] // 3
    grad_ext = jnp.zeros(extended.shape, jnp.float32)
    grad_flat = jnp.zeros(matrix.shape, jnp.float32)
    for piece_index in range(3):
        first_cell = piece_index * block_cells
        part_table = neighbour[:, first_cell : first_cell + block_cells]
        slope_part = slope_grad[:, first_cell : first_cell + block_cells]
        picked = jnp.take(extended, part_table, axis=1).reshape(-1, block_cells)
        grad_flat = grad_flat + jnp.dot(slope_part, picked.T, preferred_element_type=jnp.float32)
        spread = jnp.dot(matrix.T, slope_part, preferred_element_type=jnp.float32)
        grad_ext = grad_ext.at[:, part_table].add(
            spread.reshape(extended.shape[0], part_table.shape[0], block_cells)
        )
    grad_weight = grad_flat.reshape(weight.shape[1], weight.shape[2], weight.shape[0]).transpose(
        2, 0, 1
    )
    return (grad_ext, grad_weight)


def corner_flags(neighbour, span):
    centre = neighbour[0]
    flags = []
    for corner in range(4):
        row_step, col_step = STENCIL[5 + corner]
        flags.append(neighbour[5 + corner] != centre + row_step * span + col_step)
    return flags


def grid_slab(grid, row_step, col_step, lat_rows, lon_cols):
    piece = grid[:, 1 + row_step : 1 + row_step + lat_rows, 1 + col_step : 1 + col_step + lon_cols]
    return piece.reshape(grid.shape[0], lat_rows * lon_cols)


def stencil_stack(extended, neighbour, lat_rows, lon_cols):
    grid = extended.reshape(extended.shape[0], lat_rows + 2, lon_cols + 2)
    flags = corner_flags(neighbour, lon_cols + 2)
    slabs = [
        grid_slab(grid, row_step, col_step, lat_rows, lon_cols)
        for row_step, col_step in STENCIL[:5]
    ]
    for corner in range(4):
        row_step, col_step = STENCIL[5 + corner]
        alt_row, alt_col = FALLBACK[corner]
        slabs.append(
            jnp.where(
                flags[corner][None, :],
                grid_slab(grid, alt_row, alt_col, lat_rows, lon_cols),
                grid_slab(grid, row_step, col_step, lat_rows, lon_cols),
            )
        )
    return (jnp.stack(slabs, axis=1).reshape(-1, lat_rows * lon_cols), flags)


def stencil_ahead(extended, neighbour, weight, lat_rows, lon_cols):
    stacked, flags = stencil_stack(extended, neighbour, lat_rows, lon_cols)
    return jnp.dot(flat_weight(weight), stacked, preferred_element_type=jnp.float32)


def place_shifted(piece, row_step, col_step, lat_rows, lon_cols):
    grid_piece = piece.reshape(piece.shape[0], lat_rows, lon_cols)
    return jnp.pad(grid_piece, ((0, 0), (1 + row_step, 1 - row_step), (1 + col_step, 1 - col_step)))


def stencil_back(extended, neighbour, weight, slope_grad, lat_rows, lon_cols):
    matrix = flat_weight(weight)
    stacked, flags = stencil_stack(extended, neighbour, lat_rows, lon_cols)
    grad_flat = jnp.dot(slope_grad, stacked.T, preferred_element_type=jnp.float32)
    spread = jnp.dot(matrix.T, slope_grad, preferred_element_type=jnp.float32)
    spread = spread.reshape(extended.shape[0], len(STENCIL), lat_rows * lon_cols)
    north_extra = jnp.zeros_like(spread[:, 0])
    south_extra = jnp.zeros_like(spread[:, 0])
    corner_parts = []
    for corner in range(4):
        term = spread[:, 5 + corner]
        moved = jnp.where(flags[corner][None, :], term, 0.0)
        corner_parts.append(term - moved)
        if corner < 2:
            north_extra = north_extra + moved
        else:
            south_extra = south_extra + moved
    pieces = [
        spread[:, 0],
        spread[:, 1] + north_extra,
        spread[:, 2] + south_extra,
        spread[:, 3],
        spread[:, 4],
    ] + corner_parts
    grad_grid = jnp.zeros((extended.shape[0], lat_rows + 2, lon_cols + 2), jnp.float32)
    for stencil_index in range(len(STENCIL)):
        row_step, col_step = STENCIL[stencil_index]
        grad_grid = grad_grid + place_shifted(
            pieces[stencil_index], row_step, col_step, lat_rows, lon_cols
        )
    grad_weight = grad_flat.reshape(weight.shape[1], weight.shape[2], weight.shape[0]).transpose(
        2, 0, 1
    )
    return (grad_grid.reshape(extended.shape[0], -1), grad_weight)


def shards(
    state,
    cotangent,
    neighbours,
    sea_cells,
    atm_lift,
    atm_conv,
    atm_head,
    ocn_lift,
    ocn_conv,
    ocn_head,
):
    field_count = state.shape[2]
    number_of_cells = state.shape[3]
    channels = atm_lift.shape[0]
    sea_count = sea_cells.shape[2]
    group_count = lax.axis_size("group")
    last_cycle = group_count - 2
    cycle_index = lax.axis_index("group")
    is_ocean = cycle_index == group_count - 1
    cycle_clipped = jnp.minimum(cycle_index, last_cycle)
    lon_cols = LON
    lat_rows = number_of_cells // lon_cols
    step_count = STEPS
    grad_scale = 1.0 / math.sqrt(group_count * lax.axis_size("tile") * number_of_cells)
    starting_variables = state[0, 0]
    neighbour = neighbours[0, 0]
    seawater_point_locator = lax.dynamic_index_in_dim(
        sea_cells[:, 0, :], cycle_clipped, 0, keepdims=False
    )

    def widen(grid_block):
        extended = extended_2(grid_block, (("group", 1), ("tile", 2)), 1)
        row_ids = lax.broadcasted_iota(jnp.int32, extended.shape, 1)
        dropped = (row_ids == 0) & (cycle_index == 0) | (row_ids == lat_rows + 1) & (
            cycle_index == last_cycle
        )
        return jnp.where(dropped, jnp.zeros_like(extended), extended).reshape(
            grid_block.shape[0], -1
        )

    def fold_back(grad_ext):
        grid_block = grad_ext.reshape(grad_ext.shape[0], lat_rows + 2, lon_cols + 2)
        outer_rim = extended_2(
            grid_block.astype(jnp.bfloat16), (("group", 1), ("tile", 2)), 1
        ).astype(grid_block.dtype)
        north_rim = jnp.where(cycle_index == 0, 0.0, outer_rim[:, 0, :])
        south_rim = jnp.where(cycle_index == last_cycle, 0.0, outer_rim[:, lat_rows + 3, :])
        inner_part = grid_block[:, 1 : lat_rows + 1, 1 : lon_cols + 1]
        inner_part = inner_part.at[:, 0, :].add(north_rim[:, 2 : lon_cols + 2])
        inner_part = inner_part.at[:, lat_rows - 1, :].add(south_rim[:, 2 : lon_cols + 2])
        inner_part = inner_part.at[:, :, 0].add(outer_rim[:, 2 : lat_rows + 2, 0])
        inner_part = inner_part.at[:, :, lon_cols - 1].add(
            outer_rim[:, 2 : lat_rows + 2, lon_cols + 3]
        )
        inner_part = inner_part.at[:, 0, 0].add(north_rim[:, 0])
        inner_part = inner_part.at[:, 0, lon_cols - 1].add(north_rim[:, lon_cols + 3])
        inner_part = inner_part.at[:, lat_rows - 1, 0].add(south_rim[:, 0])
        inner_part = inner_part.at[:, lat_rows - 1, lon_cols - 1].add(south_rim[:, lon_cols + 3])
        return inner_part.reshape(grad_ext.shape[0], number_of_cells)

    def seawater_feedback(values):
        shaped = values.reshape(values.shape[0], group_count - 1, sea_count)
        spread = broadcast(shaped, "group", group_count - 1)
        return lax.dynamic_index_in_dim(spread, cycle_clipped, 1, keepdims=False)

    seawater_skin_warmth = seawater_feedback(starting_variables[:1])[0]
    skin_warmth_map = (
        jnp.zeros((number_of_cells,), jnp.float32)
        .at[seawater_point_locator]
        .set(seawater_skin_warmth)
    )
    water_indicator = jnp.zeros((number_of_cells,), jnp.float32).at[seawater_point_locator].set(1.0)
    history = []
    present_variables = starting_variables
    flux_total = jnp.zeros((atm_head.shape[0] - field_count, number_of_cells), jnp.float32)
    for step_index in range(step_count):
        learner_feature_vector = jnp.concatenate(
            [present_variables, skin_warmth_map[None], water_indicator[None]], axis=0
        ).astype(jnp.bfloat16)
        source = learner_feature_vector
        lifted = jnp.dot(
            atm_lift, learner_feature_vector, preferred_element_type=jnp.float32
        ).astype(jnp.bfloat16)
        lifted_ext = widen(lifted.reshape(channels, lat_rows, lon_cols))
        pre_one = stencil_ahead(lifted_ext, neighbour, atm_conv[0], lat_rows, lon_cols)
        hidden_one = jax.nn.silu(pre_one).astype(jnp.bfloat16)
        hidden_ext = widen(hidden_one.reshape(channels, lat_rows, lon_cols))
        pre_two = stencil_ahead(hidden_ext, neighbour, atm_conv[1], lat_rows, lon_cols)
        hidden_two = jax.nn.silu(pre_two).astype(jnp.bfloat16)
        update = jnp.dot(atm_head, hidden_two, preferred_element_type=jnp.float32)
        history.append((source, lifted_ext, pre_one, hidden_ext, pre_two, hidden_two))
        present_variables = present_variables + update[:field_count]
        flux_total = flux_total + update[field_count:]
    flux_count = flux_total.shape[0]
    flux_sea = (flux_total[:, seawater_point_locator] / step_count).astype(jnp.bfloat16)
    outgoing = jnp.zeros((flux_count, group_count, sea_count), jnp.bfloat16)
    outgoing = outgoing.at[:, group_count - 1, :].set(flux_sea)
    incoming = lax.all_to_all(outgoing, "group", split_axis=1, concat_axis=1, tiled=True)
    ocean_flux = incoming[:, : group_count - 1, :].reshape(flux_count, number_of_cells)
    ocean_table = jnp.minimum(neighbour, number_of_cells - 1)
    ocean_inputs = jnp.concatenate([starting_variables.astype(jnp.bfloat16), ocean_flux], axis=0)
    ocean_lifted = jnp.dot(ocn_lift, ocean_inputs, preferred_element_type=jnp.float32).astype(
        jnp.bfloat16
    )
    ocean_pre_one = conv_ahead(ocean_lifted, ocean_table, ocn_conv[0])
    ocean_one = jax.nn.silu(ocean_pre_one).astype(jnp.bfloat16)
    ocean_pre_two = conv_ahead(ocean_one, ocean_table, ocn_conv[1])
    ocean_two = jax.nn.silu(ocean_pre_two).astype(jnp.bfloat16)
    ocean_next = starting_variables + jnp.dot(
        ocn_head, ocean_two, preferred_element_type=jnp.float32
    )
    ocean_head_grad = (cotangent[0, 0] * grad_scale).astype(jnp.bfloat16)
    ocean_head_weight = jnp.dot(ocean_head_grad, ocean_two.T, preferred_element_type=jnp.float32)
    ocean_grad_two = jnp.dot(ocn_head.T, ocean_head_grad, preferred_element_type=jnp.float32)
    ocean_slope_two = (ocean_grad_two * silu_slope(ocean_pre_two)).astype(jnp.bfloat16)
    ocean_grad_one, ocean_conv_two = conv_back(ocean_one, ocean_table, ocn_conv[1], ocean_slope_two)
    ocean_slope_one = (ocean_grad_one * silu_slope(ocean_pre_one)).astype(jnp.bfloat16)
    ocean_grad_lifted, ocean_conv_one = conv_back(
        ocean_lifted, ocean_table, ocn_conv[0], ocean_slope_one
    )
    ocean_lift_weight = jnp.dot(
        ocean_grad_lifted, ocean_inputs.astype(jnp.float32).T, precision=HIGHEST
    )
    ocean_grad_inputs = jnp.dot(
        ocn_lift.astype(jnp.float32).T, ocean_grad_lifted, precision=HIGHEST
    )
    flux_sea_grad = seawater_feedback(ocean_grad_inputs[field_count:]) / step_count
    flux_grad = (
        jnp.zeros((flux_count, number_of_cells), jnp.float32)
        .at[:, seawater_point_locator]
        .set(flux_sea_grad)
    )
    lift_f32 = atm_lift.astype(jnp.float32)
    state_grad = cotangent[0, 0] * grad_scale
    lift_total = jnp.zeros(atm_lift.shape, jnp.float32)
    conv_one_total = jnp.zeros(atm_conv.shape[1:], jnp.float32)
    conv_two_total = jnp.zeros(atm_conv.shape[1:], jnp.float32)
    head_total = jnp.zeros(atm_head.shape, jnp.float32)
    for step_index in reversed(range(step_count)):
        source, lifted_ext, pre_one, hidden_ext, pre_two, hidden_two = history[step_index]
        head_grad = jnp.concatenate([state_grad, flux_grad], axis=0).astype(jnp.bfloat16)
        head_total = head_total + jnp.dot(
            head_grad, hidden_two.T, preferred_element_type=jnp.float32
        )
        grad_hidden_two = jnp.dot(atm_head.T, head_grad, preferred_element_type=jnp.float32)
        slope_two = (grad_hidden_two * silu_slope(pre_two)).astype(jnp.bfloat16)
        grad_ext_two, conv_grad_two = stencil_back(
            hidden_ext, neighbour, atm_conv[1], slope_two, lat_rows, lon_cols
        )
        grad_hidden_one = fold_back(grad_ext_two)
        slope_one = (grad_hidden_one * silu_slope(pre_one)).astype(jnp.bfloat16)
        grad_ext_one, conv_grad_one = stencil_back(
            lifted_ext, neighbour, atm_conv[0], slope_one, lat_rows, lon_cols
        )
        conv_one_total = conv_one_total + conv_grad_one
        conv_two_total = conv_two_total + conv_grad_two
        grad_lifted = fold_back(grad_ext_one)
        lift_total = lift_total + jnp.dot(
            grad_lifted, source.astype(jnp.float32).T, precision=HIGHEST
        )
        grad_source = jnp.dot(lift_f32.T, grad_lifted, precision=HIGHEST)
        state_grad = state_grad + grad_source[:field_count]
    atm_keep = jnp.logical_not(is_ocean)

    def keep_only(flag, amount):
        return jnp.where(flag, amount, jnp.zeros_like(amount))

    totals = lax.psum(
        (
            keep_only(atm_keep, lift_total),
            keep_only(atm_keep, jnp.stack([conv_one_total, conv_two_total])),
            keep_only(atm_keep, head_total),
            keep_only(is_ocean, ocean_lift_weight),
            keep_only(is_ocean, jnp.stack([ocean_conv_one, ocean_conv_two])),
            keep_only(is_ocean, ocean_head_weight),
        ),
        ("group", "tile"),
    )
    next_state = jnp.where(is_ocean, ocean_next, present_variables)[None, None]
    return (next_state, totals[0], totals[1], totals[2], totals[3], totals[4], totals[5])


def solution(mesh):
    return jax.shard_map(
        shards,
        mesh=mesh,
        in_specs=(
            P("group", "tile", None, None),
            P("group", "tile", None, None),
            P("group", "tile", None, None),
            P(None, "tile", None),
            P(),
            P(),
            P(),
            P(),
            P(),
            P(),
        ),
        out_specs=(P("group", "tile", None, None), P(), P(), P(), P(), P(), P()),
        check_vma=False,
    )
```

profile of v0, /device:TPU:1, one launch (start us, length us, event | category | flops | bytes accessed | tf_op | source)
XLA Modules:
  0.0 974.8 jit_solution(11988739772936810407)
XLA Ops:
  10.3 8.8 psum.56
  47.5 5.7 collective-permute-start.7
  65.6 5.7 collective-permute-start.11
  83.5 5.7 collective-permute-start.15
  101.6 5.7 collective-permute-start.19
  119.0 5.7 collective-permute-start.23
  136.9 5.9 collective-permute-start.27
  154.6 5.7 collective-permute-start.31
  172.1 5.7 collective-permute-start.35
  267.1 6.6 collective-permute-done.53
  274.1 5.8 collective-permute-start.55
  288.3 6.3 collective-permute-done.57
  311.6 7.3 collective-permute-start.63
  325.7 6.7 all-to-all-start
  362.9 9.0 scatter_custom_fusion.2
  372.2 9.9 %scatter_fusion = f32[64,384]{0,1:T(8,128)S(1)} fusion(f32[64,384]{0,1:T(8,128)S(1)} %scatter_custom_fusion.2, s32[1152]{0:T(1024)S(1)} %get-tuple-element.2161, f32[1152,64]{1,0:T(8,128)S(1)} %bitcast.2063), kind=kCustom, calls=%fused_computation.10 | custom fusion | flops 73728 | bytes 889344 | tf_op jit(solution)/shard_map/scatter-add | solution.py:70
  382.1 10.1 %scatter_fusion.1 = f32[64,384]{0,1:T(8,128)S(1)} fusion(f32[64,384]{0,1:T(8,128)S(1)} %scatter_fusion, s32[1152]{0:T(1024)S(1)} %get-tuple-element.2160, f32[1152,64]{1,0:T(8,128)S(1)} %bitcast.2061), kind=kCustom, calls=%fused_computation.11 | custom fusion | flops 73728 | bytes 889344 | tf_op jit(solution)/shard_map/scatter-add | solution.py:70
  393.5 9.0 scatter_custom_fusion.5
  402.9 9.5 scatter_fusion.2
  412.4 10.2 %scatter_fusion.3 = f32[64,384]{0,1:T(8,128)S(1)} fusion(f32[64,384]{0,1:T(8,128)S(1)} %scatter_fusion.2, s32[1152]{0:T(1024)S(1)} %get-tuple-element.2160, f32[1152,64]{1,0:T(8,128)S(1)} %bitcast.2060), kind=kCustom, calls=%fused_computation.14 | custom fusion | flops 73728 | bytes 889344 | tf_op jit(solution)/shard_map/scatter-add | solution.py:70
  425.5 7.3 psum.57
  447.4 6.8 collective-permute-start.67
  497.1 6.5 collective-permute-start.75
  547.4 6.3 collective-permute-start.83
  596.3 6.1 collective-permute-start.91
  644.9 5.9 collective-permute-start.99
  668.9 6.1 collective-permute-start.103
  693.7 5.7 collective-permute-start.107
  743.5 6.1 collective-permute-start.115
  792.1 6.9 collective-permute-start.123
  829.3 66.3 %all-reduce.145 = (f32[64,10]{0,1:T(8,128)}, f32[12,64]{1,0:T(8,128)}, f32[64,12]{0,1:T(8,128)}, f32[8,64]{1,0:T(8,128)}) all-reduce(f32[64,10]{0,1:T(8,128)S(1)} %fusion.33, f32[12,64]{1,0:T(8,128)S(1)} %fusion.32, f32[64,12]{0,1:T(8,128)S(1)} %copy-done.144, ...), channel_id=1, replica_groups=mesh['group'=4,'tile'=32] {'group','tile'}, use_global_device_ids=true, to_apply=%region_12.14 | all-reduce | flops 2688 | bytes 21504 | tf_op jit(solution)/shard_map/psum | solution.py:327
  895.6 69.4 %all-reduce.149.cloned.1.call-done = (f32[2,9,64,64]{3,2,1,0:T(8,128)}, f32[2,9,64,64]{3,2,1,0:T(8,128)}) async-done(((f32[2,9,64,64]{3,2,1,0:T(8,128)}, f32[2,9,64,64]{3,2,1,0:T(8,128)}), (f32[2,9,64,64]{3,2,1,0:T(8,128)}, f32[2,9,64,64]{3,2,1,0:T(8,128)})) %all-reduce.149.cloned.1.call-update) | async-done | bytes 589840 | tf_op jit(solution)/shard_map/psum | solution.py:327
  (1647 shorter events, 608.8 us)
Async XLA Ops:
  29.7 9.4 collective-permute-start.2
  47.4 9.0 collective-permute-start.6
  47.5 8.9 collective-permute-start.7
  83.4 9.0 collective-permute-start.14
  83.5 8.9 collective-permute-start.15
  101.5 8.7 collective-permute-start.18
  101.6 8.6 collective-permute-start.19
  118.9 8.8 collective-permute-start.22
  119.0 8.7 collective-permute-start.23
  136.9 8.6 collective-permute-start.26
  136.9 8.5 collective-permute-start.27
  154.5 8.9 collective-permute-start.30
  154.6 8.8 collective-permute-start.31
  184.4 9.2 collective-permute-start.37
  244.1 8.7 collective-permute-start.49
  264.5 9.3 collective-permute-start.53
  274.0 9.4 collective-permute-start.54
  274.1 9.3 collective-permute-start.55
  294.8 9.0 collective-permute-start.58
  294.9 8.9 collective-permute-start.59
  311.5 9.7 collective-permute-start.62
  311.6 9.6 collective-permute-start.63
  325.7 11.2 %all-to-all-start = ((bf16[4,4,128]{2,0,1:T(4,128)(2,1)}), bf16[4,4,128]{2,0,1:T(4,128)(2,1)S(1)}, u32[]{:S(2)}, u32[]{:S(2)}) async-start(bf16[4,4,128]{2,0,1:T(4,128)(2,1)} %scatter.28.clone), calls=%async_computation | async-start | bytes 8192 | tf_op jit(solution)/shard_map/all_to_all | solution.py:257
  332.4 632.6 %all-reduce.149.cloned.1.call-start = ((), (), s32[]{:S(2)}) async-start(), calls=%async_computation.1 | async-start | bytes 2359296 | tf_op jit(solution)/shard_map/psum | solution.py:327
  447.4 9.0 collective-permute-start.66
  447.4 8.9 collective-permute-start.67
  497.1 8.7 collective-permute-start.74
  497.1 8.6 collective-permute-start.75
  547.3 8.5 collective-permute-start.82
  547.4 8.4 collective-permute-start.83
  792.0 9.1 collective-permute-start.122
  792.1 9.0 collective-permute-start.123
  (275 other events, 5808.7 us)
Sparse Core Ops, SparseCore 0:
  822.8 142.1 all-reduce.148
where the time goes:
time: 984 us; the launch traced here: 975 us
  waiting for transfers between devices  286 us (29%)
  starting transfers between devices  264 us (27%)
  local copies, waits for them, and re-layouts  145 us (15%)
  other arithmetic  122 us (12%)
  blocking collectives  82.4 us (8%)
  matrix products  53 us (5%)
  between operations  21.8 us (2%)
    ppermute x64, starting transfers between devices, extended_2(): lax.ppermute(lax.slice_in_dim(block, 0, width, axis=dim), axis, backward)  210 us
    ppermute x64, waiting for transfers between devices, extended_2(): lax.ppermute(lax.slice_in_dim(block, 0, width, axis=dim), axis, backward)  129 us
    ppermute x64, waiting for transfers between devices, extended_2(): lax.ppermute(lax.slice_in_dim(block, block.shape[dim] - width, None, axis...  84.9 us
    psum x1, waiting for transfers between devices, shards(): lax.psum((keep_only(atm_keep, lift_total), keep_only(atm_keep, jnp.stack(...  69.4 us
    psum x1, blocking collectives, shards(): lax.psum((keep_only(atm_keep, lift_total), keep_only(atm_keep, jnp.stack(...  66.3 us
    scatter-add x6, other arithmetic, conv_back(): grad_ext.at[:, part_table]  57.7 us
    ppermute x64, starting transfers between devices, extended_2(): lax.ppermute(lax.slice_in_dim(block, block.shape[dim] - width, None, axis...  47.1 us
    slice x16, local copies, waits for them, and re-layouts, stencil_back(): spread[:, 0]  36.9 us
  transfers between devices with their start and end apart: 130, of which 97 were waited for; matrix products, arithmetic and copies ran while one was open for 4% of the time, Pallas kernels for 0%

commit v1 on v0

v1 whole, which is shorter than its diff:
```python
import functools
import math

import jax
import jax.numpy as jnp
from jax import lax
from jax.experimental import pallas as pl
from jax.experimental.pallas import tpu as pltpu
from jax.sharding import PartitionSpec as P

STEPS = 8
LON = 128
ROWS = 9
CELLS = 384
WIN = ROWS * LON
K = 9
CH = 64
HALO = 32
WIRE = 512
BOTH = ("group", "tile")
BF = jnp.bfloat16
F32 = jnp.float32
INTERPRET = False
VMEM_LIMIT = 48 * 1024 * 1024

NN = (((1,), (0,)), ((), ()))
NT = (((1,), (1,)), ((), ()))


def dot(a, b, dims=NN):
    return lax.dot_general(a, b, dims, preferred_element_type=F32)


def call(body, outs, scratch=(), grid=(), in_specs=None, out_specs=None):
    vmem = pl.BlockSpec(memory_space=pltpu.VMEM)
    extra = {}
    if grid:
        extra = {"grid": grid, "in_specs": in_specs, "out_specs": out_specs}
    elif in_specs is not None:
        extra = {"in_specs": in_specs, "out_specs": [vmem] * len(outs)}
    return pl.pallas_call(
        body,
        out_shape=[jax.ShapeDtypeStruct(shape, dtype) for shape, dtype in outs],
        scratch_shapes=list(scratch),
        interpret=INTERPRET,
        compiler_params=pltpu.CompilerParams(vmem_limit_bytes=VMEM_LIMIT),
        **extra,
    )


def smem():
    return pl.BlockSpec(memory_space=pltpu.SMEM)


def vmem():
    return pl.BlockSpec(memory_space=pltpu.VMEM)


def lane_ids(shape):
    return lax.broadcasted_iota(jnp.int32, shape, len(shape) - 1)


def sigmoid(value):
    return 0.5 * jnp.tanh(0.5 * value) + 0.5


def seg(row):
    return slice(row * LON, (row + 1) * LON)


def pack_strip(read, half, shape):
    start = jnp.where(half == 0, 0, LON - HALO)
    quarter = lane_ids(shape) // HALO
    packed = []
    for block in range(3):
        total = jnp.zeros(shape, F32)
        for place in range(4):
            row = 4 * block + place
            if row < ROWS:
                moved = pltpu.roll(read(row), lax.rem(HALO * place - start + 2 * LON, LON), 1)
                total = jnp.where(quarter == place, moved, total)
        packed.append(total)
    return packed


def to_window(own, strip, row, half):
    place = row % 4
    lanes = lane_ids(own.shape)
    target = jnp.where(half == 0, LON - HALO, 0)
    moved = pltpu.roll(strip, lax.rem(target - HALO * place + 2 * LON, LON), 1)
    outside = (lanes >= target) & (lanes < target + HALO)
    merged = jnp.where(outside, moved, own)
    return pltpu.roll(merged, jnp.where(half == 0, HALO, LON - HALO), 1)


def pack_kernel(ids, state, cotangent, table, out):
    ocean = ids[0] == 3
    out[0:8, :] = state[...]
    out[8:16, :] = cotangent[...]
    entries = table[...]
    north = (entries[5:7] == entries[1:2]).astype(F32)
    south = (entries[7:9] == entries[2:3]).astype(F32)
    flags = jnp.concatenate(
        [jnp.zeros((2, CELLS), F32), north, south, jnp.zeros((3, CELLS), F32)], axis=0
    )
    chosen = jnp.where(ocean, entries.astype(F32), flags)
    out[16:32, :] = jnp.concatenate([chosen, jnp.zeros((7, CELLS), F32)], axis=0)


def one_hot_sea(sea_row):
    cells = lax.broadcasted_iota(jnp.int32, (CELLS, LON), 0)
    return jnp.where(cells == sea_row, 1.0, 0.0).astype(BF)


def sector_kernel(ids, gathered, sea, features, strip):
    half = ids[0] % 2
    for cycle in range(3):
        cols = slice(cycle * CELLS, (cycle + 1) * CELLS)
        features[0:16, cols] = gathered[cycle, 0:16, :]
        warm = gathered[3, 0:8, cycle * LON : (cycle + 1) * LON]
        row_ids = lax.broadcasted_iota(jnp.int32, (8, LON), 0)
        sources = jnp.where(row_ids == 0, warm[0:1], jnp.where(row_ids == 1, 1.0, 0.0))
        sources = jnp.concatenate([sources, jnp.zeros((8, LON), F32)], axis=0).astype(BF)
        placed = dot(sources, one_hot_sea(sea[cycle]), NT)[0:8]
        wide_ids = lax.broadcasted_iota(jnp.int32, (8, CELLS), 0)
        features[16:24, cols] = jnp.where(wide_ids < 2, placed, gathered[cycle, 16:24, :])
    packed = pack_strip(lambda row: features[:, seg(row)], half, (24, LON))
    for block in range(3):
        strip[:, seg(block)] = packed[block]


def build_columns(out, rows, flags):
    mid = [piece.astype(BF) for piece in rows]
    west = [pltpu.roll(piece, 1, 1).astype(BF) for piece in rows]
    east = [pltpu.roll(piece, LON - 1, 1).astype(BF) for piece in rows]
    zero = jnp.zeros((CH, LON), BF)
    for row in range(ROWS):
        up = row - 1
        down = row + 1
        north = mid[up] if up >= 0 else zero
        south = mid[down] if down < ROWS else zero
        taps = [mid[row], north, south, west[row], east[row]]
        corners = (
            (west[up], east[up]) if up >= 0 else (zero, zero),
            (west[down], east[down]) if down < ROWS else (zero, zero),
        )
        for corner in range(4):
            base = north if corner < 2 else south
            side = corners[corner // 2][corner % 2]
            flag = flags[corner : corner + 1, seg(row)] > 0.5
            taps.append(jnp.where(flag, base, side))
        for k in range(K):
            out[k * CH : (k + 1) * CH, seg(row)] = taps[k]


def spread_back(spread, flags):
    results = []
    for row in range(ROWS):
        def part(k, at):
            return spread[k * CH : (k + 1) * CH, seg(at)]

        mid = part(0, row)
        west = part(3, row)
        east = part(4, row)
        for at, straight, left, right in ((row + 1, 1, 5, 6), (row - 1, 2, 7, 8)):
            if 0 <= at < ROWS:
                corner = left - 5
                flag_left = flags[corner : corner + 1, seg(at)] > 0.5
                flag_right = flags[corner + 1 : corner + 2, seg(at)] > 0.5
                term_left = part(left, at)
                term_right = part(right, at)
                mid = mid + part(straight, at)
                mid = mid + jnp.where(flag_left, term_left, 0.0)
                mid = mid + jnp.where(flag_right, term_right, 0.0)
                west = west + jnp.where(flag_left, 0.0, term_left)
                east = east + jnp.where(flag_right, 0.0, term_right)
        results.append(mid + pltpu.roll(west, LON - 1, 1) + pltpu.roll(east, 1, 1))
    return results


def forward_kernel(
    ids, features, strip, lift, flat, head,
    inputs_out, source_out, gate_one, gate_two, last_out, window_out, final_out,
    window, total, columns,
):
    step = pl.program_id(0)
    half = ids[0] % 2
    first = ids[0] // 2 == 0

    @pl.when(step == 0)
    def _():
        for row in range(ROWS):
            block = row // 4
            window[:, seg(row)] = to_window(features[:, seg(row)], strip[:, seg(block)], row, half)
        total[0:8, :] = window[0:8, :]
        total[8:16, :] = jnp.zeros((8, WIN), F32)
        window_out[...] = window[8:24, :]

    flags = window[18:22, :]
    row_ids = lax.broadcasted_iota(jnp.int32, (8, WIN), 0)
    surface = window[16:24, :]
    surface = jnp.where(row_ids < 2, surface, 0.0)
    inputs = jnp.concatenate([total[0:8, :], surface], axis=0).astype(BF)
    inputs_out[0] = inputs
    lifted = dot(lift[...], inputs)
    build_columns(columns, [lifted[:, seg(row)] for row in range(ROWS)], flags)
    pre = dot(flat[0], columns[...])
    gate = sigmoid(pre)
    hidden = pre * gate
    gate_one[0] = (gate + hidden - hidden * gate).astype(BF)
    source_out[0] = jnp.where(first, lifted, hidden).astype(BF)
    build_columns(columns, [hidden[:, seg(row)] for row in range(ROWS)], flags)
    pre = dot(flat[1], columns[...])
    gate = sigmoid(pre)
    hidden = pre * gate
    gate_two[0] = (gate + hidden - hidden * gate).astype(BF)
    hidden = hidden.astype(BF)
    last_out[0] = hidden
    total[...] = total[...] + dot(head[...], hidden)

    @pl.when(step == STEPS - 1)
    def _():
        for row in range(ROWS):
            shift = jnp.where(half == 0, LON - HALO, HALO)
            final_out[:, seg(row)] = pltpu.roll(total[:, seg(row)], shift, 1)


def ocean_kernel(
    scale, ids, gathered, own, other, sea, lift, flat, head, lift_back, flat_back, head_back,
    next_state, flux_grad, strip, wire,
    hot, columns, scatter,
):
    group = ids[0]
    half = group % 2
    first = group // 2 == 0
    lanes = lane_ids((16, WIN))
    mine = ((lanes % LON) // (LON // 2)) == half
    merged = jnp.where(mine, own[...], other[...])
    flux = (merged[8:16, :] * (1.0 / STEPS)).astype(BF)
    flux = jnp.concatenate([flux, flux], axis=0)
    hot_sea = [one_hot_sea(sea[cycle]) for cycle in range(3)]
    forcing = [
        dot(flux[:, cycle * CELLS : (cycle + 1) * CELLS], hot_sea[cycle])[0:8] for cycle in range(3)
    ]
    forcing = jnp.concatenate(forcing, axis=1)
    fields = gathered[3, 0:8, :]
    inputs = jnp.concatenate([fields, forcing], axis=0).astype(BF)
    cell_ids = lax.broadcasted_iota(jnp.int32, (CELLS, CELLS), 0)
    for k in range(K):
        table = gathered[3, 16 + k : 17 + k, :].astype(jnp.int32)
        hot[k] = jnp.where(cell_ids == table, 1.0, 0.0).astype(BF)

    def gather(at, value):
        for k in range(K):
            columns[at, k * CH : (k + 1) * CH, :] = dot(value, hot[k]).astype(BF)

    def spread(index, slope):
        scatter[...] = dot(flat_back[index], slope).astype(BF)
        result = jnp.zeros((CH, CELLS), F32)
        for k in range(K):
            result = result + dot(scatter[k * CH : (k + 1) * CH, :], hot[k], NT)
        return result

    lifted = dot(lift[...], inputs).astype(BF)
    gather(0, lifted)
    pre = dot(flat[0], columns[0])
    gate = sigmoid(pre)
    hidden = pre * gate
    slope_of_one = gate + hidden - hidden * gate
    gather(1, hidden.astype(BF))
    pre = dot(flat[1], columns[1])
    gate = sigmoid(pre)
    hidden = pre * gate
    slope_of_two = gate + hidden - hidden * gate
    hidden = hidden.astype(BF)
    ocean_next = fields + dot(head[...], hidden)[0:8]
    block = jnp.where(group == 0, merged[0:8, 0:CELLS], ocean_next)
    block = jnp.where(group == 1, merged[0:8, CELLS : 2 * CELLS], block)
    next_state[...] = jnp.where(group == 2, merged[0:8, 2 * CELLS : 3 * CELLS], block)

    head_grad = gathered[3, 8:16, :] * scale
    head_grad = jnp.concatenate([head_grad, jnp.zeros((8, CELLS), F32)], axis=0).astype(BF)
    head_weight = dot(head_grad, hidden, NT)
    slope_two = (dot(head_back[...], head_grad) * slope_of_two).astype(BF)
    slope_one = (spread(1, slope_two) * slope_of_one).astype(BF)
    grad_lifted = spread(0, slope_one).astype(BF)
    lift_weight = dot(inputs, grad_lifted, NT)
    forcing_grad = dot(lift_back[...], grad_lifted)[8:16]
    forcing_grad = (forcing_grad * (1.0 / STEPS)).astype(BF)
    forcing_grad = jnp.concatenate([forcing_grad, forcing_grad], axis=0)
    for cycle in range(3):
        part = forcing_grad[:, cycle * LON : (cycle + 1) * LON]
        flux_grad[:, cycle * CELLS : (cycle + 1) * CELLS] = dot(part, hot_sea[cycle], NT)[0:8]
    packed = pack_strip(lambda row: flux_grad[:, seg(row)], half, (8, LON))
    for place in range(3):
        strip[:, seg(place)] = packed[place]

    slope = jnp.where(first, slope_one.astype(F32), slope_two.astype(F32)).astype(BF)
    chosen = jnp.where(first, 0, 1)
    weight = jnp.transpose(dot(columns[chosen], slope, NT))
    weight = jnp.where(half == 0, weight[0:32], weight[32:64])
    for j in range(4):
        wire[32 * j : 32 * j + 32, :] = weight[:, seg(j)]
    rest = weight[:, 512:576]
    wire[128:144, :] = jnp.concatenate([rest[0:16], rest[16:32]], axis=1)
    wire[144:160, :] = jnp.concatenate([lift_weight, head_weight], axis=1)


def backward_kernel(
    scale, ids, window, flux_own, flux_strip, ocean_wire, flat_back, head_back, lift_back,
    inputs, source, gate_one, gate_two, last,
    wire,
    state_grad, flux_grad, weight_total, small_total, columns, spread,
):
    step = pl.program_id(0)
    half = ids[0] % 2
    first = ids[0] // 2 == 0

    @pl.when(step == 0)
    def _():
        state_grad[...] = window[0:8, :] * scale
        for row in range(ROWS):
            place = row // 4
            flux_grad[:, seg(row)] = to_window(
                flux_own[:, seg(row)], flux_strip[:, seg(place)], row, half
            )
        weight_total[...] = jnp.zeros_like(weight_total)
        small_total[...] = jnp.zeros_like(small_total)

    flags = window[10:14, :]

    def owned(shape):
        lanes = lane_ids(shape) % LON
        return (lanes >= HALO) & (lanes < LON - HALO)

    def mask(value):
        return jnp.where(owned(value.shape), value, 0.0)

    head_grad = jnp.concatenate([state_grad[...], flux_grad[...]], axis=0)
    hidden = last[0]
    grad_two = dot(head_back[...], head_grad.astype(BF))
    slope_two = grad_two * gate_two[0].astype(F32)
    spread[...] = dot(flat_back[1], slope_two.astype(BF))
    grad_one = jnp.concatenate(spread_back(spread, flags), axis=1)
    slope_one = grad_one * gate_one[0].astype(F32)
    spread[...] = dot(flat_back[0], slope_one.astype(BF))
    grad_lifted = jnp.concatenate(spread_back(spread, flags), axis=1)
    lift_weight = dot(inputs[0], mask(grad_lifted).astype(BF), NT)
    head_weight = dot(mask(head_grad).astype(BF), hidden, NT)
    small_total[...] += jnp.concatenate([lift_weight, head_weight], axis=1)
    state_grad[...] += dot(lift_back[...], grad_lifted.astype(BF))[0:8]
    slope = mask(jnp.where(first, slope_one, slope_two)).astype(BF)
    values = source[0].astype(F32)
    build_columns(columns, [values[:, seg(row)] for row in range(ROWS)], flags)
    weight_total[...] += dot(columns[...], slope, NT)

    @pl.when(step == STEPS - 1)
    def _():
        weight = jnp.transpose(weight_total[...])
        for j in range(4):
            wire[64 * j : 64 * j + 64, :] = weight[:, seg(j)]
        rest = weight[:, 512:576]
        wire[256:288, :] = jnp.concatenate([rest[0:32], rest[32:64]], axis=1)
        wire[288:304, :] = small_total[...]
        wire[304:464, :] = ocean_wire[...]
        wire[464:512, :] = jnp.zeros((48, LON), F32)


def sum_kernel(sectors, rows, parts, out):
    sums = []
    for group in range(4):
        total = parts[group * sectors]
        for sector in range(1, sectors):
            total = total + parts[group * sectors + sector]
        sums.append(total)
    sums = jnp.concatenate(sums, axis=0).astype(BF)
    for place in range(4 * sectors):
        out[place] = sums


def final_kernel(
    rows, parts, g_lift, g_conv, g_head, o_lift, o_conv, o_head, sums
):
    places = WIRE // rows
    for place in range(places):
        piece = parts[place].astype(F32)
        for group in range(4):
            sums[group, place * rows : (place + 1) * rows, :] = piece[group * rows : (group + 1) * rows]
    for index in range(2):
        low, high = 2 * index, 2 * index + 1
        for j in range(4):
            pair = sums[low, 64 * j : 64 * j + 64, :] + sums[high, 64 * j : 64 * j + 64, :]
            g_conv[index, 2 * j] = pair[:, 0:64]
            g_conv[index, 2 * j + 1] = pair[:, 64:128]
            upper = sums[low, 304 + 32 * j : 336 + 32 * j, :]
            lower = sums[high, 304 + 32 * j : 336 + 32 * j, :]
            o_conv[index, 2 * j, 0:32] = upper[:, 0:64]
            o_conv[index, 2 * j, 32:64] = lower[:, 0:64]
            o_conv[index, 2 * j + 1, 0:32] = upper[:, 64:128]
            o_conv[index, 2 * j + 1, 32:64] = lower[:, 64:128]
        pair = sums[low, 256:288, :] + sums[high, 256:288, :]
        g_conv[index, 8, 0:32] = pair[:, 0:64]
        g_conv[index, 8, 32:64] = pair[:, 64:128]
        for side, at in ((low, 0), (high, 32)):
            piece = sums[side, 432:448, :]
            o_conv[index, 8, at : at + 16] = piece[:, 0:64]
            o_conv[index, 8, at + 16 : at + 32] = piece[:, 64:128]
    small = sums[0, 288:304, :] + sums[1, 288:304, :]
    g_lift[...] = jnp.transpose(small[:, 0:64])[:, 0:10]
    g_head[...] = small[0:12, 64:128]
    small = sums[0, 448:464, :]
    o_lift[...] = jnp.transpose(small[:, 0:64])[:, 0:12]
    o_head[...] = small[0:8, 64:128]


def padded(array, rows, columns):
    return jnp.pad(array, ((0, rows - array.shape[0]), (0, columns - array.shape[1])))


def shards(
    state,
    cotangent,
    neighbours,
    sea_cells,
    atm_lift,
    atm_conv,
    atm_head,
    ocn_lift,
    ocn_conv,
    ocn_head,
):
    sectors = lax.axis_size("tile")
    devices = 4 * sectors
    rows = WIRE // devices
    scale = 1.0 / math.sqrt(devices * CELLS)
    group = lax.axis_index("group")
    ids = group.astype(jnp.int32).reshape(1)

    partner = []
    beside = []
    for g in range(4):
        for t in range(sectors):
            partner.append((g * sectors + t, (g ^ 1) * sectors + t))
            other = (t + 1) % sectors if g % 2 else (t - 1) % sectors
            beside.append((g * sectors + t, (g ^ 1) * sectors + other))

    lift = padded(atm_lift, CH, 16)
    lift_back = padded(atm_lift.T, 16, CH)
    head = padded(atm_head, 16, CH)
    head_back = padded(atm_head.T, CH, 16)
    flat = jnp.transpose(atm_conv, (0, 2, 1, 3)).reshape(2, CH, K * CH)
    flat_back = jnp.transpose(atm_conv, (0, 1, 3, 2)).reshape(2, K * CH, CH)
    ocean_lift = padded(ocn_lift, CH, 16)
    ocean_lift_back = padded(ocn_lift.T, 16, CH)
    ocean_head = padded(ocn_head, 16, CH)
    ocean_head_back = padded(ocn_head.T, CH, 16)
    ocean_flat = jnp.transpose(ocn_conv, (0, 2, 1, 3)).reshape(2, CH, K * CH)
    ocean_flat_back = jnp.transpose(ocn_conv, (0, 1, 3, 2)).reshape(2, K * CH, CH)

    (packed,) = call(
        pack_kernel, [((32, CELLS), F32)], in_specs=[smem(), vmem(), vmem(), vmem()]
    )(ids, state[0, 0], cotangent[0, 0], neighbours[0, 0])
    gathered = lax.all_gather(packed, "group")
    features, strip = call(
        sector_kernel,
        [((24, WIN), F32), ((24, CELLS), F32)],
        in_specs=[smem(), vmem(), vmem()],
    )(ids, gathered, sea_cells)
    strip = lax.ppermute(strip, BOTH, beside)

    def whole(shape):
        return pl.BlockSpec(shape, lambda s: (0,) * len(shape))

    def at_step(shape):
        return pl.BlockSpec((1,) + shape, lambda s: (s, 0, 0))

    def at_step_back(shape):
        return pl.BlockSpec((1,) + shape, lambda s: (STEPS - 1 - s, 0, 0))

    wide = (CH, WIN)
    history = [(16, WIN), wide, wide, wide, wide]
    inputs, source, gate_one, gate_two, last, window, final = call(
        forward_kernel,
        [((STEPS,) + shape, BF) for shape in history] + [((16, WIN), F32), ((16, WIN), F32)],
        scratch=[
            pltpu.VMEM((24, WIN), F32),
            pltpu.VMEM((16, WIN), F32),
            pltpu.VMEM((K * CH, WIN), BF),
        ],
        grid=(STEPS,),
        in_specs=[
            smem(),
            whole((24, WIN)),
            whole((24, CELLS)),
            whole((CH, 16)),
            whole((2, CH, K * CH)),
            whole((16, CH)),
        ],
        out_specs=[at_step(shape) for shape in history] + [whole((16, WIN)), whole((16, WIN))],
    )(ids, features, strip, lift, flat, head)

    other_final = lax.ppermute(final, BOTH, partner)
    next_state, flux_grad, flux_strip, ocean_wire = call(
        functools.partial(ocean_kernel, scale),
        [((8, CELLS), F32), ((8, WIN), F32), ((8, CELLS), F32), ((160, LON), F32)],
        scratch=[
            pltpu.VMEM((K, CELLS, CELLS), BF),
            pltpu.VMEM((2, K * CH, CELLS), BF),
            pltpu.VMEM((K * CH, CELLS), BF),
        ],
        in_specs=[smem()] + [vmem()] * 10,
    )(
        ids, gathered, final, other_final, sea_cells, ocean_lift, ocean_flat, ocean_head,
        ocean_lift_back, ocean_flat_back, ocean_head_back,
    )
    flux_strip = lax.ppermute(flux_strip, BOTH, beside)

    (wire,) = call(
        functools.partial(backward_kernel, scale),
        [((WIRE, LON), F32)],
        scratch=[
            pltpu.VMEM((8, WIN), F32),
            pltpu.VMEM((8, WIN), F32),
            pltpu.VMEM((K * CH, CH), F32),
            pltpu.VMEM((16, LON), F32),
            pltpu.VMEM((K * CH, WIN), BF),
            pltpu.VMEM((K * CH, WIN), F32),
        ],
        grid=(STEPS,),
        in_specs=[
            smem(),
            whole((16, WIN)),
            whole((8, WIN)),
            whole((8, CELLS)),
            whole((160, LON)),
            whole((2, K * CH, CH)),
            whole((CH, 16)),
            whole((16, CH)),
        ]
        + [at_step_back(shape) for shape in history],
        out_specs=[whole((WIRE, LON))],
    )(
        ids, window, flux_grad, flux_strip, ocean_wire, flat_back, head_back, lift_back,
        inputs, source, gate_one, gate_two, last,
    )

    parts = lax.all_to_all(wire.reshape(devices, rows, LON), BOTH, 0, 0, tiled=True)
    (sums,) = call(
        functools.partial(sum_kernel, sectors, rows), [((devices, 4 * rows, LON), BF)]
    )(parts)
    sums = lax.all_to_all(sums, BOTH, 0, 0, tiled=True)
    totals = call(
        functools.partial(final_kernel, rows),
        [
            ((CH, 10), F32),
            ((2, K, CH, CH), F32),
            ((12, CH), F32),
            ((CH, 12), F32),
            ((2, K, CH, CH), F32),
            ((8, CH), F32),
        ],
        scratch=[pltpu.VMEM((4, WIRE, LON), F32)],
    )(sums)
    return (next_state[None, None], *totals)


def solution(mesh):
    return jax.shard_map(
        shards,
        mesh=mesh,
        in_specs=(
            P("group", "tile", None, None),
            P("group", "tile", None, None),
            P("group", "tile", None, None),
            P(None, "tile", None),
            P(),
            P(),
            P(),
            P(),
            P(),
            P(),
        ),
        out_specs=(P("group", "tile", None, None), P(), P(), P(), P(), P(), P()),
        check_vma=False,
    )
```

time: 984 us -> 115 us (0.12)
  waiting for transfers between devices: 286 us -> 2.19 us
  starting transfers between devices: 264 us -> 5.45 us
  local copies, waits for them, and re-layouts: 145 us -> 19.8 us
  other arithmetic: 122 us -> 0 us
  matrix products: 53 us -> 0 us
  Pallas kernels: 0 us -> 35.1 us
  blocking collectives: 82.4 us -> 51.1 us
  between operations: 21.8 us -> 0.81 us
    ppermute x128 -> x3, starting transfers between devices: 257 us -> 5.45 us  [the longest x1 4.38 us: shards(): other_final = lax.ppermute(final, BOTH, partner)]
    ppermute x128 -> x3, waiting for transfers between devices: 214 us -> 2.19 us  [the longest x1 1.33 us: shards(): flux_strip = lax.ppermute(flux_strip, BOTH, beside)]
    psum x3 -> x0, blocking collectives: 82.4 us -> none  [the longest x1 66.3 us: shards(): lax.psum((keep_only(atm_keep, lift_total), keep_only(atm_keep, jnp.stack(...]
    psum x1 -> x0, waiting for transfers between devices: 69.4 us -> none  [shards(): lax.psum((keep_only(atm_keep, lift_total), keep_only(atm_keep, jnp.stack(...]
    scatter-add x38 -> x0, other arithmetic: 60.2 us -> none  [the longest x6 57.7 us: conv_back(): grad_ext.at[:, part_table]]
    dot_general x119 -> x0, matrix products: 53 us -> none  [the longest x16 14.3 us: stencil_ahead(): jnp.dot(flat_weight(weight), stacked, preferred_element_type=jnp.float32)]
    slice x112 -> x0, local copies, waits for them, and re-layouts: 47.9 us -> none  [the longest x16 36.9 us: stencil_back(): spread[:, 0]]
    scatter-add x97 -> x0, local copies, waits for them, and re-layouts: 44.1 us -> none  [the longest x16 23.4 us: fold_back(): inner_part.at[:, 0, lon_cols - 1].add(north_rim[:, lon_cols + 3])]
  transfers between devices with their start and end apart: 130 -> 3, of which waited for: 97 -> 2; matrix products, arithmetic and copies ran while one was open for 4% -> 8% of each run, Pallas kernels for 0% -> 0%
where the time goes in v1:
time: 115 us; the launch traced here: 114 us
  blocking collectives  51.1 us (44%)
  Pallas kernels  35.1 us (31%)
  local copies, waits for them, and re-layouts  19.8 us (17%)
  starting transfers between devices  5.45 us (5%)
  waiting for transfers between devices  2.19 us (2%)
    all_to_all x1, blocking collectives, shards(): lax.all_to_all(wire.reshape(devices, rows, LON), BOTH, 0, 0, tiled=True)  24.1 us
    all_to_all x1, blocking collectives, shards(): sums = lax.all_to_all(sums, BOTH, 0, 0, tiled=True)  17.9 us
    pallas_call x1, Pallas kernels, shards(): call(functools.partial(backward_kernel, scale), [((WIRE, LON), F32)], scr...  17.6 us
    unnamed x39, local copies, waits for them, and re-layouts  12.7 us
    pallas_call x1, Pallas kernels, shards(): call(forward_kernel, [((STEPS,) + shape, BF) for shape in history] + [((1...  9.78 us
    all_gather x1, blocking collectives, shards(): gathered = lax.all_gather(packed, 'group')  9.11 us
    pallas_call x1, Pallas kernels, shards(): call(functools.partial(ocean_kernel, scale), [((8, CELLS), F32), ((8, WIN...  5.9 us
    ppermute x1, starting transfers between devices, shards(): other_final = lax.ppermute(final, BOTH, partner)  4.38 us
  transfers between devices with their start and end apart: 3, of which 2 were waited for; matrix products, arithmetic and copies ran while one was open for 8% of the time, Pallas kernels for 0%

profile of v1, /device:TPU:1, one launch (start us, length us, event | category | flops | bytes accessed | tf_op | source)
XLA Modules:
  0.0 114.5 jit_solution(4143791332753912759)
XLA Ops:
  0.7 0.7 copy.41
  1.4 0.7 copy-done.8
  2.1 0.7 copy-done.9
  2.8 9.1 %all-gather = f32[128,384]{1,0:T(8,128)S(1)} all-gather(f32[32,384]{1,0:T(8,128)S(1)} %shard_map.153), channel_id=2, replica_groups=mesh['group'=4,'tile'=32] {'group'}, dimensions={0}, use_global_device_ids=true | all-gather | bytes 245760 | tf_op jit(solution)/shard_map/all_gather | solution.py:463
  11.9 0.7 copy-done.10
  12.9 1.1 collective-permute-start
  14.0 1.1 %copy.28 = bf16[2,64,9,64]{1,3,2,0:T(8,128)(2,1)S(1)} copy(bf16[2,64,9,64]{3,1,2,0:T(8,128)(2,1)} %bitcast.31) | data formatting | bytes 294912 | tf_op jit(solution)/shard_map/transpose | solution.py:451
  15.5 0.9 collective-permute-done.strip
  16.4 9.8 %shard_map.155 = (bf16[8,16,1152]{2,1,0:T(8,128)(2,1)S(1)}, bf16[8,64,1152]{2,1,0:T(8,128)(2,1)S(1)}, bf16[8,64,1152]{2,1,0:T(8,128)(2,1)S(1)}, bf16[8,64,1152]{...) custom-call(s32[1]{0:T(128)} %bitcast.ids, ...), custom_call_target="tpu_custom_call" | custom-call | tf_op jit(solution)/shard_map/pallas_call | solution.py:482
  26.2 1.0 copy-done
  27.2 1.0 copy-done.2
  28.2 4.4 %collective-permute-start.1 = (f32[16,1152]{1,0:T(8,128)S(1)}, f32[16,1152]{1,0:T(8,128)S(1)}, u32[]{:S(2)}, u32[]{:S(2)}) collective-permute-start(f32[16,1152]{1,0:T(8,128)S(1)} %get-tuple-element.28.own), channel_id=1, source_target_pairs={{0,32},{1,33},{2,34},{3,35},{4,36},{5,37},{6,38},{7,39},{8,40},{9,... | collective-permute-start | bytes 221192 | tf_op jit(solution)/shard_map/ppermute | solution.py:502
  32.6 0.7 copy.33
  33.3 1.1 %copy.31 = bf16[2,64,9,64]{1,3,2,0:T(8,128)(2,1)S(1)} copy(bf16[2,64,9,64]{3,1,2,0:T(8,128)(2,1)} %bitcast.29) | data formatting | bytes 294912 | tf_op jit(solution)/shard_map/transpose | solution.py:457
  34.6 1.2 %copy.32 = bf16[2,9,64,64]{3,2,1,0:T(8,128)(2,1)S(1)} copy(bf16[2,9,64,64]{2,3,1,0:T(8,128)(2,1)} %bitcast.30) | data formatting | bytes 294912 | tf_op jit(solution)/shard_map/transpose | solution.py:458
  35.8 0.7 copy.30
  36.5 0.7 pad.32.lift
  37.2 0.7 pad.35.head_back
  38.0 5.9 %shard_map.156 = (f32[8,384]{1,0:T(8,128)}, f32[8,1152]{1,0:T(8,128)S(1)}, f32[8,384]{1,0:T(8,128)}, f32[160,128]{1,0:T(8,128)S(1)}) custom-call(s32[1]{0:T(128)} %bitcast.ids, f32[4,32,384]{2,1,0:T(8,128)S(1)} %bitcast.22, f32[16,1152]{1,0:T(8,128)S(1)} %get-tuple-element.28.own, f32[16,1152]{1,0:T(8,128)S(1)} %collective-permute-done.1.other, ...), custom_call_target="tpu_custom_call" | custom-call | tf_op jit(solution)/shard_map/pallas_call | solution.py:503
  44.6 1.2 %copy.35 = bf16[2,9,64,64]{3,2,1,0:T(8,128)(2,1)S(1)} copy(bf16[2,9,64,64]{2,3,1,0:T(8,128)(2,1)} %bitcast.32) | data formatting | bytes 294912 | tf_op jit(solution)/shard_map/transpose | solution.py:452
  45.8 0.7 pad.37.lift_back
  46.5 1.3 %collective-permute-done.2.flux_strip = f32[8,384]{1,0:T(8,128)S(1)} collective-permute-done((f32[8,384]{1,0:T(8,128)}, f32[8,384]{1,0:T(8,128)S(1)}, u32[]{:S(2)}, u32[]{:S(2)}) %collective-permute-start.2) | collective-permute-done | bytes 12320 | tf_op jit(solution)/shard_map/ppermute | solution.py:516
  47.8 1.3 %copy-done.1 = bf16[8,64,1152]{2,1,0:T(8,128)(2,1)S(1)} copy-done((bf16[8,64,1152]{2,1,0:T(8,128)(2,1)S(1)}, bf16[8,64,1152]{2,1,0:T(8,128)(2,1)}, u32[]{:S(2)}) %copy-start.1) | copy-done | bytes 1179672
  49.1 1.3 %copy-done.3 = bf16[8,64,1152]{2,1,0:T(8,128)(2,1)S(1)} copy-done((bf16[8,64,1152]{2,1,0:T(8,128)(2,1)S(1)}, bf16[8,64,1152]{2,1,0:T(8,128)(2,1)}, u32[]{:S(2)}) %copy-start.3) | copy-done | bytes 1179672
  50.4 0.9 copy-done.5
  51.3 0.8 copy-done.7
  52.0 17.6 %shard_map.157 = f32[512,128]{1,0:T(8,128)S(1)} custom-call(s32[1]{0:T(128)} %bitcast.ids, f32[16,1152]{1,0:T(8,128)S(1)} %copy-done.5, f32[8,1152]{1,0:T(8,128)S(1)} %copy-done.7, f32[8,384]{1,0:T(8,128)S(1)} %collective-permute-done.2.flux_strip, f32[160,128]{1,0:T(8,128)S(1)} %get-tuple-element.33.ocean_wire, bf16[2,576,64]{2,1,0:T(8,128)(2,1)S(1)} %bitcast.24, ...), custom_call_target="tpu_custom_call" | custom-call | tf_op jit(solution)/shard_map/pallas_call | solution.py:518
  69.7 24.1 %all_to_all.10.parts = f32[128,4,128]{2,1,0:T(4,128)S(1)} all-to-all(f32[128,4,128]{2,1,0:T(4,128)S(1)} %bitcast.25), channel_id=1, replica_groups=mesh['group'=4,'tile'=32] {'group','tile'}, dimensions={0} | all-to-all | bytes 524288 | tf_op jit(solution)/shard_map/all_to_all | solution.py:547
  93.9 17.9 %all_to_all.11.parts = bf16[128,16,128]{2,1,0:T(8,128)(2,1)S(1)} all-to-all(bf16[128,16,128]{2,1,0:T(8,128)(2,1)S(1)} %shard_map.158), channel_id=1, replica_groups=mesh['group'=4,'tile'=32] {'group','tile'}, dimensions={0} | all-to-all | bytes 1048576 | tf_op jit(solution)/shard_map/all_to_all | solution.py:551
  111.8 1.3 %shard_map.159 = (f32[64,10]{1,0:T(8,128)S(1)}, f32[2,9,64,64]{3,2,1,0:T(8,128)}, f32[12,64]{1,0:T(8,128)}, f32[64,12]{1,0:T(8,128)S(1)}, f32[2,9,64,64]{3,2,1,0:T(8,128)}, /*index=5*/f32[8,64]{1,0:T(8,128)}) custom-call(bf16[128,16,128]{2,1,0:T(8,128)(2,1)S(1)} %all_to_all.11.parts), custom_call_target="tpu_custom_call" | custom-call | tf_op jit(solution)/shard_map/pallas_call | solution.py:552
  113.1 0.7 copy.37
  113.8 0.7 copy.38
  (37 shorter events, 1.7 us)
Async XLA Ops:
  0.6 14.7 %copy-start.14 = (bf16[64,10]{0,1:T(8,128)(2,1)S(1)}, bf16[64,10]{0,1:T(8,128)(2,1)}, u32[]{:S(2)}) copy-start(bf16[64,10]{0,1:T(8,128)(2,1)} %param.14) | copy-start | bytes 3844
  0.6 14.8 %copy-start.13 = (bf16[12,64]{1,0:T(8,128)(2,1)S(1)}, bf16[12,64]{1,0:T(8,128)(2,1)}, u32[]{:S(2)}) copy-start(bf16[12,64]{1,0:T(8,128)(2,1)} %param.16) | copy-start | bytes 4612
  0.7 31.9 %copy-start.15 = (bf16[8,64]{1,0:T(8,128)(2,1)S(1)}, bf16[8,64]{1,0:T(8,128)(2,1)}, u32[]{:S(2)}) copy-start(bf16[8,64]{1,0:T(8,128)(2,1)} %param.19) | copy-start | bytes 3076
  1.4 0.7 copy-start.8
  2.1 0.7 copy-start.9
  11.9 0.7 copy-start.10
  12.9 3.4 %collective-permute-start = (f32[24,384]{1,0:T(8,128)S(1)}, f32[24,384]{1,0:T(8,128)S(1)}, u32[]{:S(2)}, u32[]{:S(2)}) collective-permute-start(f32[24,384]{1,0:T(8,128)S(1)} %get-tuple-element.27), channel_id=1, source_target_pairs={{0,63},{1,32},{2,33},{3,34},{4,35},{5,36},{6,37},{7,38},{8,39},{9,... | collective-permute-start | bytes 110600 | tf_op jit(solution)/shard_map/ppermute | solution.py:469
  15.2 20.6 %copy-start.12 = (bf16[64,12]{0,1:T(8,128)(2,1)S(1)}, bf16[64,12]{0,1:T(8,128)(2,1)}, u32[]{:S(2)}) copy-start(bf16[64,12]{0,1:T(8,128)(2,1)} %param.17) | copy-start | bytes 4612
  15.4 22.6 %copy-start.11 = (s32[3,1,128]{2,1,0:T(1,128)S(1)}, s32[3,1,128]{2,1,0:T(1,128)}, u32[]{:S(2)}) copy-start(s32[3,1,128]{2,1,0:T(1,128)} %sea.3) | copy-start | bytes 4612
  26.1 1.1 copy-start
  27.2 1.0 copy-start.2
  28.2 9.8 %copy-start.4 = (f32[16,1152]{1,0:T(8,128)}, f32[16,1152]{1,0:T(8,128)S(1)}, u32[]{:S(2)}) copy-start(f32[16,1152]{1,0:T(8,128)S(1)} %get-tuple-element.30.window) | copy-start | bytes 221188
  28.2 9.7 %collective-permute-start.1 = (f32[16,1152]{1,0:T(8,128)S(1)}, f32[16,1152]{1,0:T(8,128)S(1)}, u32[]{:S(2)}, u32[]{:S(2)}) collective-permute-start(f32[16,1152]{1,0:T(8,128)S(1)} %get-tuple-element.28.own), channel_id=1, source_target_pairs={{0,32},{1,33},{2,34},{3,35},{4,36},{5,37},{6,38},{7,39},{8,40},{9,... | collective-permute-start | bytes 221192 | tf_op jit(solution)/shard_map/ppermute | solution.py:502
  43.9 0.6 copy-start.6
  44.5 3.3 %collective-permute-start.2 = (f32[8,384]{1,0:T(8,128)}, f32[8,384]{1,0:T(8,128)S(1)}, u32[]{:S(2)}, u32[]{:S(2)}) collective-permute-start(f32[8,384]{1,0:T(8,128)} %get-tuple-element.32), channel_id=1, source_target_pairs={{0,63},{1,32},{2,33},{3,34},{4,35},{5,36},{6,37},{7,38},{8,39},{9,... | collective-permute-start | bytes 36872 | tf_op jit(solution)/shard_map/ppermute | solution.py:516
  47.8 1.3 %copy-start.1 = (bf16[8,64,1152]{2,1,0:T(8,128)(2,1)S(1)}, bf16[8,64,1152]{2,1,0:T(8,128)(2,1)}, u32[]{:S(2)}) copy-start(bf16[8,64,1152]{2,1,0:T(8,128)(2,1)} %copy-done) | copy-start | bytes 3538948
  49.1 1.3 %copy-start.3 = (bf16[8,64,1152]{2,1,0:T(8,128)(2,1)S(1)}, bf16[8,64,1152]{2,1,0:T(8,128)(2,1)}, u32[]{:S(2)}) copy-start(bf16[8,64,1152]{2,1,0:T(8,128)(2,1)} %copy-done.2) | copy-start | bytes 3538948
  50.4 0.9 copy-start.5
  51.3 0.8 copy-start.7

commit v2 on v1

--- a/solution.py
+++ b/solution.py
@@ -21,7 +21,9 @@
 BF = jnp.bfloat16
 F32 = jnp.float32
 INTERPRET = False
-VMEM_LIMIT = 48 * 1024 * 1024
+VMEM_LIMIT = 16 * 1024 * 1024
+WHOLE_VMEM = 62 * 1024 * 1024
+BACK = (0, 1, 2, 3, 4, 5, 6, 7, 8, 5, 6, 7, 8)
 
 NN = (((1,), (0,)), ((), ()))
 NT = (((1,), (1,)), ((), ()))
@@ -31,7 +33,7 @@
     return lax.dot_general(a, b, dims, preferred_element_type=F32)
 
 
-def call(body, outs, scratch=(), grid=(), in_specs=None, out_specs=None):
+def call(body, outs, scratch=(), grid=(), in_specs=None, out_specs=None, limit=VMEM_LIMIT):
     vmem = pl.BlockSpec(memory_space=pltpu.VMEM)
     extra = {}
     if grid:
@@ -43,13 +45,17 @@
         out_shape=[jax.ShapeDtypeStruct(shape, dtype) for shape, dtype in outs],
         scratch_shapes=list(scratch),
         interpret=INTERPRET,
-        compiler_params=pltpu.CompilerParams(vmem_limit_bytes=VMEM_LIMIT),
+        compiler_params=pltpu.CompilerParams(vmem_limit_bytes=limit),
         **extra,
     )
 
 
 def smem():
     return pl.BlockSpec(memory_space=pltpu.SMEM)
+
+
+def hbm():
+    return pl.BlockSpec(memory_space=pltpu.HBM)
 
 
 def vmem():
@@ -93,26 +99,74 @@
     return pltpu.roll(merged, jnp.where(half == 0, HALO, LON - HALO), 1)
 
 
-def pack_kernel(ids, state, cotangent, table, out):
-    ocean = ids[0] == 3
-    out[0:8, :] = state[...]
-    out[8:16, :] = cotangent[...]
-    entries = table[...]
-    north = (entries[5:7] == entries[1:2]).astype(F32)
-    south = (entries[7:9] == entries[2:3]).astype(F32)
-    flags = jnp.concatenate(
-        [jnp.zeros((2, CELLS), F32), north, south, jnp.zeros((3, CELLS), F32)], axis=0
-    )
-    chosen = jnp.where(ocean, entries.astype(F32), flags)
-    out[16:32, :] = jnp.concatenate([chosen, jnp.zeros((7, CELLS), F32)], axis=0)
-
-
-def one_hot_sea(sea_row):
+def pack_kernel(state, cotangent, table, sea, out, held, held_sea, done):
+    copies = [
+        pltpu.make_async_copy(state, out.at[0:8], done.at[0]),
+        pltpu.make_async_copy(cotangent, out.at[8:16], done.at[1]),
+        pltpu.make_async_copy(table, held, done.at[2]),
+        pltpu.make_async_copy(sea, held_sea, done.at[3]),
+    ]
+    for copy in copies:
+        copy.start()
+    for copy in copies:
+        copy.wait()
+    rows = [held[k] for k in range(K)]
+    rows.append(jnp.concatenate([held_sea[cycle] for cycle in range(3)], axis=1))
+    rows.append(jnp.zeros((6, CELLS), jnp.int32))
+    out[16:32, :] = jnp.concatenate(rows, axis=0).astype(F32)
+
+
+def turned(value):
+    return jnp.transpose(value.astype(F32)).astype(BF)
+
+
+def to_sixteen(value):
+    zeros = jnp.zeros((16 - value.shape[0], value.shape[1]), F32)
+    return jnp.concatenate([value.astype(F32), zeros], axis=0).astype(BF)
+
+
+def weights_kernel(
+    far_atm_lift, far_atm_conv, far_atm_head, far_ocn_lift, far_ocn_conv, far_ocn_head,
+    lift, lift_back, head, head_back, flat, back,
+    ocean_lift, ocean_lift_back, ocean_head, ocean_head_back, ocean_flat, ocean_back,
+    atm_lift, atm_conv, atm_head, ocn_lift, ocn_conv, ocn_head, done,
+):
+    far = (far_atm_lift, far_atm_conv, far_atm_head, far_ocn_lift, far_ocn_conv, far_ocn_head)
+    near = (atm_lift, atm_conv, atm_head, ocn_lift, ocn_conv, ocn_head)
+    copies = [pltpu.make_async_copy(a, b, done.at[i]) for i, (a, b) in enumerate(zip(far, near))]
+    for copy in copies:
+        copy.start()
+    for copy in copies:
+        copy.wait()
+    for raw, ahead, behind in ((atm_lift, lift, lift_back), (ocn_lift, ocean_lift, ocean_lift_back)):
+        full = to_sixteen(raw[...])
+        behind[...] = full
+        ahead[...] = turned(full)
+    for raw, ahead, behind in ((atm_head, head, head_back), (ocn_head, ocean_head, ocean_head_back)):
+        full = to_sixteen(raw[...])
+        ahead[...] = full
+        behind[...] = turned(full)
+    for index in range(2):
+        blocks = [atm_conv[index, k] for k in range(K)]
+        flat[index] = jnp.concatenate(blocks, axis=1)
+        blocks = [turned(block) for block in blocks]
+        back[index] = jnp.concatenate([blocks[k] for k in BACK], axis=1)
+        blocks = [ocn_conv[index, k] for k in range(K)]
+        ocean_flat[index] = jnp.concatenate(blocks, axis=1)
+        for k in range(K):
+            ocean_back[index, k * CH : (k + 1) * CH, :] = turned(blocks[k])
+
+
+def one_hot_sea(row):
     cells = lax.broadcasted_iota(jnp.int32, (CELLS, LON), 0)
-    return jnp.where(cells == sea_row, 1.0, 0.0).astype(BF)
-
-
-def sector_kernel(ids, gathered, sea, features, strip):
+    return jnp.where(cells == row, 1.0, 0.0).astype(BF)
+
+
+def sea_row(gathered, cycle):
+    return gathered[3, 25:26, cycle * LON : (cycle + 1) * LON].astype(jnp.int32)
+
+
+def sector_kernel(ids, gathered, features, strip):
     half = ids[0] % 2
     for cycle in range(3):
         cols = slice(cycle * CELLS, (cycle + 1) * CELLS)
@@ -121,9 +175,11 @@
         row_ids = lax.broadcasted_iota(jnp.int32, (8, LON), 0)
         sources = jnp.where(row_ids == 0, warm[0:1], jnp.where(row_ids == 1, 1.0, 0.0))
         sources = jnp.concatenate([sources, jnp.zeros((8, LON), F32)], axis=0).astype(BF)
-        placed = dot(sources, one_hot_sea(sea[cycle]), NT)[0:8]
-        wide_ids = lax.broadcasted_iota(jnp.int32, (8, CELLS), 0)
-        features[16:24, cols] = jnp.where(wide_ids < 2, placed, gathered[cycle, 16:24, :])
+        placed = dot(sources, one_hot_sea(sea_row(gathered, cycle)), NT)[0:8]
+        features[16:24, cols] = placed
+        table = gathered[cycle, 16:32, :]
+        features[18:20, cols] = jnp.where(table[5:7] == table[1:2], 1.0, 0.0)
+        features[20:22, cols] = jnp.where(table[7:9] == table[2:3], 1.0, 0.0)
     packed = pack_strip(lambda row: features[:, seg(row)], half, (24, LON))
     for block in range(3):
         strip[:, seg(block)] = packed[block]
@@ -153,29 +209,37 @@
             out[k * CH : (k + 1) * CH, seg(row)] = taps[k]
 
 
-def spread_back(spread, flags):
-    results = []
+def build_back(out, at, rows, flags):
+    mid = [piece.astype(BF) for piece in rows]
+    from_east = [pltpu.roll(piece, LON - 1, 1).astype(BF) for piece in rows]
+    from_west = [pltpu.roll(piece, 1, 1).astype(BF) for piece in rows]
+    zero = jnp.zeros((CH, LON), BF)
+
+    def flag(index, row):
+        return flags[index : index + 1, seg(row)] > 0.5
+
     for row in range(ROWS):
-        def part(k, at):
-            return spread[k * CH : (k + 1) * CH, seg(at)]
-
-        mid = part(0, row)
-        west = part(3, row)
-        east = part(4, row)
-        for at, straight, left, right in ((row + 1, 1, 5, 6), (row - 1, 2, 7, 8)):
-            if 0 <= at < ROWS:
-                corner = left - 5
-                flag_left = flags[corner : corner + 1, seg(at)] > 0.5
-                flag_right = flags[corner + 1 : corner + 2, seg(at)] > 0.5
-                term_left = part(left, at)
-                term_right = part(right, at)
-                mid = mid + part(straight, at)
-                mid = mid + jnp.where(flag_left, term_left, 0.0)
-                mid = mid + jnp.where(flag_right, term_right, 0.0)
-                west = west + jnp.where(flag_left, 0.0, term_left)
-                east = east + jnp.where(flag_right, 0.0, term_right)
-        results.append(mid + pltpu.roll(west, LON - 1, 1) + pltpu.roll(east, 1, 1))
-    return results
+        below = row + 1 if row + 1 < ROWS else None
+        above = row - 1 if row > 0 else None
+        blocks = [mid[row], zero, zero, from_east[row], from_west[row]] + [zero] * 8
+        for source, straight, first in ((below, 1, 0), (above, 2, 2)):
+            if source is not None:
+                blocks[straight] = mid[source]
+                blocks[5 + first] = jnp.where(flag(4 + first, source), zero, from_east[source])
+                blocks[6 + first] = jnp.where(flag(5 + first, source), zero, from_west[source])
+                blocks[9 + first] = jnp.where(flag(first, source), mid[source], zero)
+                blocks[10 + first] = jnp.where(flag(first + 1, source), mid[source], zero)
+        for j in range(13):
+            out[at, j * CH : (j + 1) * CH, seg(row)] = blocks[j]
+
+
+def split_rows(value):
+    return [value[:, seg(row)] for row in range(ROWS)]
+
+
+def keep_owned(value):
+    lanes = lane_ids(value.shape) % LON
+    return jnp.where((lanes >= HALO) & (lanes < LON - HALO), value, 0.0)
 
 
 def forward_kernel(
@@ -201,21 +265,21 @@
     surface = window[16:24, :]
     surface = jnp.where(row_ids < 2, surface, 0.0)
     inputs = jnp.concatenate([total[0:8, :], surface], axis=0).astype(BF)
-    inputs_out[0] = inputs
+    inputs_out[0] = keep_owned(jnp.concatenate([total[0:8, :], surface], axis=0)).astype(BF)
     lifted = dot(lift[...], inputs)
     build_columns(columns, [lifted[:, seg(row)] for row in range(ROWS)], flags)
     pre = dot(flat[0], columns[...])
     gate = sigmoid(pre)
     hidden = pre * gate
     gate_one[0] = (gate + hidden - hidden * gate).astype(BF)
-    source_out[0] = jnp.where(first, lifted, hidden).astype(BF)
+    source_out[0] = keep_owned(jnp.where(first, lifted, hidden)).astype(BF)
     build_columns(columns, [hidden[:, seg(row)] for row in range(ROWS)], flags)
     pre = dot(flat[1], columns[...])
     gate = sigmoid(pre)
     hidden = pre * gate
     gate_two[0] = (gate + hidden - hidden * gate).astype(BF)
+    last_out[0] = keep_owned(hidden).astype(BF)
     hidden = hidden.astype(BF)
-    last_out[0] = hidden
     total[...] = total[...] + dot(head[...], hidden)
 
     @pl.when(step == STEPS - 1)
@@ -226,7 +290,7 @@
 
 
 def ocean_kernel(
-    scale, ids, gathered, own, other, sea, lift, flat, head, lift_back, flat_back, head_back,
+    scale, ids, gathered, own, other, lift, flat, head, lift_back, flat_back, head_back,
     next_state, flux_grad, strip, wire,
     hot, columns, scatter,
 ):
@@ -238,7 +302,7 @@
     merged = jnp.where(mine, own[...], other[...])
     flux = (merged[8:16, :] * (1.0 / STEPS)).astype(BF)
     flux = jnp.concatenate([flux, flux], axis=0)
-    hot_sea = [one_hot_sea(sea[cycle]) for cycle in range(3)]
+    hot_sea = [one_hot_sea(sea_row(gathered, cycle)) for cycle in range(3)]
     forcing = [
         dot(flux[:, cycle * CELLS : (cycle + 1) * CELLS], hot_sea[cycle])[0:8] for cycle in range(3)
     ]
@@ -307,60 +371,57 @@
 
 
 def backward_kernel(
-    scale, ids, window, flux_own, flux_strip, ocean_wire, flat_back, head_back, lift_back,
+    scale, ids, window, flux_own, flux_strip, ocean_wire, back, head_back, lift_back,
     inputs, source, gate_one, gate_two, last,
     wire,
-    state_grad, flux_grad, weight_total, small_total, columns, spread,
+    head_grad, flags, weight_total, small_total, taps,
 ):
     step = pl.program_id(0)
     half = ids[0] % 2
-    first = ids[0] // 2 == 0
+    chosen = 1 - jnp.where(ids[0] // 2 == 0, 1, 0)
 
     @pl.when(step == 0)
     def _():
-        state_grad[...] = window[0:8, :] * scale
+        head_grad[0:8, :] = window[0:8, :] * scale
         for row in range(ROWS):
             place = row // 4
-            flux_grad[:, seg(row)] = to_window(
+            head_grad[8:16, seg(row)] = to_window(
                 flux_own[:, seg(row)], flux_strip[:, seg(place)], row, half
             )
+            plain = window[10:14, seg(row)]
+            east = pltpu.roll(window[8:16, seg(row)], LON - 1, 1)
+            west = pltpu.roll(window[8:16, seg(row)], 1, 1)
+            flags[0:4, seg(row)] = plain
+            flags[4:5, seg(row)] = east[2:3]
+            flags[5:6, seg(row)] = west[3:4]
+            flags[6:7, seg(row)] = east[4:5]
+            flags[7:8, seg(row)] = west[5:6]
         weight_total[...] = jnp.zeros_like(weight_total)
         small_total[...] = jnp.zeros_like(small_total)
 
-    flags = window[10:14, :]
-
-    def owned(shape):
-        lanes = lane_ids(shape) % LON
-        return (lanes >= HALO) & (lanes < LON - HALO)
-
-    def mask(value):
-        return jnp.where(owned(value.shape), value, 0.0)
-
-    head_grad = jnp.concatenate([state_grad[...], flux_grad[...]], axis=0)
-    hidden = last[0]
-    grad_two = dot(head_back[...], head_grad.astype(BF))
-    slope_two = grad_two * gate_two[0].astype(F32)
-    spread[...] = dot(flat_back[1], slope_two.astype(BF))
-    grad_one = jnp.concatenate(spread_back(spread, flags), axis=1)
-    slope_one = grad_one * gate_one[0].astype(F32)
-    spread[...] = dot(flat_back[0], slope_one.astype(BF))
-    grad_lifted = jnp.concatenate(spread_back(spread, flags), axis=1)
-    lift_weight = dot(inputs[0], mask(grad_lifted).astype(BF), NT)
-    head_weight = dot(mask(head_grad).astype(BF), hidden, NT)
+    grad = head_grad[...].astype(BF)
+    slope_two = dot(head_back[...], grad) * gate_two[0].astype(F32)
+    build_back(taps, 1, split_rows(slope_two), flags)
+    slope_one = dot(back[1], taps[1]) * gate_one[0].astype(F32)
+    build_back(taps, 0, split_rows(slope_one), flags)
+    grad_lifted = dot(back[0], taps[0]).astype(BF)
+    head_grad[0:8, :] += dot(lift_back[...], grad_lifted)[0:8]
+    lift_weight = dot(inputs[0], grad_lifted, NT)
+    head_weight = dot(grad, last[0], NT)
     small_total[...] += jnp.concatenate([lift_weight, head_weight], axis=1)
-    state_grad[...] += dot(lift_back[...], grad_lifted.astype(BF))[0:8]
-    slope = mask(jnp.where(first, slope_one, slope_two)).astype(BF)
-    values = source[0].astype(F32)
-    build_columns(columns, [values[:, seg(row)] for row in range(ROWS)], flags)
-    weight_total[...] += dot(columns[...], slope, NT)
+    weight_total[...] += dot(taps[chosen], source[0], NT)
 
     @pl.when(step == STEPS - 1)
     def _():
-        weight = jnp.transpose(weight_total[...])
+        blocks = []
+        for k in range(K):
+            block = weight_total[k * CH : (k + 1) * CH, :]
+            if k >= 5:
+                block = block + weight_total[(k + 4) * CH : (k + 5) * CH, :]
+            blocks.append(block)
         for j in range(4):
-            wire[64 * j : 64 * j + 64, :] = weight[:, seg(j)]
-        rest = weight[:, 512:576]
-        wire[256:288, :] = jnp.concatenate([rest[0:32], rest[32:64]], axis=1)
+            wire[64 * j : 64 * j + 64, :] = jnp.concatenate(blocks[2 * j : 2 * j + 2], axis=1)
+        wire[256:288, :] = jnp.concatenate([blocks[8][0:32], blocks[8][32:64]], axis=1)
         wire[288:304, :] = small_total[...]
         wire[304:464, :] = ocean_wire[...]
         wire[464:512, :] = jnp.zeros((48, LON), F32)
@@ -406,15 +467,11 @@
             o_conv[index, 8, at : at + 16] = piece[:, 0:64]
             o_conv[index, 8, at + 16 : at + 32] = piece[:, 64:128]
     small = sums[0, 288:304, :] + sums[1, 288:304, :]
-    g_lift[...] = jnp.transpose(small[:, 0:64])[:, 0:10]
+    g_lift[...] = small[0:10, 0:64]
     g_head[...] = small[0:12, 64:128]
     small = sums[0, 448:464, :]
-    o_lift[...] = jnp.transpose(small[:, 0:64])[:, 0:12]
+    o_lift[...] = small[0:12, 0:64]
     o_head[...] = small[0:8, 64:128]
-
-
-def padded(array, rows, columns):
-    return jnp.pad(array, ((0, rows - array.shape[0]), (0, columns - array.shape[1])))
 
 
 def shards(
@@ -444,28 +501,49 @@
             other = (t + 1) % sectors if g % 2 else (t - 1) % sectors
             beside.append((g * sectors + t, (g ^ 1) * sectors + other))
 
-    lift = padded(atm_lift, CH, 16)
-    lift_back = padded(atm_lift.T, 16, CH)
-    head = padded(atm_head, 16, CH)
-    head_back = padded(atm_head.T, CH, 16)
-    flat = jnp.transpose(atm_conv, (0, 2, 1, 3)).reshape(2, CH, K * CH)
-    flat_back = jnp.transpose(atm_conv, (0, 1, 3, 2)).reshape(2, K * CH, CH)
-    ocean_lift = padded(ocn_lift, CH, 16)
-    ocean_lift_back = padded(ocn_lift.T, 16, CH)
-    ocean_head = padded(ocn_head, 16, CH)
-    ocean_head_back = padded(ocn_head.T, CH, 16)
-    ocean_flat = jnp.transpose(ocn_conv, (0, 2, 1, 3)).reshape(2, CH, K * CH)
-    ocean_flat_back = jnp.transpose(ocn_conv, (0, 1, 3, 2)).reshape(2, K * CH, CH)
-
     (packed,) = call(
-        pack_kernel, [((32, CELLS), F32)], in_specs=[smem(), vmem(), vmem(), vmem()]
-    )(ids, state[0, 0], cotangent[0, 0], neighbours[0, 0])
+        pack_kernel,
+        [((32, CELLS), F32)],
+        scratch=[
+            pltpu.VMEM((K, 1, CELLS), jnp.int32),
+            pltpu.VMEM((3, 1, LON), jnp.int32),
+            pltpu.SemaphoreType.DMA((4,)),
+        ],
+        in_specs=[hbm()] * 4,
+        limit=WHOLE_VMEM,
+    )(state[0, 0], cotangent[0, 0], neighbours.reshape(K, 1, CELLS), sea_cells)
+    weights = call(
+        weights_kernel,
+        [
+            ((CH, 16), BF),
+            ((16, CH), BF),
+            ((16, CH), BF),
+            ((CH, 16), BF),
+            ((2, CH, K * CH), BF),
+            ((2, CH, 13 * CH), BF),
+            ((CH, 16), BF),
+            ((16, CH), BF),
+            ((16, CH), BF),
+            ((CH, 16), BF),
+            ((2, CH, K * CH), BF),
+            ((2, K * CH, CH), BF),
+        ],
+        scratch=[
+            pltpu.VMEM(array.shape, BF)
+            for array in (atm_lift.T, atm_conv, atm_head, ocn_lift.T, ocn_conv, ocn_head)
+        ]
+        + [pltpu.SemaphoreType.DMA((6,))],
+        in_specs=[hbm()] * 6,
+    )(atm_lift.T, atm_conv, atm_head, ocn_lift.T, ocn_conv, ocn_head)
+    lift, lift_back, head, head_back, flat, back = weights[:6]
+    ocean_lift, ocean_lift_back, ocean_head, ocean_head_back, ocean_flat, ocean_back = weights[6:]
+
     gathered = lax.all_gather(packed, "group")
     features, strip = call(
         sector_kernel,
         [((24, WIN), F32), ((24, CELLS), F32)],
-        in_specs=[smem(), vmem(), vmem()],
-    )(ids, gathered, sea_cells)
+        in_specs=[smem(), vmem()],
+    )(ids, gathered)
     strip = lax.ppermute(strip, BOTH, beside)
 
     def whole(shape):
@@ -508,10 +586,10 @@
             pltpu.VMEM((2, K * CH, CELLS), BF),
             pltpu.VMEM((K * CH, CELLS), BF),
         ],
-        in_specs=[smem()] + [vmem()] * 10,
+        in_specs=[smem()] + [vmem()] * 9,
     )(
-        ids, gathered, final, other_final, sea_cells, ocean_lift, ocean_flat, ocean_head,
-        ocean_lift_back, ocean_flat_back, ocean_head_back,
+        ids, gathered, final, other_final, ocean_lift, ocean_flat, ocean_head,
+        ocean_lift_back, ocean_back, ocean_head_back,
     )
     flux_strip = lax.ppermute(flux_strip, BOTH, beside)
 
@@ -519,12 +597,11 @@
         functools.partial(backward_kernel, scale),
         [((WIRE, LON), F32)],
         scratch=[
+            pltpu.VMEM((16, WIN), F32),
             pltpu.VMEM((8, WIN), F32),
-            pltpu.VMEM((8, WIN), F32),
-            pltpu.VMEM((K * CH, CH), F32),
+            pltpu.VMEM((13 * CH, CH), F32),
             pltpu.VMEM((16, LON), F32),
-            pltpu.VMEM((K * CH, WIN), BF),
-            pltpu.VMEM((K * CH, WIN), F32),
+            pltpu.VMEM((2, 13 * CH, WIN), BF),
         ],
         grid=(STEPS,),
         in_specs=[
@@ -533,14 +610,14 @@
             whole((8, WIN)),
             whole((8, CELLS)),
             whole((160, LON)),
-            whole((2, K * CH, CH)),
+            whole((2, CH, 13 * CH)),
             whole((CH, 16)),
             whole((16, CH)),
         ]
         + [at_step_back(shape) for shape in history],
         out_specs=[whole((WIRE, LON))],
     )(
-        ids, window, flux_grad, flux_strip, ocean_wire, flat_back, head_back, lift_back,
+        ids, window, flux_grad, flux_strip, ocean_wire, back, head_back, lift_back,
         inputs, source, gate_one, gate_two, last,
     )
 
@@ -552,16 +629,17 @@
     totals = call(
         functools.partial(final_kernel, rows),
         [
-            ((CH, 10), F32),
+            ((10, CH), F32),
             ((2, K, CH, CH), F32),
             ((12, CH), F32),
-            ((CH, 12), F32),
+            ((12, CH), F32),
             ((2, K, CH, CH), F32),
             ((8, CH), F32),
         ],
         scratch=[pltpu.VMEM((4, WIRE, LON), F32)],
     )(sums)
-    return (next_state[None, None], *totals)
+    g_lift, g_conv, g_head, o_lift, o_conv, o_head = totals
+    return (next_state[None, None], g_lift.T, g_conv, g_head, o_lift.T, o_conv, o_head)
 
 
 def solution(mesh):

time: 115 us -> 98.9 us (0.86)
  local copies, waits for them, and re-layouts: 19.8 us -> 4.66 us
  blocking collectives: 51.1 us -> 48.2 us
  waiting for transfers between devices: 2.19 us -> 4.03 us
    unnamed x39 -> x12, local copies, waits for them, and re-layouts: 12.7 us -> 4.66 us
    transpose x4 -> x0, local copies, waits for them, and re-layouts: 4.61 us -> none  [the longest x1 1.17 us: shards(): flat_back = jnp.transpose(atm_conv, (0, 1, 3, 2)).reshape(2, K * CH, CH)]
    all_to_all x1, blocking collectives: 24.1 us -> 20.9 us  [shards(): lax.all_to_all(wire.reshape(devices, rows, LON), BOTH, 0, 0, tiled=True)]
    pad x8 -> x0, local copies, waits for them, and re-layouts: 2.19 us -> none  [padded(): jnp.pad(array, ((0, rows - array.shape[0]), (0, columns - array.shape[1])))]
    pallas_call x2 -> x3, Pallas kernels: 1.35 us -> 3.32 us  [the longest x1 1.41 us: shards(): call(pack_kernel, [((32, CELLS), F32)], scratch=[pltpu.VMEM((K, 1, CELLS)...]
    pallas_call x1, Pallas kernels: 17.6 us -> 15.8 us  [shards(): call(functools.partial(backward_kernel, scale), [((WIRE, LON), F32)], scr...]
    ppermute x1, waiting for transfers between devices: 1.33 us -> 3.12 us  [shards(): flux_strip = lax.ppermute(flux_strip, BOTH, beside)]
  transfers between devices with their start and end apart: 3 -> 3, of which waited for: 2 -> 2; matrix products, arithmetic and copies ran while one was open for 8% -> 0% of each run, Pallas kernels for 0% -> 1%
where the time goes in v2:
time: 98.9 us; the launch traced here: 98.5 us
  blocking collectives  48.2 us (49%)
  Pallas kernels  34.8 us (35%)
  starting transfers between devices  6.14 us (6%)
  local copies, waits for them, and re-layouts  4.66 us (5%)
  waiting for transfers between devices  4.03 us (4%)
    all_to_all x1, blocking collectives, shards(): lax.all_to_all(wire.reshape(devices, rows, LON), BOTH, 0, 0, tiled=True)  20.9 us
    all_to_all x1, blocking collectives, shards(): sums = lax.all_to_all(sums, BOTH, 0, 0, tiled=True)  17.9 us
    pallas_call x1, Pallas kernels, shards(): call(functools.partial(backward_kernel, scale), [((WIRE, LON), F32)], scr...  15.8 us
    pallas_call x1, Pallas kernels, shards(): call(forward_kernel, [((STEPS,) + shape, BF) for shape in history] + [((1...  9.77 us
    all_gather x1, blocking collectives, shards(): gathered = lax.all_gather(packed, 'group')  9.33 us
    pallas_call x1, Pallas kernels, shards(): call(functools.partial(ocean_kernel, scale), [((8, CELLS), F32), ((8, WIN...  5.6 us
    ppermute x1, starting transfers between devices, shards(): other_final = lax.ppermute(final, BOTH, partner)  5.07 us
    unnamed x12, local copies, waits for them, and re-layouts  4.66 us
  transfers between devices with their start and end apart: 3, of which 2 were waited for; matrix products, arithmetic and copies ran while one was open for 0% of the time, Pallas kernels for 1%

profile of v2, /device:TPU:1, one launch (start us, length us, event | category | flops | bytes accessed | tf_op | source)
XLA Modules:
  0.0 98.5 jit_solution(17991255122408808612)
XLA Ops:
  0.6 1.4 %shard_map.153 = f32[32,384]{1,0:T(8,128)} custom-call(f32[8,384]{1,0:T(8,128)} %bitcast.17, f32[8,384]{1,0:T(8,128)} %bitcast.18, s32[9,1,384]{2,1,0:T(1,128)} %bitcast.16, s32[3,1,128]{2,1,0:T(1,128)} %sea.1), custom_call_target="tpu_custom_call" | custom-call | tf_op jit(solution)/shard_map/pallas_call | solution.py:504
  2.1 9.3 %all-gather = f32[128,384]{1,0:T(8,128)S(1)} all-gather(f32[32,384]{1,0:T(8,128)} %shard_map.153), channel_id=2, replica_groups=mesh['group'=4,'tile'=32] {'group'}, dimensions={0}, use_global_device_ids=true | all-gather | bytes 245760 | tf_op jit(solution)/shard_map/all_gather | solution.py:541
  11.4 0.3 shard_map.154
  11.7 1.1 %collective-permute-start = (f32[24,384]{1,0:T(8,128)S(1)}, f32[24,384]{1,0:T(8,128)S(1)}, u32[]{:S(2)}, u32[]{:S(2)}) collective-permute-start(f32[24,384]{1,0:T(8,128)S(1)} %get-tuple-element.39), channel_id=1, source_target_pairs={{0,63},{1,32},{2,33},{3,34},{4,35},{5,36},{6,37},{7,38},{8,39},{9,... | collective-permute-start | bytes 110600 | tf_op jit(solution)/shard_map/ppermute | solution.py:547
  12.8 0.0 copy-start
  12.8 1.0 copy-done
  13.7 0.0 copy-start.1
  13.7 1.0 copy-done.1
  14.7 0.0 copy-start.2
  14.7 0.7 copy-done.2
  15.4 0.0 copy-start.3
  15.4 0.7 copy-done.3
  16.1 0.0 copy-start.4
  16.1 0.7 copy-done.4
  16.8 0.0 copy-start.5
  16.8 0.7 copy-done.5
  17.4 0.6 shard_map.155
  18.0 0.0 collective-permute-done.strip
  18.0 9.8 %shard_map.156 = (bf16[8,16,1152]{2,1,0:T(8,128)(2,1)S(1)}, bf16[8,64,1152]{2,1,0:T(8,128)(2,1)S(1)}, bf16[8,64,1152]{2,1,0:T(8,128)(2,1)S(1)}, bf16[8,64,1152]{...) custom-call(s32[1]{0:T(128)} %bitcast.ids, ...), custom_call_target="tpu_custom_call" | custom-call | tf_op jit(solution)/shard_map/pallas_call | solution.py:560
  27.8 5.1 %collective-permute-start.1 = (f32[16,1152]{1,0:T(8,128)S(1)}, f32[16,1152]{1,0:T(8,128)S(1)}, u32[]{:S(2)}, u32[]{:S(2)}) collective-permute-start(f32[16,1152]{1,0:T(8,128)S(1)} %get-tuple-element.43.own), channel_id=1, source_target_pairs={{0,32},{1,33},{2,34},{3,35},{4,36},{5,37},{6,38},{7,39},{8,40},{9,... | collective-permute-start | bytes 221192 | tf_op jit(solution)/shard_map/ppermute | solution.py:580
  32.9 0.9 collective-permute-done.1.other
  33.8 5.6 %shard_map.157 = (f32[8,384]{1,0:T(8,128)}, f32[8,1152]{1,0:T(8,128)S(1)}, f32[8,384]{1,0:T(8,128)S(1)}, f32[160,128]{1,0:T(8,128)S(1)}) custom-call(s32[1]{0:T(128)} %bitcast.ids, f32[4,32,384]{2,1,0:T(8,128)S(1)} %bitcast.12, f32[16,1152]{1,0:T(8,128)S(1)} %get-tuple-element.43.own, f32[16,1152]{1,0:T(8,128)S(1)} %collective-permute-done.1.other, ...), custom_call_target="tpu_custom_call" | custom-call | tf_op jit(solution)/shard_map/pallas_call | solution.py:581
  39.4 0.0 collective-permute-start.2
  39.4 3.1 %collective-permute-done.2.flux_strip = f32[8,384]{1,0:T(8,128)S(1)} collective-permute-done((f32[8,384]{1,0:T(8,128)S(1)}, f32[8,384]{1,0:T(8,128)S(1)}, u32[]{:S(2)}, u32[]{:S(2)}) %collective-permute-start.2) | collective-permute-done | bytes 12320 | tf_op jit(solution)/shard_map/ppermute | solution.py:594
  42.5 15.8 %shard_map.158 = f32[512,128]{1,0:T(8,128)S(1)} custom-call(s32[1]{0:T(128)} %bitcast.ids, f32[16,1152]{1,0:T(8,128)S(1)} %get-tuple-element.51.window, f32[8,1152]{1,0:T(8,128)S(1)} %get-tuple-element.52.flux_own, f32[8,384]{1,0:T(8,128)S(1)} %collective-permute-done.2.flux_strip, f32[160,128]{1,0:T(8,128)S(1)} %get-tuple-element.54.ocean_wire, ...), custom_call_target="tpu_custom_call" | custom-call | tf_op jit(solution)/shard_map/pallas_call | solution.py:596
  58.3 20.9 %all_to_all.10.parts = f32[128,4,128]{2,1,0:T(4,128)S(1)} all-to-all(f32[128,4,128]{2,1,0:T(4,128)S(1)} %bitcast.13), channel_id=1, replica_groups=mesh['group'=4,'tile'=32] {'group','tile'}, dimensions={0} | all-to-all | bytes 524288 | tf_op jit(solution)/shard_map/all_to_all | solution.py:624
  79.2 0.1 shard_map.159
  79.3 17.9 %all_to_all.11.parts = bf16[128,16,128]{2,1,0:T(8,128)(2,1)S(1)} all-to-all(bf16[128,16,128]{2,1,0:T(8,128)(2,1)S(1)} %shard_map.159), channel_id=1, replica_groups=mesh['group'=4,'tile'=32] {'group','tile'}, dimensions={0} | all-to-all | bytes 1048576 | tf_op jit(solution)/shard_map/all_to_all | solution.py:628
  97.2 1.3 %shard_map.160 = (f32[10,64]{1,0:T(8,128)}, f32[2,9,64,64]{3,2,1,0:T(8,128)}, f32[12,64]{1,0:T(8,128)}, f32[12,64]{1,0:T(8,128)}, f32[2,9,64,64]{3,2,1,0:T(8,128)}, /*index=5*/f32[8,64]{1,0:T(8,128)}) custom-call(bf16[128,16,128]{2,1,0:T(8,128)(2,1)S(1)} %all_to_all.11.parts), custom_call_target="tpu_custom_call" | custom-call | tf_op jit(solution)/shard_map/pallas_call | solution.py:629
Async XLA Ops:
  11.7 6.3 %collective-permute-start = (f32[24,384]{1,0:T(8,128)S(1)}, f32[24,384]{1,0:T(8,128)S(1)}, u32[]{:S(2)}, u32[]{:S(2)}) collective-permute-start(f32[24,384]{1,0:T(8,128)S(1)} %get-tuple-element.39), channel_id=1, source_target_pairs={{0,63},{1,32},{2,33},{3,34},{4,35},{5,36},{6,37},{7,38},{8,39},{9,... | collective-permute-start | bytes 110600 | tf_op jit(solution)/shard_map/ppermute | solution.py:547
  12.8 1.0 copy-start
  13.7 1.0 copy-start.1
  14.7 0.7 copy-start.2
  15.4 0.7 copy-start.3
  16.1 0.7 copy-start.4
  16.8 0.7 copy-start.5
  27.8 6.0 %collective-permute-start.1 = (f32[16,1152]{1,0:T(8,128)S(1)}, f32[16,1152]{1,0:T(8,128)S(1)}, u32[]{:S(2)}, u32[]{:S(2)}) collective-permute-start(f32[16,1152]{1,0:T(8,128)S(1)} %get-tuple-element.43.own), channel_id=1, source_target_pairs={{0,32},{1,33},{2,34},{3,35},{4,36},{5,37},{6,38},{7,39},{8,40},{9,... | collective-permute-start | bytes 221192 | tf_op jit(solution)/shard_map/ppermute | solution.py:580
  39.4 3.1 %collective-permute-start.2 = (f32[8,384]{1,0:T(8,128)S(1)}, f32[8,384]{1,0:T(8,128)S(1)}, u32[]{:S(2)}, u32[]{:S(2)}) collective-permute-start(f32[8,384]{1,0:T(8,128)S(1)} %get-tuple-element.53), channel_id=1, source_target_pairs={{0,63},{1,32},{2,33},{3,34},{4,35},{5,36},{6,37},{7,38},{8,39},{9,... | collective-permute-start | bytes 36872 | tf_op jit(solution)/shard_map/ppermute | solution.py:594

commit v3 on v2

--- a/solution.py
+++ b/solution.py
@@ -23,7 +23,7 @@
 INTERPRET = False
 VMEM_LIMIT = 16 * 1024 * 1024
 WHOLE_VMEM = 62 * 1024 * 1024
-BACK = (0, 1, 2, 3, 4, 5, 6, 7, 8, 5, 6, 7, 8)
+BACK = (0, 1, 2, 5, 6, 7, 8, 3, 4, 5, 6, 7, 8)
 
 NN = (((1,), (0,)), ((), ()))
 NT = (((1,), (1,)), ((), ()))
@@ -99,21 +99,27 @@
     return pltpu.roll(merged, jnp.where(half == 0, HALO, LON - HALO), 1)
 
 
-def pack_kernel(state, cotangent, table, sea, out, held, held_sea, done):
-    copies = [
-        pltpu.make_async_copy(state, out.at[0:8], done.at[0]),
-        pltpu.make_async_copy(cotangent, out.at[8:16], done.at[1]),
-        pltpu.make_async_copy(table, held, done.at[2]),
-        pltpu.make_async_copy(sea, held_sea, done.at[3]),
-    ]
+def pack_kernel(
+    ids, state, cotangent, table, sea, atm_lift, atm_head, ocn_lift, ocn_head,
+    out, held, held_sea, near_one, near_two, near_three, near_four, done,
+):
+    near = (near_one, near_two, near_three, near_four)
+    pairs = [(state, out.at[0:8]), (cotangent, out.at[8:16]), (table, held), (sea, held_sea)]
+    pairs += list(zip((atm_lift, atm_head, ocn_lift, ocn_head), near))
+    copies = [pltpu.make_async_copy(a, b, done.at[i]) for i, (a, b) in enumerate(pairs)]
     for copy in copies:
         copy.start()
     for copy in copies:
         copy.wait()
-    rows = [held[k] for k in range(K)]
-    rows.append(jnp.concatenate([held_sea[cycle] for cycle in range(3)], axis=1))
-    rows.append(jnp.zeros((6, CELLS), jnp.int32))
-    out[16:32, :] = jnp.concatenate(rows, axis=0).astype(F32)
+    small = [to_sixteen(ref[...]) for ref in near]
+    small = jnp.concatenate(small + [jnp.zeros((16, LON), F32)], axis=1)
+    share = small[0:4]
+    for place in range(1, 4):
+        share = jnp.where(ids[0] == place, small[4 * place : 4 * place + 4], share)
+    rows = [held[k].astype(F32) for k in range(K)]
+    rows.append(jnp.concatenate([held_sea[cycle] for cycle in range(3)], axis=1).astype(F32))
+    rows += [share, jnp.zeros((2, CELLS), F32)]
+    out[16:32, :] = jnp.concatenate(rows, axis=0)
 
 
 def turned(value):
@@ -122,30 +128,23 @@
 
 def to_sixteen(value):
     zeros = jnp.zeros((16 - value.shape[0], value.shape[1]), F32)
-    return jnp.concatenate([value.astype(F32), zeros], axis=0).astype(BF)
+    return jnp.concatenate([value.astype(F32), zeros], axis=0)
 
 
 def weights_kernel(
-    far_atm_lift, far_atm_conv, far_atm_head, far_ocn_lift, far_ocn_conv, far_ocn_head,
+    gathered, atm_conv, ocn_conv,
     lift, lift_back, head, head_back, flat, back,
     ocean_lift, ocean_lift_back, ocean_head, ocean_head_back, ocean_flat, ocean_back,
-    atm_lift, atm_conv, atm_head, ocn_lift, ocn_conv, ocn_head, done,
 ):
-    far = (far_atm_lift, far_atm_conv, far_atm_head, far_ocn_lift, far_ocn_conv, far_ocn_head)
-    near = (atm_lift, atm_conv, atm_head, ocn_lift, ocn_conv, ocn_head)
-    copies = [pltpu.make_async_copy(a, b, done.at[i]) for i, (a, b) in enumerate(zip(far, near))]
-    for copy in copies:
-        copy.start()
-    for copy in copies:
-        copy.wait()
-    for raw, ahead, behind in ((atm_lift, lift, lift_back), (ocn_lift, ocean_lift, ocean_lift_back)):
-        full = to_sixteen(raw[...])
-        behind[...] = full
-        ahead[...] = turned(full)
-    for raw, ahead, behind in ((atm_head, head, head_back), (ocn_head, ocean_head, ocean_head_back)):
-        full = to_sixteen(raw[...])
-        ahead[...] = full
-        behind[...] = turned(full)
+    small = jnp.concatenate([gathered[group, 26:30, :] for group in range(4)], axis=0)
+    lift_back[...] = small[:, 0:64].astype(BF)
+    lift[...] = turned(small[:, 0:64])
+    head[...] = small[:, 64:128].astype(BF)
+    head_back[...] = turned(small[:, 64:128])
+    ocean_lift_back[...] = small[:, 128:192].astype(BF)
+    ocean_lift[...] = turned(small[:, 128:192])
+    ocean_head[...] = small[:, 192:256].astype(BF)
+    ocean_head_back[...] = turned(small[:, 192:256])
     for index in range(2):
         blocks = [atm_conv[index, k] for k in range(K)]
         flat[index] = jnp.concatenate(blocks, axis=1)
@@ -155,6 +154,18 @@
         ocean_flat[index] = jnp.concatenate(blocks, axis=1)
         for k in range(K):
             ocean_back[index, k * CH : (k + 1) * CH, :] = turned(blocks[k])
+
+
+def hot_kernel(gathered, hot, hot_back):
+    table = gathered[3, 16:32, :]
+    columns = jnp.transpose(table).astype(jnp.int32)
+    table = table.astype(jnp.int32)
+    cell_rows = lax.broadcasted_iota(jnp.int32, (CELLS, CELLS), 0)
+    cell_lanes = lane_ids((CELLS, CELLS))
+    for k in range(K):
+        hot[k] = jnp.where(cell_rows == table[k : k + 1], 1.0, 0.0).astype(BF)
+        target = columns[:, k : k + 1]
+        hot_back[k * CELLS : (k + 1) * CELLS, :] = jnp.where(cell_lanes == target, 1.0, 0.0).astype(BF)
 
 
 def one_hot_sea(row):
@@ -185,28 +196,29 @@
         strip[:, seg(block)] = packed[block]
 
 
+def pick(mask, chosen, other):
+    shape = (CH // 16, 16, LON)
+    result = jnp.where(mask[None], chosen.reshape(shape), other.reshape(shape))
+    return result.reshape(CH, LON)
+
+
+def shifted(piece):
+    mid = piece.astype(BF)
+    return mid, pltpu.roll(mid, 1, 1), pltpu.roll(mid, LON - 1, 1)
+
+
 def build_columns(out, rows, flags):
-    mid = [piece.astype(BF) for piece in rows]
-    west = [pltpu.roll(piece, 1, 1).astype(BF) for piece in rows]
-    east = [pltpu.roll(piece, LON - 1, 1).astype(BF) for piece in rows]
-    zero = jnp.zeros((CH, LON), BF)
     for row in range(ROWS):
-        up = row - 1
-        down = row + 1
-        north = mid[up] if up >= 0 else zero
-        south = mid[down] if down < ROWS else zero
-        taps = [mid[row], north, south, west[row], east[row]]
-        corners = (
-            (west[up], east[up]) if up >= 0 else (zero, zero),
-            (west[down], east[down]) if down < ROWS else (zero, zero),
-        )
-        for corner in range(4):
-            base = north if corner < 2 else south
-            side = corners[corner // 2][corner % 2]
-            flag = flags[corner : corner + 1, seg(row)] > 0.5
-            taps.append(jnp.where(flag, base, side))
-        for k in range(K):
-            out[k * CH : (k + 1) * CH, seg(row)] = taps[k]
+        mid, west, east = shifted(rows[row])
+        places = [(0, row, mid), (3, row, west), (4, row, east)]
+        for cell, straight, first in ((row + 1, 1, 5), (row - 1, 2, 7)):
+            if 0 <= cell < ROWS:
+                places.append((straight, cell, mid))
+                for side, k in ((west, first), (east, first + 1)):
+                    flag = flags[k - 5, :, seg(cell)] > 0.5
+                    places.append((k, cell, pick(flag, mid, side)))
+        for k, cell, value in places:
+            out[k * CH : (k + 1) * CH, seg(cell)] = value
 
 
 def build_back(out, at, rows, flags):
@@ -219,18 +231,16 @@
         return flags[index : index + 1, seg(row)] > 0.5
 
     for row in range(ROWS):
-        below = row + 1 if row + 1 < ROWS else None
-        above = row - 1 if row > 0 else None
-        blocks = [mid[row], zero, zero, from_east[row], from_west[row]] + [zero] * 8
-        for source, straight, first in ((below, 1, 0), (above, 2, 2)):
-            if source is not None:
+        blocks = {0: mid[row], 7: from_east[row], 8: from_west[row]}
+        for source, straight, first in ((row + 1, 1, 0), (row - 1, 2, 2)):
+            if 0 <= source < ROWS:
                 blocks[straight] = mid[source]
-                blocks[5 + first] = jnp.where(flag(4 + first, source), zero, from_east[source])
-                blocks[6 + first] = jnp.where(flag(5 + first, source), zero, from_west[source])
-                blocks[9 + first] = jnp.where(flag(first, source), mid[source], zero)
-                blocks[10 + first] = jnp.where(flag(first + 1, source), mid[source], zero)
-        for j in range(13):
-            out[at, j * CH : (j + 1) * CH, seg(row)] = blocks[j]
+                blocks[3 + first] = jnp.where(flag(first, source), mid[source], zero)
+                blocks[4 + first] = jnp.where(flag(first + 1, source), mid[source], zero)
+                blocks[9 + first] = jnp.where(flag(4 + first, source), zero, from_east[source])
+                blocks[10 + first] = jnp.where(flag(5 + first, source), zero, from_west[source])
+        for j, value in blocks.items():
+            out[at, j * CH : (j + 1) * CH, seg(row)] = value
 
 
 def split_rows(value):
@@ -239,13 +249,13 @@
 
 def keep_owned(value):
     lanes = lane_ids(value.shape) % LON
-    return jnp.where((lanes >= HALO) & (lanes < LON - HALO), value, 0.0)
+    return jnp.where((lanes >= HALO) & (lanes < LON - HALO), value, jnp.zeros_like(value))
 
 
 def forward_kernel(
     ids, features, strip, lift, flat, head,
     inputs_out, source_out, gate_one, gate_two, last_out, window_out, final_out,
-    window, total, columns,
+    window, total, columns, flags,
 ):
     step = pl.program_id(0)
     half = ids[0] % 2
@@ -259,8 +269,10 @@
         total[0:8, :] = window[0:8, :]
         total[8:16, :] = jnp.zeros((8, WIN), F32)
         window_out[...] = window[8:24, :]
-
-    flags = window[18:22, :]
+        for j in range(4):
+            flags[j] = jnp.broadcast_to(window[18 + j : 19 + j, :], (16, WIN)).astype(BF)
+        columns[...] = jnp.zeros_like(columns)
+
     row_ids = lax.broadcasted_iota(jnp.int32, (8, WIN), 0)
     surface = window[16:24, :]
     surface = jnp.where(row_ids < 2, surface, 0.0)
@@ -272,7 +284,7 @@
     gate = sigmoid(pre)
     hidden = pre * gate
     gate_one[0] = (gate + hidden - hidden * gate).astype(BF)
-    source_out[0] = keep_owned(jnp.where(first, lifted, hidden)).astype(BF)
+    source_out[0] = jnp.where(first, lifted, hidden).astype(BF)
     build_columns(columns, [hidden[:, seg(row)] for row in range(ROWS)], flags)
     pre = dot(flat[1], columns[...])
     gate = sigmoid(pre)
@@ -290,13 +302,13 @@
 
 
 def ocean_kernel(
-    scale, ids, gathered, own, other, lift, flat, head, lift_back, flat_back, head_back,
-    next_state, flux_grad, strip, wire,
-    hot, columns, scatter,
+    scale, ids, gathered, own, other, hot, hot_back,
+    lift, flat, head, lift_back, flat_back, head_back,
+    next_state, flux_grad, strip, columns, slopes, sixteen, wide,
+    scatter,
 ):
     group = ids[0]
     half = group % 2
-    first = group // 2 == 0
     lanes = lane_ids((16, WIN))
     mine = ((lanes % LON) // (LON // 2)) == half
     merged = jnp.where(mine, own[...], other[...])
@@ -309,21 +321,16 @@
     forcing = jnp.concatenate(forcing, axis=1)
     fields = gathered[3, 0:8, :]
     inputs = jnp.concatenate([fields, forcing], axis=0).astype(BF)
-    cell_ids = lax.broadcasted_iota(jnp.int32, (CELLS, CELLS), 0)
-    for k in range(K):
-        table = gathered[3, 16 + k : 17 + k, :].astype(jnp.int32)
-        hot[k] = jnp.where(cell_ids == table, 1.0, 0.0).astype(BF)
 
     def gather(at, value):
         for k in range(K):
             columns[at, k * CH : (k + 1) * CH, :] = dot(value, hot[k]).astype(BF)
 
     def spread(index, slope):
-        scatter[...] = dot(flat_back[index], slope).astype(BF)
-        result = jnp.zeros((CH, CELLS), F32)
+        parts = dot(flat_back[index], slope).astype(BF)
         for k in range(K):
-            result = result + dot(scatter[k * CH : (k + 1) * CH, :], hot[k], NT)
-        return result
+            scatter[:, k * CELLS : (k + 1) * CELLS] = parts[k * CH : (k + 1) * CH]
+        return dot(scatter[...], hot_back[...])
 
     lifted = dot(lift[...], inputs).astype(BF)
     gather(0, lifted)
@@ -344,11 +351,9 @@
 
     head_grad = gathered[3, 8:16, :] * scale
     head_grad = jnp.concatenate([head_grad, jnp.zeros((8, CELLS), F32)], axis=0).astype(BF)
-    head_weight = dot(head_grad, hidden, NT)
     slope_two = (dot(head_back[...], head_grad) * slope_of_two).astype(BF)
     slope_one = (spread(1, slope_two) * slope_of_one).astype(BF)
     grad_lifted = spread(0, slope_one).astype(BF)
-    lift_weight = dot(inputs, grad_lifted, NT)
     forcing_grad = dot(lift_back[...], grad_lifted)[8:16]
     forcing_grad = (forcing_grad * (1.0 / STEPS)).astype(BF)
     forcing_grad = jnp.concatenate([forcing_grad, forcing_grad], axis=0)
@@ -358,23 +363,32 @@
     packed = pack_strip(lambda row: flux_grad[:, seg(row)], half, (8, LON))
     for place in range(3):
         strip[:, seg(place)] = packed[place]
-
-    slope = jnp.where(first, slope_one.astype(F32), slope_two.astype(F32)).astype(BF)
-    chosen = jnp.where(first, 0, 1)
-    weight = jnp.transpose(dot(columns[chosen], slope, NT))
+    slopes[0] = slope_one
+    slopes[1] = slope_two
+    sixteen[0] = inputs
+    sixteen[1] = head_grad
+    wide[0] = grad_lifted
+    wide[1] = hidden
+
+
+def ocean_weight_kernel(ids, columns, slopes, sixteen, wide, wire):
+    half = ids[0] % 2
+    chosen = ids[0] // 2
+    weight = jnp.transpose(dot(columns[chosen], slopes[chosen], NT))
     weight = jnp.where(half == 0, weight[0:32], weight[32:64])
     for j in range(4):
-        wire[32 * j : 32 * j + 32, :] = weight[:, seg(j)]
+        wire[32 * j : 32 * j + 32, :] = weight[:, seg(j)].astype(BF)
     rest = weight[:, 512:576]
-    wire[128:144, :] = jnp.concatenate([rest[0:16], rest[16:32]], axis=1)
-    wire[144:160, :] = jnp.concatenate([lift_weight, head_weight], axis=1)
+    wire[128:144, :] = jnp.concatenate([rest[0:16], rest[16:32]], axis=1).astype(BF)
+    small = [dot(sixteen[index], wide[index], NT) for index in range(2)]
+    wire[144:160, :] = jnp.concatenate(small, axis=1).astype(BF)
 
 
 def backward_kernel(
     scale, ids, window, flux_own, flux_strip, ocean_wire, back, head_back, lift_back,
     inputs, source, gate_one, gate_two, last,
     wire,
-    head_grad, flags, weight_total, small_total, taps,
+    head_grad, flags, weight_total, small_total, taps, sources,
 ):
     step = pl.program_id(0)
     half = ids[0] % 2
@@ -388,17 +402,20 @@
             head_grad[8:16, seg(row)] = to_window(
                 flux_own[:, seg(row)], flux_strip[:, seg(place)], row, half
             )
-            plain = window[10:14, seg(row)]
-            east = pltpu.roll(window[8:16, seg(row)], LON - 1, 1)
-            west = pltpu.roll(window[8:16, seg(row)], 1, 1)
-            flags[0:4, seg(row)] = plain
-            flags[4:5, seg(row)] = east[2:3]
-            flags[5:6, seg(row)] = west[3:4]
-            flags[6:7, seg(row)] = east[4:5]
-            flags[7:8, seg(row)] = west[5:6]
+            plain = window[8:16, seg(row)]
+            east = pltpu.roll(plain, LON - 1, 1)
+            west = pltpu.roll(plain, 1, 1)
+            for j in range(4):
+                flags[j : j + 1, seg(row)] = plain[2 + j : 3 + j]
+                flags[4 + j : 5 + j, seg(row)] = (east, west)[j % 2][2 + j : 3 + j]
+        taps[...] = jnp.zeros_like(taps)
         weight_total[...] = jnp.zeros_like(weight_total)
         small_total[...] = jnp.zeros_like(small_total)
 
+    for row in range(ROWS):
+        mid = source[0, :, seg(row)]
+        for place, value in enumerate((pltpu.roll(mid, 1, 1), mid, pltpu.roll(mid, LON - 1, 1))):
+            sources[place * CH : (place + 1) * CH, seg(row)] = keep_owned(value)
     grad = head_grad[...].astype(BF)
     slope_two = dot(head_back[...], grad) * gate_two[0].astype(F32)
     build_back(taps, 1, split_rows(slope_two), flags)
@@ -409,44 +426,45 @@
     lift_weight = dot(inputs[0], grad_lifted, NT)
     head_weight = dot(grad, last[0], NT)
     small_total[...] += jnp.concatenate([lift_weight, head_weight], axis=1)
-    weight_total[...] += dot(taps[chosen], source[0], NT)
+    weight_total[...] += dot(taps[chosen, 0 : 7 * CH, :], sources[...], NT)
 
     @pl.when(step == STEPS - 1)
     def _():
-        blocks = []
-        for k in range(K):
-            block = weight_total[k * CH : (k + 1) * CH, :]
-            if k >= 5:
-                block = block + weight_total[(k + 4) * CH : (k + 5) * CH, :]
-            blocks.append(block)
+        def product(slope, side):
+            rows = weight_total[slope * CH : (slope + 1) * CH, :]
+            return rows[:, side * CH : (side + 1) * CH]
+
+        blocks = [product(0, 1), product(1, 1), product(2, 1), product(0, 0), product(0, 2)]
         for j in range(4):
-            wire[64 * j : 64 * j + 64, :] = jnp.concatenate(blocks[2 * j : 2 * j + 2], axis=1)
-        wire[256:288, :] = jnp.concatenate([blocks[8][0:32], blocks[8][32:64]], axis=1)
-        wire[288:304, :] = small_total[...]
+            straight, side = 1 + j // 2, 2 * (j % 2)
+            turned_part = product(straight, side) - product(3 + j, side)
+            blocks.append(product(3 + j, 1) + turned_part)
+        for j in range(4):
+            pair = jnp.concatenate(blocks[2 * j : 2 * j + 2], axis=1)
+            wire[64 * j : 64 * j + 64, :] = pair.astype(BF)
+        pair = jnp.concatenate([blocks[8][0:32], blocks[8][32:64]], axis=1)
+        wire[256:288, :] = pair.astype(BF)
+        wire[288:304, :] = small_total[...].astype(BF)
         wire[304:464, :] = ocean_wire[...]
-        wire[464:512, :] = jnp.zeros((48, LON), F32)
-
-
-def sum_kernel(sectors, rows, parts, out):
-    sums = []
+        wire[464:512, :] = jnp.zeros((48, LON), BF)
+
+
+def sum_kernel(sectors, devices, parts, out):
+    total = parts[0].astype(F32)
+    for sector in range(1, sectors):
+        total = total + parts[sector].astype(F32)
+    total = total.astype(BF)
+    for place in range(devices):
+        out[place] = total
+
+
+def final_kernel(
+    sectors, rows, parts, g_lift, g_conv, g_head, o_lift, o_conv, o_head, sums
+):
     for group in range(4):
-        total = parts[group * sectors]
-        for sector in range(1, sectors):
-            total = total + parts[group * sectors + sector]
-        sums.append(total)
-    sums = jnp.concatenate(sums, axis=0).astype(BF)
-    for place in range(4 * sectors):
-        out[place] = sums
-
-
-def final_kernel(
-    rows, parts, g_lift, g_conv, g_head, o_lift, o_conv, o_head, sums
-):
-    places = WIRE // rows
-    for place in range(places):
-        piece = parts[place].astype(F32)
-        for group in range(4):
-            sums[group, place * rows : (place + 1) * rows, :] = piece[group * rows : (group + 1) * rows]
+        for sector in range(sectors):
+            piece = parts[group * sectors + sector].astype(F32)
+            sums[group, sector * rows : (sector + 1) * rows, :] = piece
     for index in range(2):
         low, high = 2 * index, 2 * index + 1
         for j in range(4):
@@ -488,7 +506,7 @@
 ):
     sectors = lax.axis_size("tile")
     devices = 4 * sectors
-    rows = WIRE // devices
+    rows = WIRE // sectors
     scale = 1.0 / math.sqrt(devices * CELLS)
     group = lax.axis_index("group")
     ids = group.astype(jnp.int32).reshape(1)
@@ -501,17 +519,27 @@
             other = (t + 1) % sectors if g % 2 else (t - 1) % sectors
             beside.append((g * sectors + t, (g ^ 1) * sectors + other))
 
+    lifts = (atm_lift.T, atm_head, ocn_lift.T, ocn_head)
     (packed,) = call(
         pack_kernel,
         [((32, CELLS), F32)],
         scratch=[
             pltpu.VMEM((K, 1, CELLS), jnp.int32),
             pltpu.VMEM((3, 1, LON), jnp.int32),
-            pltpu.SemaphoreType.DMA((4,)),
-        ],
-        in_specs=[hbm()] * 4,
+        ]
+        + [pltpu.VMEM(array.shape, BF) for array in lifts]
+        + [pltpu.SemaphoreType.DMA((8,))],
+        in_specs=[smem()] + [hbm()] * 8,
         limit=WHOLE_VMEM,
-    )(state[0, 0], cotangent[0, 0], neighbours.reshape(K, 1, CELLS), sea_cells)
+    )(ids, state[0, 0], cotangent[0, 0], neighbours.reshape(K, 1, CELLS), sea_cells, *lifts)
+    gathered = lax.all_gather(packed, "group")
+    features, strip = call(
+        sector_kernel,
+        [((24, WIN), F32), ((24, CELLS), F32)],
+        in_specs=[smem(), vmem()],
+    )(ids, gathered)
+    strip = lax.ppermute(strip, BOTH, beside)
+
     weights = call(
         weights_kernel,
         [
@@ -528,23 +556,12 @@
             ((2, CH, K * CH), BF),
             ((2, K * CH, CH), BF),
         ],
-        scratch=[
-            pltpu.VMEM(array.shape, BF)
-            for array in (atm_lift.T, atm_conv, atm_head, ocn_lift.T, ocn_conv, ocn_head)
-        ]
-        + [pltpu.SemaphoreType.DMA((6,))],
-        in_specs=[hbm()] * 6,
-    )(atm_lift.T, atm_conv, atm_head, ocn_lift.T, ocn_conv, ocn_head)
+    )(gathered, atm_conv, ocn_conv)
     lift, lift_back, head, head_back, flat, back = weights[:6]
     ocean_lift, ocean_lift_back, ocean_head, ocean_head_back, ocean_flat, ocean_back = weights[6:]
 
-    gathered = lax.all_gather(packed, "group")
-    features, strip = call(
-        sector_kernel,
-        [((24, WIN), F32), ((24, CELLS), F32)],
-        in_specs=[smem(), vmem()],
-    )(ids, gathered)
-    strip = lax.ppermute(strip, BOTH, beside)
+    hot, hot_back = call(hot_kernel, [((K, CELLS, CELLS), BF), ((K * CELLS, CELLS), BF)])(gathered)
+    strip, hot, hot_back = lax.optimization_barrier((strip, hot, hot_back))
 
     def whole(shape):
         return pl.BlockSpec(shape, lambda s: (0,) * len(shape))
@@ -564,6 +581,7 @@
             pltpu.VMEM((24, WIN), F32),
             pltpu.VMEM((16, WIN), F32),
             pltpu.VMEM((K * CH, WIN), BF),
+            pltpu.VMEM((4, 16, WIN), BF),
         ],
         grid=(STEPS,),
         in_specs=[
@@ -578,30 +596,38 @@
     )(ids, features, strip, lift, flat, head)
 
     other_final = lax.ppermute(final, BOTH, partner)
-    next_state, flux_grad, flux_strip, ocean_wire = call(
+    next_state, flux_grad, flux_strip, *ocean_parts = call(
         functools.partial(ocean_kernel, scale),
-        [((8, CELLS), F32), ((8, WIN), F32), ((8, CELLS), F32), ((160, LON), F32)],
-        scratch=[
-            pltpu.VMEM((K, CELLS, CELLS), BF),
-            pltpu.VMEM((2, K * CH, CELLS), BF),
-            pltpu.VMEM((K * CH, CELLS), BF),
+        [
+            ((8, CELLS), F32),
+            ((8, WIN), F32),
+            ((8, CELLS), F32),
+            ((2, K * CH, CELLS), BF),
+            ((2, CH, CELLS), BF),
+            ((2, 16, CELLS), BF),
+            ((2, CH, CELLS), BF),
         ],
-        in_specs=[smem()] + [vmem()] * 9,
+        scratch=[pltpu.VMEM((CH, K * CELLS), BF)],
+        in_specs=[smem()] + [vmem()] * 11,
     )(
-        ids, gathered, final, other_final, ocean_lift, ocean_flat, ocean_head,
+        ids, gathered, final, other_final, hot, hot_back, ocean_lift, ocean_flat, ocean_head,
         ocean_lift_back, ocean_back, ocean_head_back,
     )
     flux_strip = lax.ppermute(flux_strip, BOTH, beside)
+    (ocean_wire,) = call(
+        ocean_weight_kernel, [((160, LON), BF)], in_specs=[smem()] + [vmem()] * 4
+    )(ids, *ocean_parts)
 
     (wire,) = call(
         functools.partial(backward_kernel, scale),
-        [((WIRE, LON), F32)],
+        [((WIRE, LON), BF)],
         scratch=[
             pltpu.VMEM((16, WIN), F32),
             pltpu.VMEM((8, WIN), F32),
-            pltpu.VMEM((13 * CH, CH), F32),
+            pltpu.VMEM((7 * CH, 3 * CH), F32),
             pltpu.VMEM((16, LON), F32),
             pltpu.VMEM((2, 13 * CH, WIN), BF),
+            pltpu.VMEM((3 * CH, WIN), BF),
         ],
         grid=(STEPS,),
         in_specs=[
@@ -621,13 +647,13 @@
         inputs, source, gate_one, gate_two, last,
     )
 
-    parts = lax.all_to_all(wire.reshape(devices, rows, LON), BOTH, 0, 0, tiled=True)
+    parts = lax.all_to_all(wire.reshape(sectors, rows, LON), "tile", 0, 0, tiled=True)
     (sums,) = call(
-        functools.partial(sum_kernel, sectors, rows), [((devices, 4 * rows, LON), BF)]
+        functools.partial(sum_kernel, sectors, devices), [((devices, rows, LON), BF)]
     )(parts)
     sums = lax.all_to_all(sums, BOTH, 0, 0, tiled=True)
     totals = call(
-        functools.partial(final_kernel, rows),
+        functools.partial(final_kernel, sectors, rows),
         [
             ((10, CH), F32),
             ((2, K, CH, CH), F32),

time: 98.9 us -> 92.2 us (0.932)
  local copies, waits for them, and re-layouts: 4.66 us -> 1.92 us
  blocking collectives: 48.2 us -> 45.9 us
  Pallas kernels: 34.8 us -> 33.7 us
    all_to_all x1, blocking collectives: 20.9 us -> 16.6 us  [shards(): lax.all_to_all(wire.reshape(sectors, rows, LON), 'tile', 0, 0, tiled=True)]
    unnamed x12 -> x4, local copies, waits for them, and re-layouts: 4.66 us -> 1.92 us
    all_to_all x1, blocking collectives: 17.9 us -> 20 us  [shards(): sums = lax.all_to_all(sums, BOTH, 0, 0, tiled=True)]
    pallas_call x1, Pallas kernels: 5.6 us -> 4.31 us  [shards(): call(functools.partial(ocean_kernel, scale), [((8, CELLS), F32), ((8, WIN...]
    pallas_call x3 -> x5, Pallas kernels: 17.2 us -> 17.6 us  [the longest x1 14.4 us: shards(): call(functools.partial(backward_kernel, scale), [((WIRE, LON), BF)], scra...]
  transfers between devices with their start and end apart: 3 -> 3, of which waited for: 2 -> 2; matrix products, arithmetic and copies ran while one was open for 0% -> 0% of each run, Pallas kernels for 1% -> 3%
where the time goes in v3:
time: 92.2 us; the launch traced here: 91.9 us
  blocking collectives  45.9 us (50%)
  Pallas kernels  33.7 us (37%)
  starting transfers between devices  6.14 us (7%)
  waiting for transfers between devices  3.6 us (4%)
  local copies, waits for them, and re-layouts  1.92 us (2%)
    all_to_all x1, blocking collectives, shards(): sums = lax.all_to_all(sums, BOTH, 0, 0, tiled=True)  20 us
    all_to_all x1, blocking collectives, shards(): lax.all_to_all(wire.reshape(sectors, rows, LON), 'tile', 0, 0, tiled=True)  16.6 us
    pallas_call x1, Pallas kernels, shards(): call(functools.partial(backward_kernel, scale), [((WIRE, LON), BF)], scra...  14.4 us
    pallas_call x1, Pallas kernels, shards(): call(forward_kernel, [((STEPS,) + shape, BF) for shape in history] + [((1...  9.37 us
    all_gather x1, blocking collectives, shards(): gathered = lax.all_gather(packed, 'group')  9.33 us
    ppermute x1, starting transfers between devices, shards(): other_final = lax.ppermute(final, BOTH, partner)  5.07 us
    pallas_call x1, Pallas kernels, shards(): call(functools.partial(ocean_kernel, scale), [((8, CELLS), F32), ((8, WIN...  4.31 us
    ppermute x1, waiting for transfers between devices, shards(): flux_strip = lax.ppermute(flux_strip, BOTH, beside)  2.69 us
  transfers between devices with their start and end apart: 3, of which 2 were waited for; matrix products, arithmetic and copies ran while one was open for 0% of the time, Pallas kernels for 3%

profile of v3, /device:TPU:1, one launch (start us, length us, event | category | flops | bytes accessed | tf_op | source)
XLA Modules:
  0.0 91.9 jit_solution(11462519609783555441)
XLA Ops:
  0.6 1.6 %shard_map.153 = f32[32,384]{1,0:T(8,128)} custom-call(s32[1]{0:T(128)} %bitcast.ids, f32[8,384]{1,0:T(8,128)} %bitcast.17, f32[8,384]{1,0:T(8,128)} %bitcast.18, s32[9,1,384]{2,1,0:T(1,128)} %bitcast.16, s32[3,1,128]{2,1,0:T(1,128)} %sea.1, bf16[10,64]{1,0:T(8,128)(2,1)} %bitcast.19, bf16[12,64]{1,0:T(8,128)(2,1)} %atm_head.1, bf16[12,64]{1,0:T(8,128)(2,1)} %bitcast.20, ...), custom_call_target="tpu_custom_call" | custom-call | tf_op jit(solution)/shard_map/pallas_call | solution.py:523
  2.2 9.3 %all-gather = f32[128,384]{1,0:T(8,128)S(1)} all-gather(f32[32,384]{1,0:T(8,128)} %shard_map.153), channel_id=2, replica_groups=mesh['group'=4,'tile'=32] {'group'}, dimensions={0}, use_global_device_ids=true | all-gather | bytes 245760 | tf_op jit(solution)/shard_map/all_gather | solution.py:535
  11.5 0.3 shard_map.154
  11.9 1.1 %collective-permute-start = (f32[24,384]{1,0:T(8,128)S(1)}, f32[24,384]{1,0:T(8,128)S(1)}, u32[]{:S(2)}, u32[]{:S(2)}) collective-permute-start(f32[24,384]{1,0:T(8,128)S(1)} %get-tuple-element.47), channel_id=1, source_target_pairs={{0,63},{1,32},{2,33},{3,34},{4,35},{5,36},{6,37},{7,38},{8,39},{9,... | collective-permute-start | bytes 110600 | tf_op jit(solution)/shard_map/ppermute | solution.py:541
  12.9 1.6 %shard_map.155 = (bf16[9,384,384]{2,1,0:T(8,128)(2,1)S(1)}, bf16[3456,384]{1,0:T(8,128)(2,1)S(1)}) custom-call(f32[4,32,384]{2,1,0:T(8,128)S(1)} %bitcast.12), custom_call_target="tpu_custom_call" | custom-call | tf_op jit(solution)/shard_map/pallas_call | solution.py:563
  14.5 0.0 copy-start
  14.5 1.0 %copy-done = bf16[2,9,64,64]{3,2,1,0:T(8,128)(2,1)S(1)} copy-done((bf16[2,9,64,64]{3,2,1,0:T(8,128)(2,1)S(1)}, bf16[2,9,64,64]{3,2,1,0:T(8,128)(2,1)}, u32[]{:S(2)}) %copy-start) | copy-done | bytes 147480
  15.5 0.0 copy-start.1
  15.5 1.0 %copy-done.1 = bf16[2,9,64,64]{3,2,1,0:T(8,128)(2,1)S(1)} copy-done((bf16[2,9,64,64]{3,2,1,0:T(8,128)(2,1)S(1)}, bf16[2,9,64,64]{3,2,1,0:T(8,128)(2,1)}, u32[]{:S(2)}) %copy-start.1) | copy-done | bytes 147480
  16.5 0.5 shard_map.156
  16.9 0.0 collective-permute-done.strip
  16.9 9.4 %shard_map.157 = (bf16[8,16,1152]{2,1,0:T(8,128)(2,1)S(1)}, bf16[8,64,1152]{2,1,0:T(8,128)(2,1)S(1)}, bf16[8,64,1152]{2,1,0:T(8,128)(2,1)S(1)}, bf16[8,64,1152]{...) custom-call(s32[1]{0:T(128)} %bitcast.ids, ...), custom_call_target="tpu_custom_call" | custom-call | tf_op jit(solution)/shard_map/pallas_call | solution.py:577
  26.3 5.1 %collective-permute-start.1 = (f32[16,1152]{1,0:T(8,128)S(1)}, f32[16,1152]{1,0:T(8,128)S(1)}, u32[]{:S(2)}, u32[]{:S(2)}) collective-permute-start(f32[16,1152]{1,0:T(8,128)S(1)} %get-tuple-element.54.own), channel_id=1, source_target_pairs={{0,32},{1,33},{2,34},{3,35},{4,36},{5,37},{6,38},{7,39},{8,40},{9,... | collective-permute-start | bytes 221192 | tf_op jit(solution)/shard_map/ppermute | solution.py:598
  31.4 0.9 collective-permute-done.1.other
  32.3 4.3 %shard_map.158 = (f32[8,384]{1,0:T(8,128)}, f32[8,1152]{1,0:T(8,128)S(1)}, f32[8,384]{1,0:T(8,128)S(1)}, bf16[2,576,384]{2,1,0:T(8,128)(2,1)S(1)}, bf16[2,64,384...) custom-call(s32[1]{0:T(128)} %bitcast.ids, f32[4,32,384]{2,1,0:T(8,128)S(1)} %bitcast.14, ...), custom_call_target="tpu_custom_call" | custom-call | tf_op jit(solution)/shard_map/pallas_call | solution.py:599
  36.6 0.0 collective-permute-start.2
  36.6 0.4 shard_map.159.ocean_wire
  37.0 2.7 %collective-permute-done.2.flux_strip = f32[8,384]{1,0:T(8,128)S(1)} collective-permute-done((f32[8,384]{1,0:T(8,128)S(1)}, f32[8,384]{1,0:T(8,128)S(1)}, u32[]{:S(2)}, u32[]{:S(2)}) %collective-permute-start.2) | collective-permute-done | bytes 12320 | tf_op jit(solution)/shard_map/ppermute | solution.py:616
  39.7 14.4 %shard_map.160 = bf16[512,128]{1,0:T(8,128)(2,1)S(1)} custom-call(s32[1]{0:T(128)} %bitcast.ids, f32[16,1152]{1,0:T(8,128)S(1)} %get-tuple-element.64.window, f32[8,1152]{1,0:T(8,128)S(1)} %get-tuple-element.65.flux_own, f32[8,384]{1,0:T(8,128)S(1)} %collective-permute-done.2.flux_strip, bf16[160,128]{1,0:T(8,128)(2,1)S(1)} %shard_map.159.ocean_wire, ...), custom_call_target="tpu_custom_call" | custom-call | tf_op jit(solution)/shard_map/pallas_call | solution.py:621
  54.1 16.6 %all_to_all.10.parts = bf16[32,16,128]{2,1,0:T(8,128)(2,1)S(1)} all-to-all(bf16[32,16,128]{2,1,0:T(8,128)(2,1)S(1)} %bitcast.15), channel_id=1, replica_groups=mesh['group'=4,'tile'=32] {'tile'}, dimensions={0} | all-to-all | bytes 262144 | tf_op jit(solution)/shard_map/all_to_all | solution.py:650
  70.6 0.1 shard_map.161
  70.7 20.0 %all_to_all.11.parts = bf16[128,16,128]{2,1,0:T(8,128)(2,1)S(1)} all-to-all(bf16[128,16,128]{2,1,0:T(8,128)(2,1)S(1)} %shard_map.161), channel_id=1, replica_groups=mesh['group'=4,'tile'=32] {'group','tile'}, dimensions={0} | all-to-all | bytes 1048576 | tf_op jit(solution)/shard_map/all_to_all | solution.py:654
  90.7 1.2 %shard_map.162 = (f32[10,64]{1,0:T(8,128)}, f32[2,9,64,64]{3,2,1,0:T(8,128)}, f32[12,64]{1,0:T(8,128)}, f32[12,64]{1,0:T(8,128)}, f32[2,9,64,64]{3,2,1,0:T(8,128)}, /*index=5*/f32[8,64]{1,0:T(8,128)}) custom-call(bf16[128,16,128]{2,1,0:T(8,128)(2,1)S(1)} %all_to_all.11.parts), custom_call_target="tpu_custom_call" | custom-call | tf_op jit(solution)/shard_map/pallas_call | solution.py:655
Async XLA Ops:
  11.9 5.1 %collective-permute-start = (f32[24,384]{1,0:T(8,128)S(1)}, f32[24,384]{1,0:T(8,128)S(1)}, u32[]{:S(2)}, u32[]{:S(2)}) collective-permute-start(f32[24,384]{1,0:T(8,128)S(1)} %get-tuple-element.47), channel_id=1, source_target_pairs={{0,63},{1,32},{2,33},{3,34},{4,35},{5,36},{6,37},{7,38},{8,39},{9,... | collective-permute-start | bytes 110600 | tf_op jit(solution)/shard_map/ppermute | solution.py:541
  14.5 1.0 %copy-start = (bf16[2,9,64,64]{3,2,1,0:T(8,128)(2,1)S(1)}, bf16[2,9,64,64]{3,2,1,0:T(8,128)(2,1)}, u32[]{:S(2)}) copy-start(bf16[2,9,64,64]{3,2,1,0:T(8,128)(2,1)} %atm_conv.1) | copy-start | bytes 442372
  15.5 1.0 %copy-start.1 = (bf16[2,9,64,64]{3,2,1,0:T(8,128)(2,1)S(1)}, bf16[2,9,64,64]{3,2,1,0:T(8,128)(2,1)}, u32[]{:S(2)}) copy-start(bf16[2,9,64,64]{3,2,1,0:T(8,128)(2,1)} %ocn_conv.1) | copy-start | bytes 442372
  26.3 6.0 %collective-permute-start.1 = (f32[16,1152]{1,0:T(8,128)S(1)}, f32[16,1152]{1,0:T(8,128)S(1)}, u32[]{:S(2)}, u32[]{:S(2)}) collective-permute-start(f32[16,1152]{1,0:T(8,128)S(1)} %get-tuple-element.54.own), channel_id=1, source_target_pairs={{0,32},{1,33},{2,34},{3,35},{4,36},{5,37},{6,38},{7,39},{8,40},{9,... | collective-permute-start | bytes 221192 | tf_op jit(solution)/shard_map/ppermute | solution.py:598
  36.6 3.1 %collective-permute-start.2 = (f32[8,384]{1,0:T(8,128)S(1)}, f32[8,384]{1,0:T(8,128)S(1)}, u32[]{:S(2)}, u32[]{:S(2)}) collective-permute-start(f32[8,384]{1,0:T(8,128)S(1)} %get-tuple-element.66), channel_id=1, source_target_pairs={{0,63},{1,32},{2,33},{3,34},{4,35},{5,36},{6,37},{7,38},{8,39},{9,... | collective-permute-start | bytes 36872 | tf_op jit(solution)/shard_map/ppermute | solution.py:616

commit v4 on v3

--- a/solution.py
+++ b/solution.py
@@ -21,7 +21,7 @@
 BF = jnp.bfloat16
 F32 = jnp.float32
 INTERPRET = False
-VMEM_LIMIT = 16 * 1024 * 1024
+VMEM_LIMIT = 24 * 1024 * 1024
 WHOLE_VMEM = 62 * 1024 * 1024
 BACK = (0, 1, 2, 5, 6, 7, 8, 3, 4, 5, 6, 7, 8)
 
@@ -33,13 +33,10 @@
     return lax.dot_general(a, b, dims, preferred_element_type=F32)
 
 
-def call(body, outs, scratch=(), grid=(), in_specs=None, out_specs=None, limit=VMEM_LIMIT):
-    vmem = pl.BlockSpec(memory_space=pltpu.VMEM)
+def call(body, outs, scratch=(), in_specs=None, limit=VMEM_LIMIT):
     extra = {}
-    if grid:
-        extra = {"grid": grid, "in_specs": in_specs, "out_specs": out_specs}
-    elif in_specs is not None:
-        extra = {"in_specs": in_specs, "out_specs": [vmem] * len(outs)}
+    if in_specs is not None:
+        extra = {"in_specs": in_specs, "out_specs": [vmem()] * len(outs)}
     return pl.pallas_call(
         body,
         out_shape=[jax.ShapeDtypeStruct(shape, dtype) for shape, dtype in outs],
@@ -137,10 +134,13 @@
     ocean_lift, ocean_lift_back, ocean_head, ocean_head_back, ocean_flat, ocean_back,
 ):
     small = jnp.concatenate([gathered[group, 26:30, :] for group in range(4)], axis=0)
-    lift_back[...] = small[:, 0:64].astype(BF)
     lift[...] = turned(small[:, 0:64])
-    head[...] = small[:, 64:128].astype(BF)
     head_back[...] = turned(small[:, 64:128])
+    row_ids = lax.broadcasted_iota(jnp.int32, (16, CH), 0)
+    fields = jnp.where(row_ids < 8, small[:, 64:128], 0.0).astype(BF)
+    mixed = dot(turned(small[:, 0:64]), fields)
+    head[...] = jnp.concatenate([small[:, 64:128], mixed], axis=0).astype(BF)
+    lift_back[...] = jnp.concatenate([small[:, 0:64], jnp.transpose(mixed)], axis=0).astype(BF)
     ocean_lift_back[...] = small[:, 128:192].astype(BF)
     ocean_lift[...] = turned(small[:, 128:192])
     ocean_head[...] = small[:, 192:256].astype(BF)
@@ -255,50 +255,53 @@
 def forward_kernel(
     ids, features, strip, lift, flat, head,
     inputs_out, source_out, gate_one, gate_two, last_out, window_out, final_out,
-    window, total, columns, flags,
+    window, total, columns, columns_two, flags, surface, lifted_total,
 ):
-    step = pl.program_id(0)
     half = ids[0] % 2
     first = ids[0] // 2 == 0
 
-    @pl.when(step == 0)
-    def _():
-        for row in range(ROWS):
-            block = row // 4
-            window[:, seg(row)] = to_window(features[:, seg(row)], strip[:, seg(block)], row, half)
-        total[0:8, :] = window[0:8, :]
-        total[8:16, :] = jnp.zeros((8, WIN), F32)
-        window_out[...] = window[8:24, :]
-        for j in range(4):
-            flags[j] = jnp.broadcast_to(window[18 + j : 19 + j, :], (16, WIN)).astype(BF)
-        columns[...] = jnp.zeros_like(columns)
+    for row in range(ROWS):
+        block = row // 4
+        window[:, seg(row)] = to_window(features[:, seg(row)], strip[:, seg(block)], row, half)
+    total[0:8, :] = window[0:8, :]
+    total[8:16, :] = jnp.zeros((8, WIN), F32)
+    window_out[...] = window[8:24, :]
+    for j in range(4):
+        flags[j] = jnp.broadcast_to(window[18 + j : 19 + j, :], (16, WIN)).astype(BF)
+    for held in (columns, columns_two):
+        for row, blocks in ((0, (1, 5, 6)), (ROWS - 1, (2, 7, 8))):
+            for k in blocks:
+                held[k * CH : (k + 1) * CH, seg(row)] = jnp.zeros((CH, LON), BF)
 
     row_ids = lax.broadcasted_iota(jnp.int32, (8, WIN), 0)
-    surface = window[16:24, :]
-    surface = jnp.where(row_ids < 2, surface, 0.0)
-    inputs = jnp.concatenate([total[0:8, :], surface], axis=0).astype(BF)
-    inputs_out[0] = keep_owned(jnp.concatenate([total[0:8, :], surface], axis=0)).astype(BF)
-    lifted = dot(lift[...], inputs)
-    build_columns(columns, [lifted[:, seg(row)] for row in range(ROWS)], flags)
-    pre = dot(flat[0], columns[...])
-    gate = sigmoid(pre)
-    hidden = pre * gate
-    gate_one[0] = (gate + hidden - hidden * gate).astype(BF)
-    source_out[0] = jnp.where(first, lifted, hidden).astype(BF)
-    build_columns(columns, [hidden[:, seg(row)] for row in range(ROWS)], flags)
-    pre = dot(flat[1], columns[...])
-    gate = sigmoid(pre)
-    hidden = pre * gate
-    gate_two[0] = (gate + hidden - hidden * gate).astype(BF)
-    last_out[0] = keep_owned(hidden).astype(BF)
-    hidden = hidden.astype(BF)
-    total[...] = total[...] + dot(head[...], hidden)
-
-    @pl.when(step == STEPS - 1)
-    def _():
-        for row in range(ROWS):
-            shift = jnp.where(half == 0, LON - HALO, HALO)
-            final_out[:, seg(row)] = pltpu.roll(total[:, seg(row)], shift, 1)
+    surface[...] = jnp.where(row_ids < 2, window[16:24, :], 0.0)
+    inputs = jnp.concatenate([total[0:8, :], surface[...]], axis=0)
+    lifted_total[...] = dot(lift[...], inputs.astype(BF))
+
+    for at in range(STEPS):
+        inputs = jnp.concatenate([total[0:8, :], surface[...]], axis=0)
+        inputs_out[at] = keep_owned(inputs).astype(BF)
+        lifted = lifted_total[...]
+        build_columns(columns, [lifted[:, seg(row)] for row in range(ROWS)], flags)
+        pre = dot(flat[0], columns[...])
+        gate = sigmoid(pre)
+        hidden = pre * gate
+        gate_one[at] = (gate + hidden - hidden * gate).astype(BF)
+        source_out[at] = jnp.where(first, lifted, hidden).astype(BF)
+        build_columns(columns_two, [hidden[:, seg(row)] for row in range(ROWS)], flags)
+        pre = dot(flat[1], columns_two[...])
+        gate = sigmoid(pre)
+        hidden = pre * gate
+        gate_two[at] = (gate + hidden - hidden * gate).astype(BF)
+        last_out[at] = keep_owned(hidden).astype(BF)
+        hidden = hidden.astype(BF)
+        change = dot(head[...], hidden)
+        total[...] += change[0:16]
+        lifted_total[...] += change[16:]
+
+    for row in range(ROWS):
+        shift = jnp.where(half == 0, LON - HALO, HALO)
+        final_out[:, seg(row)] = pltpu.roll(total[:, seg(row)], shift, 1)
 
 
 def ocean_kernel(
@@ -388,65 +391,72 @@
     scale, ids, window, flux_own, flux_strip, ocean_wire, back, head_back, lift_back,
     inputs, source, gate_one, gate_two, last,
     wire,
-    head_grad, flags, weight_total, small_total, taps, sources,
+    head_grad, flags, weight_total, small_total, taps_even, taps_odd, sources_even, sources_odd, grad_total,
 ):
-    step = pl.program_id(0)
     half = ids[0] % 2
+    all_taps = (taps_even, taps_odd)
+    all_sources = (sources_even, sources_odd)
     chosen = 1 - jnp.where(ids[0] // 2 == 0, 1, 0)
 
-    @pl.when(step == 0)
-    def _():
-        head_grad[0:8, :] = window[0:8, :] * scale
+    head_grad[0:8, :] = window[0:8, :] * scale
+    for row in range(ROWS):
+        place = row // 4
+        head_grad[8:16, seg(row)] = to_window(
+            flux_own[:, seg(row)], flux_strip[:, seg(place)], row, half
+        )
+        plain = window[8:16, seg(row)]
+        east = pltpu.roll(plain, LON - 1, 1)
+        west = pltpu.roll(plain, 1, 1)
+        for j in range(4):
+            flags[j : j + 1, seg(row)] = plain[2 + j : 3 + j]
+            flags[4 + j : 5 + j, seg(row)] = (east, west)[j % 2][2 + j : 3 + j]
+    for taps in all_taps:
+        for row, blocks in ((ROWS - 1, (1, 3, 4, 9, 10)), (0, (2, 5, 6, 11, 12))):
+            for j in blocks:
+                for at in range(2):
+                    taps[at, j * CH : (j + 1) * CH, seg(row)] = jnp.zeros((CH, LON), BF)
+    grad_total[...] = dot(head_back[...], head_grad[...].astype(BF))
+    weight_total[...] = jnp.zeros_like(weight_total)
+    small_total[...] = jnp.zeros_like(small_total)
+
+    for at in reversed(range(STEPS)):
+        taps = all_taps[at % 2]
+        sources = all_sources[at % 2]
         for row in range(ROWS):
-            place = row // 4
-            head_grad[8:16, seg(row)] = to_window(
-                flux_own[:, seg(row)], flux_strip[:, seg(place)], row, half
-            )
-            plain = window[8:16, seg(row)]
-            east = pltpu.roll(plain, LON - 1, 1)
-            west = pltpu.roll(plain, 1, 1)
-            for j in range(4):
-                flags[j : j + 1, seg(row)] = plain[2 + j : 3 + j]
-                flags[4 + j : 5 + j, seg(row)] = (east, west)[j % 2][2 + j : 3 + j]
-        taps[...] = jnp.zeros_like(taps)
-        weight_total[...] = jnp.zeros_like(weight_total)
-        small_total[...] = jnp.zeros_like(small_total)
-
-    for row in range(ROWS):
-        mid = source[0, :, seg(row)]
-        for place, value in enumerate((pltpu.roll(mid, 1, 1), mid, pltpu.roll(mid, LON - 1, 1))):
-            sources[place * CH : (place + 1) * CH, seg(row)] = keep_owned(value)
-    grad = head_grad[...].astype(BF)
-    slope_two = dot(head_back[...], grad) * gate_two[0].astype(F32)
-    build_back(taps, 1, split_rows(slope_two), flags)
-    slope_one = dot(back[1], taps[1]) * gate_one[0].astype(F32)
-    build_back(taps, 0, split_rows(slope_one), flags)
-    grad_lifted = dot(back[0], taps[0]).astype(BF)
-    head_grad[0:8, :] += dot(lift_back[...], grad_lifted)[0:8]
-    lift_weight = dot(inputs[0], grad_lifted, NT)
-    head_weight = dot(grad, last[0], NT)
-    small_total[...] += jnp.concatenate([lift_weight, head_weight], axis=1)
-    weight_total[...] += dot(taps[chosen, 0 : 7 * CH, :], sources[...], NT)
-
-    @pl.when(step == STEPS - 1)
-    def _():
-        def product(slope, side):
-            rows = weight_total[slope * CH : (slope + 1) * CH, :]
-            return rows[:, side * CH : (side + 1) * CH]
-
-        blocks = [product(0, 1), product(1, 1), product(2, 1), product(0, 0), product(0, 2)]
-        for j in range(4):
-            straight, side = 1 + j // 2, 2 * (j % 2)
-            turned_part = product(straight, side) - product(3 + j, side)
-            blocks.append(product(3 + j, 1) + turned_part)
-        for j in range(4):
-            pair = jnp.concatenate(blocks[2 * j : 2 * j + 2], axis=1)
-            wire[64 * j : 64 * j + 64, :] = pair.astype(BF)
-        pair = jnp.concatenate([blocks[8][0:32], blocks[8][32:64]], axis=1)
-        wire[256:288, :] = pair.astype(BF)
-        wire[288:304, :] = small_total[...].astype(BF)
-        wire[304:464, :] = ocean_wire[...]
-        wire[464:512, :] = jnp.zeros((48, LON), BF)
+            mid = source[at, :, seg(row)]
+            for place, value in enumerate((pltpu.roll(mid, 1, 1), mid, pltpu.roll(mid, LON - 1, 1))):
+                sources[place * CH : (place + 1) * CH, seg(row)] = keep_owned(value)
+        grad = head_grad[...].astype(BF)
+        slope_two = grad_total[...] * gate_two[at].astype(F32)
+        build_back(taps, 1, split_rows(slope_two), flags)
+        slope_one = dot(back[1], taps[1]) * gate_one[at].astype(F32)
+        build_back(taps, 0, split_rows(slope_one), flags)
+        grad_lifted = dot(back[0], taps[0]).astype(BF)
+        change = dot(lift_back[...], grad_lifted)
+        grad_total[...] += change[16:]
+        head_grad[0:8, :] += change[0:8]
+        lift_weight = dot(inputs[at], grad_lifted, NT)
+        head_weight = dot(grad, last[at], NT)
+        small_total[...] += jnp.concatenate([lift_weight, head_weight], axis=1)
+        weight_total[...] += dot(taps[chosen, 0 : 7 * CH, :], sources[...], NT)
+
+    def product(slope, side):
+        rows = weight_total[slope * CH : (slope + 1) * CH, :]
+        return rows[:, side * CH : (side + 1) * CH]
+
+    blocks = [product(0, 1), product(1, 1), product(2, 1), product(0, 0), product(0, 2)]
+    for j in range(4):
+        straight, side = 1 + j // 2, 2 * (j % 2)
+        turned_part = product(straight, side) - product(3 + j, side)
+        blocks.append(product(3 + j, 1) + turned_part)
+    for j in range(4):
+        pair = jnp.concatenate(blocks[2 * j : 2 * j + 2], axis=1)
+        wire[64 * j : 64 * j + 64, :] = pair.astype(BF)
+    pair = jnp.concatenate([blocks[8][0:32], blocks[8][32:64]], axis=1)
+    wire[256:288, :] = pair.astype(BF)
+    wire[288:304, :] = small_total[...].astype(BF)
+    wire[304:464, :] = ocean_wire[...]
+    wire[464:512, :] = jnp.zeros((48, LON), BF)
 
 
 def sum_kernel(sectors, devices, parts, out):
@@ -544,8 +554,8 @@
         weights_kernel,
         [
             ((CH, 16), BF),
-            ((16, CH), BF),
-            ((16, CH), BF),
+            ((16 + CH, CH), BF),
+            ((16 + CH, CH), BF),
             ((CH, 16), BF),
             ((2, CH, K * CH), BF),
             ((2, CH, 13 * CH), BF),
@@ -563,15 +573,6 @@
     hot, hot_back = call(hot_kernel, [((K, CELLS, CELLS), BF), ((K * CELLS, CELLS), BF)])(gathered)
     strip, hot, hot_back = lax.optimization_barrier((strip, hot, hot_back))
 
-    def whole(shape):
-        return pl.BlockSpec(shape, lambda s: (0,) * len(shape))
-
-    def at_step(shape):
-        return pl.BlockSpec((1,) + shape, lambda s: (s, 0, 0))
-
-    def at_step_back(shape):
-        return pl.BlockSpec((1,) + shape, lambda s: (STEPS - 1 - s, 0, 0))
-
     wide = (CH, WIN)
     history = [(16, WIN), wide, wide, wide, wide]
     inputs, source, gate_one, gate_two, last, window, final = call(
@@ -581,18 +582,12 @@
             pltpu.VMEM((24, WIN), F32),
             pltpu.VMEM((16, WIN), F32),
             pltpu.VMEM((K * CH, WIN), BF),
+            pltpu.VMEM((K * CH, WIN), BF),
             pltpu.VMEM((4, 16, WIN), BF),
+            pltpu.VMEM((8, WIN), F32),
+            pltpu.VMEM((CH, WIN), F32),
         ],
-        grid=(STEPS,),
-        in_specs=[
-            smem(),
-            whole((24, WIN)),
-            whole((24, CELLS)),
-            whole((CH, 16)),
-            whole((2, CH, K * CH)),
-            whole((16, CH)),
-        ],
-        out_specs=[at_step(shape) for shape in history] + [whole((16, WIN)), whole((16, WIN))],
+        in_specs=[smem()] + [vmem()] * 5,
     )(ids, features, strip, lift, flat, head)
 
     other_final = lax.ppermute(final, BOTH, partner)
@@ -627,21 +622,12 @@
             pltpu.VMEM((7 * CH, 3 * CH), F32),
             pltpu.VMEM((16, LON), F32),
             pltpu.VMEM((2, 13 * CH, WIN), BF),
+            pltpu.VMEM((2, 13 * CH, WIN), BF),
             pltpu.VMEM((3 * CH, WIN), BF),
+            pltpu.VMEM((3 * CH, WIN), BF),
+            pltpu.VMEM((CH, WIN), F32),
         ],
-        grid=(STEPS,),
-        in_specs=[
-            smem(),
-            whole((16, WIN)),
-            whole((8, WIN)),
-            whole((8, CELLS)),
-            whole((160, LON)),
-            whole((2, CH, 13 * CH)),
-            whole((CH, 16)),
-            whole((16, CH)),
-        ]
-        + [at_step_back(shape) for shape in history],
-        out_specs=[whole((WIRE, LON))],
+        in_specs=[smem()] + [vmem()] * 12,
     )(
         ids, window, flux_grad, flux_strip, ocean_wire, back, head_back, lift_back,
         inputs, source, gate_one, gate_two, last,

time: 92.2 us -> 88.5 us (0.960)
  Pallas kernels: 33.7 us -> 30.1 us
    pallas_call x1, Pallas kernels: 14.4 us -> 12.1 us  [shards(): call(functools.partial(backward_kernel, scale), [((WIRE, LON), BF)], scra...]
    pallas_call x1, Pallas kernels: 9.37 us -> 7.85 us  [shards(): call(forward_kernel, [((STEPS,) + shape, BF) for shape in history] + [((1...]
where the time goes in v4:
time: 88.5 us; the launch traced here: 88.2 us
  blocking collectives  45.7 us (52%)
  Pallas kernels  30.1 us (34%)
  starting transfers between devices  6.3 us (7%)
  waiting for transfers between devices  3.6 us (4%)
  local copies, waits for them, and re-layouts  1.92 us (2%)
    all_to_all x1, blocking collectives, shards(): sums = lax.all_to_all(sums, BOTH, 0, 0, tiled=True)  20 us
    all_to_all x1, blocking collectives, shards(): lax.all_to_all(wire.reshape(sectors, rows, LON), 'tile', 0, 0, tiled=True)  16.4 us
    pallas_call x1, Pallas kernels, shards(): call(functools.partial(backward_kernel, scale), [((WIRE, LON), BF)], scra...  12.1 us
    all_gather x1, blocking collectives, shards(): gathered = lax.all_gather(packed, 'group')  9.33 us
    pallas_call x1, Pallas kernels, shards(): call(forward_kernel, [((STEPS,) + shape, BF) for shape in history] + [((1...  7.85 us
    ppermute x1, starting transfers between devices, shards(): other_final = lax.ppermute(final, BOTH, partner)  5.23 us
    pallas_call x1, Pallas kernels, shards(): call(functools.partial(ocean_kernel, scale), [((8, CELLS), F32), ((8, WIN...  4.32 us
    ppermute x1, waiting for transfers between devices, shards(): flux_strip = lax.ppermute(flux_strip, BOTH, beside)  2.69 us
  transfers between devices with their start and end apart: 3, of which 2 were waited for; matrix products, arithmetic and copies ran while one was open for 0% of the time, Pallas kernels for 3%

profile of v4, /device:TPU:1, one launch (start us, length us, event | category | flops | bytes accessed | tf_op | source)
XLA Modules:
  0.0 88.2 jit_solution(9920824368930640748)
XLA Ops:
  0.6 1.6 %shard_map.153 = f32[32,384]{1,0:T(8,128)} custom-call(s32[1]{0:T(128)} %bitcast.ids, f32[8,384]{1,0:T(8,128)} %bitcast.17, f32[8,384]{1,0:T(8,128)} %bitcast.18, s32[9,1,384]{2,1,0:T(1,128)} %bitcast.16, s32[3,1,128]{2,1,0:T(1,128)} %sea.1, bf16[10,64]{1,0:T(8,128)(2,1)} %bitcast.19, bf16[12,64]{1,0:T(8,128)(2,1)} %atm_head.1, bf16[12,64]{1,0:T(8,128)(2,1)} %bitcast.20, ...), custom_call_target="tpu_custom_call" | custom-call | tf_op jit(solution)/shard_map/pallas_call | solution.py:533
  2.2 9.3 %all-gather = f32[128,384]{1,0:T(8,128)S(1)} all-gather(f32[32,384]{1,0:T(8,128)} %shard_map.153), channel_id=2, replica_groups=mesh['group'=4,'tile'=32] {'group'}, dimensions={0}, use_global_device_ids=true | all-gather | bytes 245760 | tf_op jit(solution)/shard_map/all_gather | solution.py:545
  11.5 0.3 shard_map.154
  11.9 1.1 %collective-permute-start = (f32[24,384]{1,0:T(8,128)S(1)}, f32[24,384]{1,0:T(8,128)S(1)}, u32[]{:S(2)}, u32[]{:S(2)}) collective-permute-start(f32[24,384]{1,0:T(8,128)S(1)} %get-tuple-element.47), channel_id=1, source_target_pairs={{0,63},{1,32},{2,33},{3,34},{4,35},{5,36},{6,37},{7,38},{8,39},{9,... | collective-permute-start | bytes 110600 | tf_op jit(solution)/shard_map/ppermute | solution.py:551
  12.9 1.6 %shard_map.155 = (bf16[9,384,384]{2,1,0:T(8,128)(2,1)S(1)}, bf16[3456,384]{1,0:T(8,128)(2,1)S(1)}) custom-call(f32[4,32,384]{2,1,0:T(8,128)S(1)} %bitcast.12), custom_call_target="tpu_custom_call" | custom-call | tf_op jit(solution)/shard_map/pallas_call | solution.py:573
  14.5 0.0 copy-start
  14.5 1.0 %copy-done = bf16[2,9,64,64]{3,2,1,0:T(8,128)(2,1)S(1)} copy-done((bf16[2,9,64,64]{3,2,1,0:T(8,128)(2,1)S(1)}, bf16[2,9,64,64]{3,2,1,0:T(8,128)(2,1)}, u32[]{:S(2)}) %copy-start) | copy-done | bytes 147480
  15.5 0.0 copy-start.1
  15.5 1.0 %copy-done.1 = bf16[2,9,64,64]{3,2,1,0:T(8,128)(2,1)S(1)} copy-done((bf16[2,9,64,64]{3,2,1,0:T(8,128)(2,1)S(1)}, bf16[2,9,64,64]{3,2,1,0:T(8,128)(2,1)}, u32[]{:S(2)}) %copy-start.1) | copy-done | bytes 147480
  16.5 0.6 shard_map.156
  17.1 0.0 collective-permute-done.strip
  17.1 7.8 %shard_map.157 = (bf16[8,16,1152]{2,1,0:T(8,128)(2,1)S(1)}, bf16[8,64,1152]{2,1,0:T(8,128)(2,1)S(1)}, bf16[8,64,1152]{2,1,0:T(8,128)(2,1)S(1)}, bf16[8,64,1152]{...) custom-call(s32[1]{0:T(128)} %bitcast.ids, ...), custom_call_target="tpu_custom_call" | custom-call | tf_op jit(solution)/shard_map/pallas_call | solution.py:578
  25.0 5.2 %collective-permute-start.1 = (f32[16,1152]{1,0:T(8,128)S(1)}, f32[16,1152]{1,0:T(8,128)S(1)}, u32[]{:S(2)}, u32[]{:S(2)}) collective-permute-start(f32[16,1152]{1,0:T(8,128)S(1)} %get-tuple-element.54.own), channel_id=1, source_target_pairs={{0,32},{1,33},{2,34},{3,35},{4,36},{5,37},{6,38},{7,39},{8,40},{9,... | collective-permute-start | bytes 221192 | tf_op jit(solution)/shard_map/ppermute | solution.py:593
  30.2 0.9 %collective-permute-done.1.other = f32[16,1152]{1,0:T(8,128)S(1)} collective-permute-done((f32[16,1152]{1,0:T(8,128)S(1)}, f32[16,1152]{1,0:T(8,128)S(1)}, u32[]{:S(2)}, u32[]{:S(2)}) %collective-permute-start.1) | collective-permute-done | bytes 73760 | tf_op jit(solution)/shard_map/ppermute | solution.py:593
  31.1 4.3 %shard_map.158 = (f32[8,384]{1,0:T(8,128)}, f32[8,1152]{1,0:T(8,128)S(1)}, f32[8,384]{1,0:T(8,128)S(1)}, bf16[2,576,384]{2,1,0:T(8,128)(2,1)S(1)}, bf16[2,64,384...) custom-call(s32[1]{0:T(128)} %bitcast.ids, f32[4,32,384]{2,1,0:T(8,128)S(1)} %bitcast.14, ...), custom_call_target="tpu_custom_call" | custom-call | tf_op jit(solution)/shard_map/pallas_call | solution.py:594
  35.4 0.0 collective-permute-start.2
  35.4 0.4 shard_map.159.ocean_wire
  35.8 2.7 %collective-permute-done.2.flux_strip = f32[8,384]{1,0:T(8,128)S(1)} collective-permute-done((f32[8,384]{1,0:T(8,128)S(1)}, f32[8,384]{1,0:T(8,128)S(1)}, u32[]{:S(2)}, u32[]{:S(2)}) %collective-permute-start.2) | collective-permute-done | bytes 12320 | tf_op jit(solution)/shard_map/ppermute | solution.py:611
  38.5 12.1 %shard_map.160 = bf16[512,128]{1,0:T(8,128)(2,1)S(1)} custom-call(s32[1]{0:T(128)} %bitcast.ids, f32[16,1152]{1,0:T(8,128)S(1)} %get-tuple-element.64.window, f32[8,1152]{1,0:T(8,128)S(1)} %get-tuple-element.65.flux_own, f32[8,384]{1,0:T(8,128)S(1)} %collective-permute-done.2.flux_strip, bf16[160,128]{1,0:T(8,128)(2,1)S(1)} %shard_map.159.ocean_wire, ...), custom_call_target="tpu_custom_call" | custom-call | tf_op jit(solution)/shard_map/pallas_call | solution.py:616
  50.6 16.4 %all_to_all.10.parts = bf16[32,16,128]{2,1,0:T(8,128)(2,1)S(1)} all-to-all(bf16[32,16,128]{2,1,0:T(8,128)(2,1)S(1)} %bitcast.15), channel_id=1, replica_groups=mesh['group'=4,'tile'=32] {'tile'}, dimensions={0} | all-to-all | bytes 262144 | tf_op jit(solution)/shard_map/all_to_all | solution.py:636
  67.0 0.1 shard_map.161
  67.1 20.0 %all_to_all.11.parts = bf16[128,16,128]{2,1,0:T(8,128)(2,1)S(1)} all-to-all(bf16[128,16,128]{2,1,0:T(8,128)(2,1)S(1)} %shard_map.161), channel_id=1, replica_groups=mesh['group'=4,'tile'=32] {'group','tile'}, dimensions={0} | all-to-all | bytes 1048576 | tf_op jit(solution)/shard_map/all_to_all | solution.py:640
  87.1 1.2 %shard_map.162 = (f32[10,64]{1,0:T(8,128)}, f32[2,9,64,64]{3,2,1,0:T(8,128)}, f32[12,64]{1,0:T(8,128)}, f32[12,64]{1,0:T(8,128)}, f32[2,9,64,64]{3,2,1,0:T(8,128)}, /*index=5*/f32[8,64]{1,0:T(8,128)}) custom-call(bf16[128,16,128]{2,1,0:T(8,128)(2,1)S(1)} %all_to_all.11.parts), custom_call_target="tpu_custom_call" | custom-call | tf_op jit(solution)/shard_map/pallas_call | solution.py:641
Async XLA Ops:
  11.9 5.2 %collective-permute-start = (f32[24,384]{1,0:T(8,128)S(1)}, f32[24,384]{1,0:T(8,128)S(1)}, u32[]{:S(2)}, u32[]{:S(2)}) collective-permute-start(f32[24,384]{1,0:T(8,128)S(1)} %get-tuple-element.47), channel_id=1, source_target_pairs={{0,63},{1,32},{2,33},{3,34},{4,35},{5,36},{6,37},{7,38},{8,39},{9,... | collective-permute-start | bytes 110600 | tf_op jit(solution)/shard_map/ppermute | solution.py:551
  14.5 1.0 %copy-start = (bf16[2,9,64,64]{3,2,1,0:T(8,128)(2,1)S(1)}, bf16[2,9,64,64]{3,2,1,0:T(8,128)(2,1)}, u32[]{:S(2)}) copy-start(bf16[2,9,64,64]{3,2,1,0:T(8,128)(2,1)} %atm_conv.1) | copy-start | bytes 442372
  15.5 1.0 %copy-start.1 = (bf16[2,9,64,64]{3,2,1,0:T(8,128)(2,1)S(1)}, bf16[2,9,64,64]{3,2,1,0:T(8,128)(2,1)}, u32[]{:S(2)}) copy-start(bf16[2,9,64,64]{3,2,1,0:T(8,128)(2,1)} %ocn_conv.1) | copy-start | bytes 442372
  25.0 6.1 %collective-permute-start.1 = (f32[16,1152]{1,0:T(8,128)S(1)}, f32[16,1152]{1,0:T(8,128)S(1)}, u32[]{:S(2)}, u32[]{:S(2)}) collective-permute-start(f32[16,1152]{1,0:T(8,128)S(1)} %get-tuple-element.54.own), channel_id=1, source_target_pairs={{0,32},{1,33},{2,34},{3,35},{4,36},{5,37},{6,38},{7,39},{8,40},{9,... | collective-permute-start | bytes 221192 | tf_op jit(solution)/shard_map/ppermute | solution.py:593
  35.4 3.1 %collective-permute-start.2 = (f32[8,384]{1,0:T(8,128)S(1)}, f32[8,384]{1,0:T(8,128)S(1)}, u32[]{:S(2)}, u32[]{:S(2)}) collective-permute-start(f32[8,384]{1,0:T(8,128)S(1)} %get-tuple-element.66), channel_id=1, source_target_pairs={{0,63},{1,32},{2,33},{3,34},{4,35},{5,36},{6,37},{7,38},{8,39},{9,... | collective-permute-start | bytes 36872 | tf_op jit(solution)/shard_map/ppermute | solution.py:611

commit v5 on v4

--- a/solution.py
+++ b/solution.py
@@ -6,6 +6,7 @@
 from jax import lax
 from jax.experimental import pallas as pl
 from jax.experimental.pallas import tpu as pltpu
+from jax.sharding import Mesh
 from jax.sharding import PartitionSpec as P
 
 STEPS = 8
@@ -17,13 +18,18 @@
 CH = 64
 HALO = 32
 WIRE = 512
-BOTH = ("group", "tile")
+GROUP = ("high", "core")
+BOTH = ("high", "core", "tile")
 BF = jnp.bfloat16
 F32 = jnp.float32
 INTERPRET = False
 VMEM_LIMIT = 24 * 1024 * 1024
 WHOLE_VMEM = 62 * 1024 * 1024
-BACK = (0, 1, 2, 5, 6, 7, 8, 3, 4, 5, 6, 7, 8)
+BACK = (
+    ((0, 1), (1, 1), (2, 1), (5, 1), (6, 1), (7, 1), (8, 1)),
+    ((3, 1), (5, 1), (7, 1), (5, -1), None, (7, -1), None),
+    ((4, 1), (6, 1), (8, 1), None, (6, -1), None, (8, -1)),
+)
 
 NN = (((1,), (0,)), ((), ()))
 NT = (((1,), (1,)), ((), ()))
@@ -149,7 +155,12 @@
         blocks = [atm_conv[index, k] for k in range(K)]
         flat[index] = jnp.concatenate(blocks, axis=1)
         blocks = [turned(block) for block in blocks]
-        back[index] = jnp.concatenate([blocks[k] for k in BACK], axis=1)
+        for side, terms in enumerate(BACK):
+            parts = [
+                jnp.zeros((CH, CH), BF) if term is None else blocks[term[0]] * term[1]
+                for term in terms
+            ]
+            back[index, side * CH : (side + 1) * CH, :] = jnp.concatenate(parts, axis=1)
         blocks = [ocn_conv[index, k] for k in range(K)]
         ocean_flat[index] = jnp.concatenate(blocks, axis=1)
         for k in range(K):
@@ -163,9 +174,10 @@
     cell_rows = lax.broadcasted_iota(jnp.int32, (CELLS, CELLS), 0)
     cell_lanes = lane_ids((CELLS, CELLS))
     for k in range(K):
+        place = slice(k * CELLS, (k + 1) * CELLS)
         hot[k] = jnp.where(cell_rows == table[k : k + 1], 1.0, 0.0).astype(BF)
         target = columns[:, k : k + 1]
-        hot_back[k * CELLS : (k + 1) * CELLS, :] = jnp.where(cell_lanes == target, 1.0, 0.0).astype(BF)
+        hot_back[place, :] = jnp.where(cell_lanes == target, 1.0, 0.0).astype(BF)
 
 
 def one_hot_sea(row):
@@ -223,24 +235,27 @@
 
 def build_back(out, at, rows, flags):
     mid = [piece.astype(BF) for piece in rows]
-    from_east = [pltpu.roll(piece, LON - 1, 1).astype(BF) for piece in rows]
-    from_west = [pltpu.roll(piece, 1, 1).astype(BF) for piece in rows]
     zero = jnp.zeros((CH, LON), BF)
-
-    def flag(index, row):
-        return flags[index : index + 1, seg(row)] > 0.5
-
     for row in range(ROWS):
-        blocks = {0: mid[row], 7: from_east[row], 8: from_west[row]}
+        blocks = {0: mid[row]}
         for source, straight, first in ((row + 1, 1, 0), (row - 1, 2, 2)):
             if 0 <= source < ROWS:
                 blocks[straight] = mid[source]
-                blocks[3 + first] = jnp.where(flag(first, source), mid[source], zero)
-                blocks[4 + first] = jnp.where(flag(first + 1, source), mid[source], zero)
-                blocks[9 + first] = jnp.where(flag(4 + first, source), zero, from_east[source])
-                blocks[10 + first] = jnp.where(flag(5 + first, source), zero, from_west[source])
+                for j in (first, first + 1):
+                    flag = flags[j : j + 1, seg(source)] > 0.5
+                    blocks[3 + j] = jnp.where(flag, mid[source], zero)
         for j, value in blocks.items():
             out[at, j * CH : (j + 1) * CH, seg(row)] = value
+
+
+def join_sides(value):
+    rows = []
+    for row in range(ROWS):
+        here = value[0:CH, seg(row)]
+        west = pltpu.roll(value[CH : 2 * CH, seg(row)], LON - 1, 1)
+        east = pltpu.roll(value[2 * CH : 3 * CH, seg(row)], 1, 1)
+        rows.append(here + west + east)
+    return rows
 
 
 def split_rows(value):
@@ -287,14 +302,14 @@
         gate = sigmoid(pre)
         hidden = pre * gate
         gate_one[at] = (gate + hidden - hidden * gate).astype(BF)
-        source_out[at] = jnp.where(first, lifted, hidden).astype(BF)
+        source_out[at] = jnp.where(first, columns[0:CH, :], hidden.astype(BF))
         build_columns(columns_two, [hidden[:, seg(row)] for row in range(ROWS)], flags)
         pre = dot(flat[1], columns_two[...])
         gate = sigmoid(pre)
         hidden = pre * gate
         gate_two[at] = (gate + hidden - hidden * gate).astype(BF)
-        last_out[at] = keep_owned(hidden).astype(BF)
         hidden = hidden.astype(BF)
+        last_out[at] = hidden
         change = dot(head[...], hidden)
         total[...] += change[0:16]
         lifted_total[...] += change[16:]
@@ -404,14 +419,9 @@
         head_grad[8:16, seg(row)] = to_window(
             flux_own[:, seg(row)], flux_strip[:, seg(place)], row, half
         )
-        plain = window[8:16, seg(row)]
-        east = pltpu.roll(plain, LON - 1, 1)
-        west = pltpu.roll(plain, 1, 1)
-        for j in range(4):
-            flags[j : j + 1, seg(row)] = plain[2 + j : 3 + j]
-            flags[4 + j : 5 + j, seg(row)] = (east, west)[j % 2][2 + j : 3 + j]
+    flags[0:4, :] = window[10:14, :]
     for taps in all_taps:
-        for row, blocks in ((ROWS - 1, (1, 3, 4, 9, 10)), (0, (2, 5, 6, 11, 12))):
+        for row, blocks in ((ROWS - 1, (1, 3, 4)), (0, (2, 5, 6))):
             for j in blocks:
                 for at in range(2):
                     taps[at, j * CH : (j + 1) * CH, seg(row)] = jnp.zeros((CH, LON), BF)
@@ -429,16 +439,19 @@
         grad = head_grad[...].astype(BF)
         slope_two = grad_total[...] * gate_two[at].astype(F32)
         build_back(taps, 1, split_rows(slope_two), flags)
-        slope_one = dot(back[1], taps[1]) * gate_one[at].astype(F32)
-        build_back(taps, 0, split_rows(slope_one), flags)
-        grad_lifted = dot(back[0], taps[0]).astype(BF)
+        grad_one = join_sides(dot(back[1], taps[1]))
+        slope_one = [
+            grad_one[row] * gate_one[at, :, seg(row)].astype(F32) for row in range(ROWS)
+        ]
+        build_back(taps, 0, slope_one, flags)
+        grad_lifted = jnp.concatenate(join_sides(dot(back[0], taps[0])), axis=1).astype(BF)
         change = dot(lift_back[...], grad_lifted)
         grad_total[...] += change[16:]
         head_grad[0:8, :] += change[0:8]
         lift_weight = dot(inputs[at], grad_lifted, NT)
-        head_weight = dot(grad, last[at], NT)
+        head_weight = dot(keep_owned(grad), last[at], NT)
         small_total[...] += jnp.concatenate([lift_weight, head_weight], axis=1)
-        weight_total[...] += dot(taps[chosen, 0 : 7 * CH, :], sources[...], NT)
+        weight_total[...] += dot(taps[chosen], sources[...], NT)
 
     def product(slope, side):
         rows = weight_total[slope * CH : (slope + 1) * CH, :]
@@ -468,36 +481,39 @@
         out[place] = total
 
 
-def final_kernel(
-    sectors, rows, parts, g_lift, g_conv, g_head, o_lift, o_conv, o_head, sums
-):
-    for group in range(4):
-        for sector in range(sectors):
-            piece = parts[group * sectors + sector].astype(F32)
-            sums[group, sector * rows : (sector + 1) * rows, :] = piece
+def final_kernel(sectors, rows, ids, own, other, g_lift, g_conv, g_head, o_lift, o_conv, o_head):
+    def piece(group, start):
+        place = (group // 2) * sectors + start // rows
+        at = slice(start % rows, start % rows + 16)
+        value = jnp.where(ids[0] % 2 == group % 2, own[place, at, :], other[place, at, :])
+        return value.astype(F32)
+
+    def spread(out, index, j, at, value):
+        out[index, 2 * j, at : at + 16, :] = value[:, 0:64]
+        out[index, 2 * j + 1, at : at + 16, :] = value[:, 64:128]
+
     for index in range(2):
         low, high = 2 * index, 2 * index + 1
         for j in range(4):
-            pair = sums[low, 64 * j : 64 * j + 64, :] + sums[high, 64 * j : 64 * j + 64, :]
-            g_conv[index, 2 * j] = pair[:, 0:64]
-            g_conv[index, 2 * j + 1] = pair[:, 64:128]
-            upper = sums[low, 304 + 32 * j : 336 + 32 * j, :]
-            lower = sums[high, 304 + 32 * j : 336 + 32 * j, :]
-            o_conv[index, 2 * j, 0:32] = upper[:, 0:64]
-            o_conv[index, 2 * j, 32:64] = lower[:, 0:64]
-            o_conv[index, 2 * j + 1, 0:32] = upper[:, 64:128]
-            o_conv[index, 2 * j + 1, 32:64] = lower[:, 64:128]
-        pair = sums[low, 256:288, :] + sums[high, 256:288, :]
-        g_conv[index, 8, 0:32] = pair[:, 0:64]
-        g_conv[index, 8, 32:64] = pair[:, 64:128]
+            for at in range(0, 64, 16):
+                start = 64 * j + at
+                spread(g_conv, index, j, at, piece(low, start) + piece(high, start))
+            for at in range(0, 32, 16):
+                start = 304 + 32 * j + at
+                spread(o_conv, index, j, at, piece(low, start))
+                spread(o_conv, index, j, at + 32, piece(high, start))
+        for at in range(0, 32, 16):
+            pair = piece(low, 256 + at) + piece(high, 256 + at)
+            g_conv[index, 8, at : at + 16, :] = pair[:, 0:64]
+            g_conv[index, 8, at + 32 : at + 48, :] = pair[:, 64:128]
         for side, at in ((low, 0), (high, 32)):
-            piece = sums[side, 432:448, :]
-            o_conv[index, 8, at : at + 16] = piece[:, 0:64]
-            o_conv[index, 8, at + 16 : at + 32] = piece[:, 64:128]
-    small = sums[0, 288:304, :] + sums[1, 288:304, :]
+            value = piece(side, 432)
+            o_conv[index, 8, at : at + 16, :] = value[:, 0:64]
+            o_conv[index, 8, at + 16 : at + 32, :] = value[:, 64:128]
+    small = piece(0, 288) + piece(1, 288)
     g_lift[...] = small[0:10, 0:64]
     g_head[...] = small[0:12, 64:128]
-    small = sums[0, 448:464, :]
+    small = piece(0, 448)
     o_lift[...] = small[0:12, 0:64]
     o_head[...] = small[0:8, 64:128]
 
@@ -518,7 +534,7 @@
     devices = 4 * sectors
     rows = WIRE // sectors
     scale = 1.0 / math.sqrt(devices * CELLS)
-    group = lax.axis_index("group")
+    group = 2 * lax.axis_index("high") + lax.axis_index("core")
     ids = group.astype(jnp.int32).reshape(1)
 
     partner = []
@@ -542,7 +558,7 @@
         in_specs=[smem()] + [hbm()] * 8,
         limit=WHOLE_VMEM,
     )(ids, state[0, 0], cotangent[0, 0], neighbours.reshape(K, 1, CELLS), sea_cells, *lifts)
-    gathered = lax.all_gather(packed, "group")
+    gathered = lax.all_gather(packed, GROUP)
     features, strip = call(
         sector_kernel,
         [((24, WIN), F32), ((24, CELLS), F32)],
@@ -558,7 +574,7 @@
             ((16 + CH, CH), BF),
             ((CH, 16), BF),
             ((2, CH, K * CH), BF),
-            ((2, CH, 13 * CH), BF),
+            ((2, 3 * CH, 7 * CH), BF),
             ((CH, 16), BF),
             ((16, CH), BF),
             ((16, CH), BF),
@@ -621,8 +637,8 @@
             pltpu.VMEM((8, WIN), F32),
             pltpu.VMEM((7 * CH, 3 * CH), F32),
             pltpu.VMEM((16, LON), F32),
-            pltpu.VMEM((2, 13 * CH, WIN), BF),
-            pltpu.VMEM((2, 13 * CH, WIN), BF),
+            pltpu.VMEM((2, 7 * CH, WIN), BF),
+            pltpu.VMEM((2, 7 * CH, WIN), BF),
             pltpu.VMEM((3 * CH, WIN), BF),
             pltpu.VMEM((3 * CH, WIN), BF),
             pltpu.VMEM((CH, WIN), F32),
@@ -635,9 +651,10 @@
 
     parts = lax.all_to_all(wire.reshape(sectors, rows, LON), "tile", 0, 0, tiled=True)
     (sums,) = call(
-        functools.partial(sum_kernel, sectors, devices), [((devices, rows, LON), BF)]
+        functools.partial(sum_kernel, sectors, 2 * sectors), [((2 * sectors, rows, LON), BF)]
     )(parts)
-    sums = lax.all_to_all(sums, BOTH, 0, 0, tiled=True)
+    sums = lax.all_to_all(sums, ("high", "tile"), 0, 0, tiled=True)
+    other_sums = lax.ppermute(sums, "core", [(0, 1), (1, 0)])
     totals = call(
         functools.partial(final_kernel, sectors, rows),
         [
@@ -648,28 +665,20 @@
             ((2, K, CH, CH), F32),
             ((8, CH), F32),
         ],
-        scratch=[pltpu.VMEM((4, WIRE, LON), F32)],
-    )(sums)
+        in_specs=[smem(), vmem(), vmem()],
+    )(ids, sums, other_sums)
     g_lift, g_conv, g_head, o_lift, o_conv, o_head = totals
     return (next_state[None, None], g_lift.T, g_conv, g_head, o_lift.T, o_conv, o_head)
 
 
 def solution(mesh):
+    high, sectors = mesh.devices.shape[0] // 2, mesh.devices.shape[1]
+    split = Mesh(mesh.devices.reshape(high, 2, sectors), BOTH)
+    block = P(GROUP, "tile", None, None)
     return jax.shard_map(
         shards,
-        mesh=mesh,
-        in_specs=(
-            P("group", "tile", None, None),
-            P("group", "tile", None, None),
-            P("group", "tile", None, None),
-            P(None, "tile", None),
-            P(),
-            P(),
-            P(),
-            P(),
-            P(),
-            P(),
-        ),
-        out_specs=(P("group", "tile", None, None), P(), P(), P(), P(), P(), P()),
+        mesh=split,
+        in_specs=(block, block, block, P(None, "tile", None), P(), P(), P(), P(), P(), P()),
+        out_specs=(block, P(), P(), P(), P(), P(), P()),
         check_vma=False,
     )

time: 88.5 us -> 87.3 us (0.986)
  blocking collectives: 45.7 us -> 42.4 us
  starting transfers between devices: 6.3 us -> 7.71 us
  waiting for transfers between devices: 3.6 us -> 4.76 us
    all_to_all x1, blocking collectives: 20 us -> 16.7 us  [shards(): sums = lax.all_to_all(sums, ('high', 'tile'), 0, 0, tiled=True)]
    ppermute x0 -> x1, starting transfers between devices: none -> 1.42 us  [shards(): other_sums = lax.ppermute(sums, 'core', [(0, 1), (1, 0)])]
    ppermute x0 -> x1, waiting for transfers between devices: none -> 1.16 us  [shards(): other_sums = lax.ppermute(sums, 'core', [(0, 1), (1, 0)])]
  transfers between devices with their start and end apart: 3 -> 4, of which waited for: 2 -> 3; matrix products, arithmetic and copies ran while one was open for 0% -> 0% of each run, Pallas kernels for 3% -> 3%
where the time goes in v5:
time: 87.3 us; the launch traced here: 87 us
  blocking collectives  42.4 us (49%)
  Pallas kernels  29.5 us (34%)
  starting transfers between devices  7.71 us (9%)
  waiting for transfers between devices  4.76 us (5%)
  local copies, waits for them, and re-layouts  1.92 us (2%)
    all_to_all x1, blocking collectives, shards(): sums = lax.all_to_all(sums, ('high', 'tile'), 0, 0, tiled=True)  16.7 us
    all_to_all x1, blocking collectives, shards(): lax.all_to_all(wire.reshape(sectors, rows, LON), 'tile', 0, 0, tiled=True)  16.4 us
    pallas_call x1, Pallas kernels, shards(): call(functools.partial(backward_kernel, scale), [((WIRE, LON), BF)], scra...  11.6 us
    all_gather x1, blocking collectives, shards(): gathered = lax.all_gather(packed, GROUP)  9.33 us
    pallas_call x1, Pallas kernels, shards(): call(forward_kernel, [((STEPS,) + shape, BF) for shape in history] + [((1...  7.84 us
    ppermute x1, starting transfers between devices, shards(): other_final = lax.ppermute(final, BOTH, partner)  5.22 us
    pallas_call x1, Pallas kernels, shards(): call(functools.partial(ocean_kernel, scale), [((8, CELLS), F32), ((8, WIN...  4.32 us
    ppermute x1, waiting for transfers between devices, shards(): flux_strip = lax.ppermute(flux_strip, BOTH, beside)  2.68 us
  transfers between devices with their start and end apart: 4, of which 3 were waited for; matrix products, arithmetic and copies ran while one was open for 0% of the time, Pallas kernels for 3%

profile of v5, /device:TPU:1, one launch (start us, length us, event | category | flops | bytes accessed | tf_op | source)
XLA Modules:
  0.0 87.0 jit_solution(16177825358620101186)
XLA Ops:
  0.6 1.6 %shard_map.153 = f32[32,384]{1,0:T(8,128)} custom-call(s32[1]{0:T(128)} %bitcast.ids, f32[8,384]{1,0:T(8,128)} %bitcast.17, f32[8,384]{1,0:T(8,128)} %bitcast.18, s32[9,1,384]{2,1,0:T(1,128)} %bitcast.16, s32[3,1,128]{2,1,0:T(1,128)} %sea.1, bf16[10,64]{1,0:T(8,128)(2,1)} %bitcast.19, bf16[12,64]{1,0:T(8,128)(2,1)} %atm_head.1, bf16[12,64]{1,0:T(8,128)(2,1)} %bitcast.20, ...), custom_call_target="tpu_custom_call" | custom-call | tf_op jit(solution)/shard_map/pallas_call | solution.py:549
  2.2 9.3 %all-gather = f32[128,384]{1,0:T(8,128)S(1)} all-gather(f32[32,384]{1,0:T(8,128)} %shard_map.153), channel_id=2, replica_groups=mesh['high'=2,'core'=2,'tile'=32] {'high','core'}, dimensions={0}, use_global_device_ids=true | all-gather | bytes 245760 | tf_op jit(solution)/shard_map/all_gather | solution.py:561
  11.5 0.3 shard_map.154
  11.9 1.1 %collective-permute-start = (f32[24,384]{1,0:T(8,128)S(1)}, f32[24,384]{1,0:T(8,128)S(1)}, u32[]{:S(2)}, u32[]{:S(2)}) collective-permute-start(f32[24,384]{1,0:T(8,128)S(1)} %get-tuple-element.47), channel_id=1, source_target_pairs={{0,63},{1,32},{2,33},{3,34},{4,35},{5,36},{6,37},{7,38},{8,39},{9,... | collective-permute-start | bytes 110600 | tf_op jit(solution)/shard_map/ppermute | solution.py:567
  12.9 1.6 %shard_map.155 = (bf16[9,384,384]{2,1,0:T(8,128)(2,1)S(1)}, bf16[3456,384]{1,0:T(8,128)(2,1)S(1)}) custom-call(f32[4,32,384]{2,1,0:T(8,128)S(1)} %bitcast.12), custom_call_target="tpu_custom_call" | custom-call | tf_op jit(solution)/shard_map/pallas_call | solution.py:589
  14.5 0.0 copy-start
  14.5 1.0 %copy-done = bf16[2,9,64,64]{3,2,1,0:T(8,128)(2,1)S(1)} copy-done((bf16[2,9,64,64]{3,2,1,0:T(8,128)(2,1)S(1)}, bf16[2,9,64,64]{3,2,1,0:T(8,128)(2,1)}, u32[]{:S(2)}) %copy-start) | copy-done | bytes 147480
  15.5 0.0 copy-start.1
  15.5 1.0 %copy-done.1 = bf16[2,9,64,64]{3,2,1,0:T(8,128)(2,1)S(1)} copy-done((bf16[2,9,64,64]{3,2,1,0:T(8,128)(2,1)S(1)}, bf16[2,9,64,64]{3,2,1,0:T(8,128)(2,1)}, u32[]{:S(2)}) %copy-start.1) | copy-done | bytes 147480
  16.5 0.7 shard_map.156
  17.1 0.0 collective-permute-done.strip
  17.1 7.8 %shard_map.157 = (bf16[8,16,1152]{2,1,0:T(8,128)(2,1)S(1)}, bf16[8,64,1152]{2,1,0:T(8,128)(2,1)S(1)}, bf16[8,64,1152]{2,1,0:T(8,128)(2,1)S(1)}, bf16[8,64,1152]{...) custom-call(s32[1]{0:T(128)} %bitcast.ids, ...), custom_call_target="tpu_custom_call" | custom-call | tf_op jit(solution)/shard_map/pallas_call | solution.py:594
  25.0 5.2 %collective-permute-start.1 = (f32[16,1152]{1,0:T(8,128)S(1)}, f32[16,1152]{1,0:T(8,128)S(1)}, u32[]{:S(2)}, u32[]{:S(2)}) collective-permute-start(f32[16,1152]{1,0:T(8,128)S(1)} %get-tuple-element.54.own), channel_id=1, source_target_pairs={{0,32},{1,33},{2,34},{3,35},{4,36},{5,37},{6,38},{7,39},{8,40},{9,... | collective-permute-start | bytes 221192 | tf_op jit(solution)/shard_map/ppermute | solution.py:609
  30.2 0.9 %collective-permute-done.1.other = f32[16,1152]{1,0:T(8,128)S(1)} collective-permute-done((f32[16,1152]{1,0:T(8,128)S(1)}, f32[16,1152]{1,0:T(8,128)S(1)}, u32[]{:S(2)}, u32[]{:S(2)}) %collective-permute-start.1) | collective-permute-done | bytes 73760 | tf_op jit(solution)/shard_map/ppermute | solution.py:609
  31.1 4.3 %shard_map.158 = (f32[8,384]{1,0:T(8,128)}, f32[8,1152]{1,0:T(8,128)S(1)}, f32[8,384]{1,0:T(8,128)S(1)}, bf16[2,576,384]{2,1,0:T(8,128)(2,1)S(1)}, bf16[2,64,384...) custom-call(s32[1]{0:T(128)} %bitcast.ids, f32[4,32,384]{2,1,0:T(8,128)S(1)} %bitcast.14, ...), custom_call_target="tpu_custom_call" | custom-call | tf_op jit(solution)/shard_map/pallas_call | solution.py:610
  35.4 0.0 collective-permute-start.2
  35.4 0.4 shard_map.159.ocean_wire
  35.9 2.7 %collective-permute-done.2.flux_strip = f32[8,384]{1,0:T(8,128)S(1)} collective-permute-done((f32[8,384]{1,0:T(8,128)S(1)}, f32[8,384]{1,0:T(8,128)S(1)}, u32[]{:S(2)}, u32[]{:S(2)}) %collective-permute-start.2) | collective-permute-done | bytes 12320 | tf_op jit(solution)/shard_map/ppermute | solution.py:627
  38.5 11.6 %shard_map.160 = bf16[512,128]{1,0:T(8,128)(2,1)S(1)} custom-call(s32[1]{0:T(128)} %bitcast.ids, f32[16,1152]{1,0:T(8,128)S(1)} %get-tuple-element.64.window, f32[8,1152]{1,0:T(8,128)S(1)} %get-tuple-element.65.flux_own, f32[8,384]{1,0:T(8,128)S(1)} %collective-permute-done.2.flux_strip, bf16[160,128]{1,0:T(8,128)(2,1)S(1)} %shard_map.159.ocean_wire, ...), custom_call_target="tpu_custom_call" | custom-call | tf_op jit(solution)/shard_map/pallas_call | solution.py:632
  50.1 16.4 %all_to_all.10.parts = bf16[32,16,128]{2,1,0:T(8,128)(2,1)S(1)} all-to-all(bf16[32,16,128]{2,1,0:T(8,128)(2,1)S(1)} %bitcast.15), channel_id=1, replica_groups=mesh['high'=2,'core'=2,'tile'=32] {'tile'}, dimensions={0} | all-to-all | bytes 262144 | tf_op jit(solution)/shard_map/all_to_all | solution.py:652
  66.5 0.1 shard_map.161
  66.5 16.7 %all_to_all.11.own = bf16[64,16,128]{2,1,0:T(8,128)(2,1)S(1)} all-to-all(bf16[64,16,128]{2,1,0:T(8,128)(2,1)S(1)} %shard_map.161), channel_id=1, replica_groups=mesh['high'=2,'core'=2,'tile'=32] {'high','tile'}, dimensions={0} | all-to-all | bytes 524288 | tf_op jit(solution)/shard_map/all_to_all | solution.py:656
  83.2 1.4 %collective-permute-start.3 = (bf16[64,16,128]{2,1,0:T(8,128)(2,1)S(1)}, bf16[64,16,128]{2,1,0:T(8,128)(2,1)S(1)}, u32[]{:S(2)}, u32[]{:S(2)}) collective-permute-start(bf16[64,16,128]{2,1,0:T(8,128)(2,1)S(1)} %all_to_all.11.own), channel_id=1, source_target_pairs={{0,32},{32,0},{1,33},{33,1},{2,34},{34,2},{3,35},{35,3},{4,36},{36... | collective-permute-start | bytes 786440 | tf_op jit(solution)/shard_map/ppermute | solution.py:657
  84.7 1.2 %collective-permute-done.3.other = bf16[64,16,128]{2,1,0:T(8,128)(2,1)S(1)} collective-permute-done((bf16[64,16,128]{2,1,0:T(8,128)(2,1)S(1)}, bf16[64,16,128]{2,1,0:T(8,128)(2,1)S(1)}, u32[]{:S(2)}, u32[]{:S(2)}) %collective-permute-start.3) | collective-permute-done | bytes 262176 | tf_op jit(solution)/shard_map/ppermute | solution.py:657
  85.8 1.2 %shard_map.162 = (f32[10,64]{1,0:T(8,128)}, f32[2,9,64,64]{3,2,1,0:T(8,128)}, f32[12,64]{1,0:T(8,128)}, f32[12,64]{1,0:T(8,128)}, f32[2,9,64,64]{3,2,1,0:T(8,128)}, /*index=5*/f32[8,64]{1,0:T(8,128)}) custom-call(s32[1]{0:T(128)} %bitcast.ids, bf16[64,16,128]{2,1,0:T(8,128)(2,1)S(1)} %all_to_all.11.own, bf16[64,16,128]{2,1,0:T(8,128)(2,1)S(1)} %collective-permute-done.3.other), custom_call_target="tpu_custom_call" | custom-call | tf_op jit(solution)/shard_map/pallas_call | solution.py:658
Async XLA Ops:
  11.9 5.3 %collective-permute-start = (f32[24,384]{1,0:T(8,128)S(1)}, f32[24,384]{1,0:T(8,128)S(1)}, u32[]{:S(2)}, u32[]{:S(2)}) collective-permute-start(f32[24,384]{1,0:T(8,128)S(1)} %get-tuple-element.47), channel_id=1, source_target_pairs={{0,63},{1,32},{2,33},{3,34},{4,35},{5,36},{6,37},{7,38},{8,39},{9,... | collective-permute-start | bytes 110600 | tf_op jit(solution)/shard_map/ppermute | solution.py:567
  14.5 1.0 %copy-start = (bf16[2,9,64,64]{3,2,1,0:T(8,128)(2,1)S(1)}, bf16[2,9,64,64]{3,2,1,0:T(8,128)(2,1)}, u32[]{:S(2)}) copy-start(bf16[2,9,64,64]{3,2,1,0:T(8,128)(2,1)} %atm_conv.1) | copy-start | bytes 442372
  15.5 1.0 %copy-start.1 = (bf16[2,9,64,64]{3,2,1,0:T(8,128)(2,1)S(1)}, bf16[2,9,64,64]{3,2,1,0:T(8,128)(2,1)}, u32[]{:S(2)}) copy-start(bf16[2,9,64,64]{3,2,1,0:T(8,128)(2,1)} %ocn_conv.1) | copy-start | bytes 442372
  25.0 6.1 %collective-permute-start.1 = (f32[16,1152]{1,0:T(8,128)S(1)}, f32[16,1152]{1,0:T(8,128)S(1)}, u32[]{:S(2)}, u32[]{:S(2)}) collective-permute-start(f32[16,1152]{1,0:T(8,128)S(1)} %get-tuple-element.54.own), channel_id=1, source_target_pairs={{0,32},{1,33},{2,34},{3,35},{4,36},{5,37},{6,38},{7,39},{8,40},{9,... | collective-permute-start | bytes 221192 | tf_op jit(solution)/shard_map/ppermute | solution.py:609
  35.4 3.1 %collective-permute-start.2 = (f32[8,384]{1,0:T(8,128)S(1)}, f32[8,384]{1,0:T(8,128)S(1)}, u32[]{:S(2)}, u32[]{:S(2)}) collective-permute-start(f32[8,384]{1,0:T(8,128)S(1)} %get-tuple-element.66), channel_id=1, source_target_pairs={{0,63},{1,32},{2,33},{3,34},{4,35},{5,36},{6,37},{7,38},{8,39},{9,... | collective-permute-start | bytes 36872 | tf_op jit(solution)/shard_map/ppermute | solution.py:627
  83.2 2.6 %collective-permute-start.3 = (bf16[64,16,128]{2,1,0:T(8,128)(2,1)S(1)}, bf16[64,16,128]{2,1,0:T(8,128)(2,1)S(1)}, u32[]{:S(2)}, u32[]{:S(2)}) collective-permute-start(bf16[64,16,128]{2,1,0:T(8,128)(2,1)S(1)} %all_to_all.11.own), channel_id=1, source_target_pairs={{0,32},{32,0},{1,33},{33,1},{2,34},{34,2},{3,35},{35,3},{4,36},{36... | collective-permute-start | bytes 786440 | tf_op jit(solution)/shard_map/ppermute | solution.py:657

commit v6 on v5

--- a/solution.py
+++ b/solution.py
@@ -154,6 +154,9 @@
     for index in range(2):
         blocks = [atm_conv[index, k] for k in range(K)]
         flat[index] = jnp.concatenate(blocks, axis=1)
+        if index == 0:
+            folded = [dot(block, mixed.astype(BF)) for block in blocks]
+            flat[2] = jnp.concatenate(folded, axis=1).astype(BF)
         blocks = [turned(block) for block in blocks]
         for side, terms in enumerate(BACK):
             parts = [
@@ -167,7 +170,9 @@
             ocean_back[index, k * CH : (k + 1) * CH, :] = turned(blocks[k])
 
 
-def hot_kernel(gathered, hot, hot_back):
+def hot_kernel(gathered, hot, hot_back, hot_sea):
+    for cycle in range(3):
+        hot_sea[cycle] = one_hot_sea(sea_row(gathered, cycle))
     table = gathered[3, 16:32, :]
     columns = jnp.transpose(table).astype(jnp.int32)
     table = table.astype(jnp.int32)
@@ -270,7 +275,7 @@
 def forward_kernel(
     ids, features, strip, lift, flat, head,
     inputs_out, source_out, gate_one, gate_two, last_out, window_out, final_out,
-    window, total, columns, columns_two, flags, surface, lifted_total,
+    window, total, columns, columns_two, flags, surface, lifted_total, pre_total,
 ):
     half = ids[0] % 2
     first = ids[0] // 2 == 0
@@ -297,12 +302,17 @@
         inputs = jnp.concatenate([total[0:8, :], surface[...]], axis=0)
         inputs_out[at] = keep_owned(inputs).astype(BF)
         lifted = lifted_total[...]
-        build_columns(columns, [lifted[:, seg(row)] for row in range(ROWS)], flags)
-        pre = dot(flat[0], columns[...])
+        if at == 0:
+            build_columns(columns, split_rows(lifted), flags)
+            pre = dot(flat[0], columns[...])
+        else:
+            build_columns(columns, split_rows(hidden), flags)
+            pre = pre_total[...] + dot(flat[2], columns[...])
+        pre_total[...] = pre
         gate = sigmoid(pre)
         hidden = pre * gate
         gate_one[at] = (gate + hidden - hidden * gate).astype(BF)
-        source_out[at] = jnp.where(first, columns[0:CH, :], hidden.astype(BF))
+        source_out[at] = jnp.where(first, lifted.astype(BF), hidden.astype(BF))
         build_columns(columns_two, [hidden[:, seg(row)] for row in range(ROWS)], flags)
         pre = dot(flat[1], columns_two[...])
         gate = sigmoid(pre)
@@ -319,20 +329,21 @@
         final_out[:, seg(row)] = pltpu.roll(total[:, seg(row)], shift, 1)
 
 
+def join_halves(half, own, other):
+    lanes = lane_ids(own.shape)
+    return jnp.where(((lanes % LON) // (LON // 2)) == half, own, other)
+
+
 def ocean_kernel(
-    scale, ids, gathered, own, other, hot, hot_back,
-    lift, flat, head, lift_back, flat_back, head_back,
-    next_state, flux_grad, strip, columns, slopes, sixteen, wide,
+    scale, ids, gathered, own, other, hot, hot_back, hot_sea,
+    lift, flat, lift_back, flat_back, head_back,
+    flux_grad, strip, columns, slopes, sixteen, wide,
     scatter,
 ):
-    group = ids[0]
-    half = group % 2
-    lanes = lane_ids((16, WIN))
-    mine = ((lanes % LON) // (LON // 2)) == half
-    merged = jnp.where(mine, own[...], other[...])
-    flux = (merged[8:16, :] * (1.0 / STEPS)).astype(BF)
+    half = ids[0] % 2
+    flux = join_halves(half, own[8:16, :], other[8:16, :])
+    flux = (flux * (1.0 / STEPS)).astype(BF)
     flux = jnp.concatenate([flux, flux], axis=0)
-    hot_sea = [one_hot_sea(sea_row(gathered, cycle)) for cycle in range(3)]
     forcing = [
         dot(flux[:, cycle * CELLS : (cycle + 1) * CELLS], hot_sea[cycle])[0:8] for cycle in range(3)
     ]
@@ -362,10 +373,6 @@
     hidden = pre * gate
     slope_of_two = gate + hidden - hidden * gate
     hidden = hidden.astype(BF)
-    ocean_next = fields + dot(head[...], hidden)[0:8]
-    block = jnp.where(group == 0, merged[0:8, 0:CELLS], ocean_next)
-    block = jnp.where(group == 1, merged[0:8, CELLS : 2 * CELLS], block)
-    next_state[...] = jnp.where(group == 2, merged[0:8, 2 * CELLS : 3 * CELLS], block)
 
     head_grad = gathered[3, 8:16, :] * scale
     head_grad = jnp.concatenate([head_grad, jnp.zeros((8, CELLS), F32)], axis=0).astype(BF)
@@ -389,9 +396,18 @@
     wide[1] = hidden
 
 
-def ocean_weight_kernel(ids, columns, slopes, sixteen, wide, wire):
-    half = ids[0] % 2
-    chosen = ids[0] // 2
+def ocean_weight_kernel(
+    ids, gathered, own, other, head, columns, slopes, sixteen, wide, next_state, wire
+):
+    group = ids[0]
+    half = group % 2
+    chosen = group // 2
+    block = gathered[3, 0:8, :] + dot(head[...], wide[1])[0:8]
+    for cycle in range(3):
+        cols = slice(cycle * CELLS, (cycle + 1) * CELLS)
+        merged = join_halves(half, own[0:8, cols], other[0:8, cols])
+        block = jnp.where(group == cycle, merged, block)
+    next_state[...] = block
     weight = jnp.transpose(dot(columns[chosen], slopes[chosen], NT))
     weight = jnp.where(half == 0, weight[0:32], weight[32:64])
     for j in range(4):
@@ -445,9 +461,10 @@
         ]
         build_back(taps, 0, slope_one, flags)
         grad_lifted = jnp.concatenate(join_sides(dot(back[0], taps[0])), axis=1).astype(BF)
-        change = dot(lift_back[...], grad_lifted)
-        grad_total[...] += change[16:]
-        head_grad[0:8, :] += change[0:8]
+        if at > 0:
+            change = dot(lift_back[...], grad_lifted)
+            grad_total[...] += change[16:]
+            head_grad[0:8, :] += change[0:8]
         lift_weight = dot(inputs[at], grad_lifted, NT)
         head_weight = dot(keep_owned(grad), last[at], NT)
         small_total[...] += jnp.concatenate([lift_weight, head_weight], axis=1)
@@ -573,7 +590,7 @@
             ((16 + CH, CH), BF),
             ((16 + CH, CH), BF),
             ((CH, 16), BF),
-            ((2, CH, K * CH), BF),
+            ((3, CH, K * CH), BF),
             ((2, 3 * CH, 7 * CH), BF),
             ((CH, 16), BF),
             ((16, CH), BF),
@@ -586,8 +603,8 @@
     lift, lift_back, head, head_back, flat, back = weights[:6]
     ocean_lift, ocean_lift_back, ocean_head, ocean_head_back, ocean_flat, ocean_back = weights[6:]
 
-    hot, hot_back = call(hot_kernel, [((K, CELLS, CELLS), BF), ((K * CELLS, CELLS), BF)])(gathered)
-    strip, hot, hot_back = lax.optimization_barrier((strip, hot, hot_back))
+    hot, hot_back, hot_sea = call(hot_kernel, [((K, CELLS, CELLS), BF), ((K * CELLS, CELLS), BF), ((3, CELLS, LON), BF)])(gathered)
+    strip, hot, hot_back, hot_sea = lax.optimization_barrier((strip, hot, hot_back, hot_sea))
 
     wide = (CH, WIN)
     history = [(16, WIN), wide, wide, wide, wide]
@@ -602,15 +619,15 @@
             pltpu.VMEM((4, 16, WIN), BF),
             pltpu.VMEM((8, WIN), F32),
             pltpu.VMEM((CH, WIN), F32),
+            pltpu.VMEM((CH, WIN), F32),
         ],
         in_specs=[smem()] + [vmem()] * 5,
     )(ids, features, strip, lift, flat, head)
 
     other_final = lax.ppermute(final, BOTH, partner)
-    next_state, flux_grad, flux_strip, *ocean_parts = call(
+    flux_grad, flux_strip, *ocean_parts = call(
         functools.partial(ocean_kernel, scale),
         [
-            ((8, CELLS), F32),
             ((8, WIN), F32),
             ((8, CELLS), F32),
             ((2, K * CH, CELLS), BF),
@@ -621,13 +638,15 @@
         scratch=[pltpu.VMEM((CH, K * CELLS), BF)],
         in_specs=[smem()] + [vmem()] * 11,
     )(
-        ids, gathered, final, other_final, hot, hot_back, ocean_lift, ocean_flat, ocean_head,
+        ids, gathered, final, other_final, hot, hot_back, hot_sea, ocean_lift, ocean_flat,
         ocean_lift_back, ocean_back, ocean_head_back,
     )
     flux_strip = lax.ppermute(flux_strip, BOTH, beside)
-    (ocean_wire,) = call(
-        ocean_weight_kernel, [((160, LON), BF)], in_specs=[smem()] + [vmem()] * 4
-    )(ids, *ocean_parts)
+    next_state, ocean_wire = call(
+        ocean_weight_kernel,
+        [((8, CELLS), F32), ((160, LON), BF)],
+        in_specs=[smem()] + [vmem()] * 8,
+    )(ids, gathered, final, other_final, ocean_head, *ocean_parts)
 
     (wire,) = call(
         functools.partial(backward_kernel, scale),

time: 87.3 us -> 86.2 us (0.987)
  transfers between devices with their start and end apart: 4 -> 4, of which waited for: 3 -> 3; matrix products, arithmetic and copies ran while one was open for 0% -> 0% of each run, Pallas kernels for 3% -> 4%
where the time goes in v6:
time: 86.2 us; the launch traced here: 85.9 us
  blocking collectives  42 us (49%)
  Pallas kernels  28.8 us (33%)
  starting transfers between devices  7.98 us (9%)
  waiting for transfers between devices  4.44 us (5%)
  local copies, waits for them, and re-layouts  1.92 us (2%)
    all_to_all x1, blocking collectives, shards(): sums = lax.all_to_all(sums, ('high', 'tile'), 0, 0, tiled=True)  16.3 us
    all_to_all x1, blocking collectives, shards(): lax.all_to_all(wire.reshape(sectors, rows, LON), 'tile', 0, 0, tiled=True)  16.3 us
    pallas_call x1, Pallas kernels, shards(): call(functools.partial(backward_kernel, scale), [((WIRE, LON), BF)], scra...  11.5 us
    all_gather x1, blocking collectives, shards(): gathered = lax.all_gather(packed, GROUP)  9.33 us
    pallas_call x1, Pallas kernels, shards(): call(forward_kernel, [((STEPS,) + shape, BF) for shape in history] + [((1...  7.45 us
    ppermute x1, starting transfers between devices, shards(): other_final = lax.ppermute(final, BOTH, partner)  5.23 us
    pallas_call x1, Pallas kernels, shards(): call(functools.partial(ocean_kernel, scale), [((8, WIN), F32), ((8, CELLS...  3.59 us
    ppermute x1, waiting for transfers between devices, shards(): flux_strip = lax.ppermute(flux_strip, BOTH, beside)  2.36 us
  transfers between devices with their start and end apart: 4, of which 3 were waited for; matrix products, arithmetic and copies ran while one was open for 0% of the time, Pallas kernels for 4%

profile of v6, /device:TPU:1, one launch (start us, length us, event | category | flops | bytes accessed | tf_op | source)
XLA Modules:
  0.0 85.9 jit_solution(4091630516394081510)
XLA Ops:
  0.6 1.6 %shard_map.153 = f32[32,384]{1,0:T(8,128)} custom-call(s32[1]{0:T(128)} %bitcast.ids, f32[8,384]{1,0:T(8,128)} %bitcast.18, f32[8,384]{1,0:T(8,128)} %bitcast.19, s32[9,1,384]{2,1,0:T(1,128)} %bitcast.17, s32[3,1,128]{2,1,0:T(1,128)} %sea.1, bf16[10,64]{1,0:T(8,128)(2,1)} %bitcast.20, bf16[12,64]{1,0:T(8,128)(2,1)} %atm_head.1, bf16[12,64]{1,0:T(8,128)(2,1)} %bitcast.21, ...), custom_call_target="tpu_custom_call" | custom-call | tf_op jit(solution)/shard_map/pallas_call | solution.py:566
  2.2 9.3 %all-gather = f32[128,384]{1,0:T(8,128)S(1)} all-gather(f32[32,384]{1,0:T(8,128)} %shard_map.153), channel_id=2, replica_groups=mesh['high'=2,'core'=2,'tile'=32] {'high','core'}, dimensions={0}, use_global_device_ids=true | all-gather | bytes 245760 | tf_op jit(solution)/shard_map/all_gather | solution.py:578
  11.5 0.3 shard_map.154
  11.9 1.1 %collective-permute-start = (f32[24,384]{1,0:T(8,128)S(1)}, f32[24,384]{1,0:T(8,128)S(1)}, u32[]{:S(2)}, u32[]{:S(2)}) collective-permute-start(f32[24,384]{1,0:T(8,128)S(1)} %get-tuple-element.50), channel_id=1, source_target_pairs={{0,63},{1,32},{2,33},{3,34},{4,35},{5,36},{6,37},{7,38},{8,39},{9,... | collective-permute-start | bytes 110600 | tf_op jit(solution)/shard_map/ppermute | solution.py:584
  12.9 1.7 %shard_map.155 = (bf16[9,384,384]{2,1,0:T(8,128)(2,1)S(1)}, bf16[3456,384]{1,0:T(8,128)(2,1)S(1)}, bf16[3,384,128]{2,1,0:T(8,128)(2,1)S(1)}) custom-call(f32[4,32,384]{2,1,0:T(8,128)S(1)} %bitcast.12), custom_call_target="tpu_custom_call" | custom-call | tf_op jit(solution)/shard_map/pallas_call | solution.py:606
  14.6 0.0 copy-start
  14.6 1.0 %copy-done = bf16[2,9,64,64]{3,2,1,0:T(8,128)(2,1)S(1)} copy-done((bf16[2,9,64,64]{3,2,1,0:T(8,128)(2,1)S(1)}, bf16[2,9,64,64]{3,2,1,0:T(8,128)(2,1)}, u32[]{:S(2)}) %copy-start) | copy-done | bytes 147480
  15.6 0.0 copy-start.1
  15.6 1.0 %copy-done.1 = bf16[2,9,64,64]{3,2,1,0:T(8,128)(2,1)S(1)} copy-done((bf16[2,9,64,64]{3,2,1,0:T(8,128)(2,1)S(1)}, bf16[2,9,64,64]{3,2,1,0:T(8,128)(2,1)}, u32[]{:S(2)}) %copy-start.1) | copy-done | bytes 147480
  16.6 0.7 shard_map.156
  17.3 0.0 collective-permute-done.strip
  17.3 7.4 %shard_map.157 = (bf16[8,16,1152]{2,1,0:T(8,128)(2,1)S(1)}, bf16[8,64,1152]{2,1,0:T(8,128)(2,1)S(1)}, bf16[8,64,1152]{2,1,0:T(8,128)(2,1)S(1)}, bf16[8,64,1152]{...) custom-call(s32[1]{0:T(128)} %bitcast.ids, ...), custom_call_target="tpu_custom_call" | custom-call | tf_op jit(solution)/shard_map/pallas_call | solution.py:611
  24.7 5.2 %collective-permute-start.1 = (f32[16,1152]{1,0:T(8,128)S(1)}, f32[16,1152]{1,0:T(8,128)S(1)}, u32[]{:S(2)}, u32[]{:S(2)}) collective-permute-start(f32[16,1152]{1,0:T(8,128)S(1)} %get-tuple-element.58.own), channel_id=1, source_target_pairs={{0,32},{1,33},{2,34},{3,35},{4,36},{5,37},{6,38},{7,39},{8,40},{9,... | collective-permute-start | bytes 221192 | tf_op jit(solution)/shard_map/ppermute | solution.py:627
  29.9 0.9 %collective-permute-done.1.other = f32[16,1152]{1,0:T(8,128)S(1)} collective-permute-done((f32[16,1152]{1,0:T(8,128)S(1)}, f32[16,1152]{1,0:T(8,128)S(1)}, u32[]{:S(2)}, u32[]{:S(2)}) %collective-permute-start.1) | collective-permute-done | bytes 73760 | tf_op jit(solution)/shard_map/ppermute | solution.py:627
  30.9 3.6 %shard_map.158 = (f32[8,1152]{1,0:T(8,128)S(1)}, f32[8,384]{1,0:T(8,128)S(1)}, bf16[2,576,384]{2,1,0:T(8,128)(2,1)S(1)}, bf16[2,64,384]{2,1,0:T(8,128)(2,1)S(1)}...) custom-call(s32[1]{0:T(128)} %bitcast.ids, f32[4,32,384]{2,1,0:T(8,128)S(1)} %bitcast.14, ...), custom_call_target="tpu_custom_call" | custom-call | tf_op jit(solution)/shard_map/pallas_call | solution.py:628
  34.4 0.0 collective-permute-start.2
  34.5 0.7 shard_map.159
  35.2 2.4 %collective-permute-done.2.flux_strip = f32[8,384]{1,0:T(8,128)S(1)} collective-permute-done((f32[8,384]{1,0:T(8,128)S(1)}, f32[8,384]{1,0:T(8,128)S(1)}, u32[]{:S(2)}, u32[]{:S(2)}) %collective-permute-start.2) | collective-permute-done | bytes 12320 | tf_op jit(solution)/shard_map/ppermute | solution.py:644
  37.6 11.5 %shard_map.160 = bf16[512,128]{1,0:T(8,128)(2,1)S(1)} custom-call(s32[1]{0:T(128)} %bitcast.ids, f32[16,1152]{1,0:T(8,128)S(1)} %get-tuple-element.73.window, f32[8,1152]{1,0:T(8,128)S(1)} %get-tuple-element.74.flux_own, f32[8,384]{1,0:T(8,128)S(1)} %collective-permute-done.2.flux_strip, bf16[160,128]{1,0:T(8,128)(2,1)S(1)} %get-tuple-element.76.ocean_wire, ...), custom_call_target="tpu_custom_call" | custom-call | tf_op jit(solution)/shard_map/pallas_call | solution.py:651
  49.1 16.3 %all_to_all.10.parts = bf16[32,16,128]{2,1,0:T(8,128)(2,1)S(1)} all-to-all(bf16[32,16,128]{2,1,0:T(8,128)(2,1)S(1)} %bitcast.16), channel_id=1, replica_groups=mesh['high'=2,'core'=2,'tile'=32] {'tile'}, dimensions={0} | all-to-all | bytes 262144 | tf_op jit(solution)/shard_map/all_to_all | solution.py:671
  65.5 0.1 shard_map.161
  65.5 16.3 %all_to_all.11.own = bf16[64,16,128]{2,1,0:T(8,128)(2,1)S(1)} all-to-all(bf16[64,16,128]{2,1,0:T(8,128)(2,1)S(1)} %shard_map.161), channel_id=1, replica_groups=mesh['high'=2,'core'=2,'tile'=32] {'high','tile'}, dimensions={0} | all-to-all | bytes 524288 | tf_op jit(solution)/shard_map/all_to_all | solution.py:675
  81.9 1.6 %collective-permute-start.3 = (bf16[64,16,128]{2,1,0:T(8,128)(2,1)S(1)}, bf16[64,16,128]{2,1,0:T(8,128)(2,1)S(1)}, u32[]{:S(2)}, u32[]{:S(2)}) collective-permute-start(bf16[64,16,128]{2,1,0:T(8,128)(2,1)S(1)} %all_to_all.11.own), channel_id=1, source_target_pairs={{0,32},{32,0},{1,33},{33,1},{2,34},{34,2},{3,35},{35,3},{4,36},{36... | collective-permute-start | bytes 786440 | tf_op jit(solution)/shard_map/ppermute | solution.py:676
  83.5 1.2 %collective-permute-done.3.other = bf16[64,16,128]{2,1,0:T(8,128)(2,1)S(1)} collective-permute-done((bf16[64,16,128]{2,1,0:T(8,128)(2,1)S(1)}, bf16[64,16,128]{2,1,0:T(8,128)(2,1)S(1)}, u32[]{:S(2)}, u32[]{:S(2)}) %collective-permute-start.3) | collective-permute-done | bytes 262176 | tf_op jit(solution)/shard_map/ppermute | solution.py:676
  84.7 1.2 %shard_map.162 = (f32[10,64]{1,0:T(8,128)}, f32[2,9,64,64]{3,2,1,0:T(8,128)}, f32[12,64]{1,0:T(8,128)}, f32[12,64]{1,0:T(8,128)}, f32[2,9,64,64]{3,2,1,0:T(8,128)}, /*index=5*/f32[8,64]{1,0:T(8,128)}) custom-call(s32[1]{0:T(128)} %bitcast.ids, bf16[64,16,128]{2,1,0:T(8,128)(2,1)S(1)} %all_to_all.11.own, bf16[64,16,128]{2,1,0:T(8,128)(2,1)S(1)} %collective-permute-done.3.other), custom_call_target="tpu_custom_call" | custom-call | tf_op jit(solution)/shard_map/pallas_call | solution.py:677
Async XLA Ops:
  11.9 5.4 %collective-permute-start = (f32[24,384]{1,0:T(8,128)S(1)}, f32[24,384]{1,0:T(8,128)S(1)}, u32[]{:S(2)}, u32[]{:S(2)}) collective-permute-start(f32[24,384]{1,0:T(8,128)S(1)} %get-tuple-element.50), channel_id=1, source_target_pairs={{0,63},{1,32},{2,33},{3,34},{4,35},{5,36},{6,37},{7,38},{8,39},{9,... | collective-permute-start | bytes 110600 | tf_op jit(solution)/shard_map/ppermute | solution.py:584
  14.6 1.0 %copy-start = (bf16[2,9,64,64]{3,2,1,0:T(8,128)(2,1)S(1)}, bf16[2,9,64,64]{3,2,1,0:T(8,128)(2,1)}, u32[]{:S(2)}) copy-start(bf16[2,9,64,64]{3,2,1,0:T(8,128)(2,1)} %atm_conv.1) | copy-start | bytes 442372
  15.6 1.0 %copy-start.1 = (bf16[2,9,64,64]{3,2,1,0:T(8,128)(2,1)S(1)}, bf16[2,9,64,64]{3,2,1,0:T(8,128)(2,1)}, u32[]{:S(2)}) copy-start(bf16[2,9,64,64]{3,2,1,0:T(8,128)(2,1)} %ocn_conv.1) | copy-start | bytes 442372
  24.7 6.1 %collective-permute-start.1 = (f32[16,1152]{1,0:T(8,128)S(1)}, f32[16,1152]{1,0:T(8,128)S(1)}, u32[]{:S(2)}, u32[]{:S(2)}) collective-permute-start(f32[16,1152]{1,0:T(8,128)S(1)} %get-tuple-element.58.own), channel_id=1, source_target_pairs={{0,32},{1,33},{2,34},{3,35},{4,36},{5,37},{6,38},{7,39},{8,40},{9,... | collective-permute-start | bytes 221192 | tf_op jit(solution)/shard_map/ppermute | solution.py:627
  34.4 3.1 %collective-permute-start.2 = (f32[8,384]{1,0:T(8,128)S(1)}, f32[8,384]{1,0:T(8,128)S(1)}, u32[]{:S(2)}, u32[]{:S(2)}) collective-permute-start(f32[8,384]{1,0:T(8,128)S(1)} %get-tuple-element.75), channel_id=1, source_target_pairs={{0,63},{1,32},{2,33},{3,34},{4,35},{5,36},{6,37},{7,38},{8,39},{9,... | collective-permute-start | bytes 36872 | tf_op jit(solution)/shard_map/ppermute | solution.py:644
  81.9 2.8 %collective-permute-start.3 = (bf16[64,16,128]{2,1,0:T(8,128)(2,1)S(1)}, bf16[64,16,128]{2,1,0:T(8,128)(2,1)S(1)}, u32[]{:S(2)}, u32[]{:S(2)}) collective-permute-start(bf16[64,16,128]{2,1,0:T(8,128)(2,1)S(1)} %all_to_all.11.own), channel_id=1, source_target_pairs={{0,32},{32,0},{1,33},{33,1},{2,34},{34,2},{3,35},{35,3},{4,36},{36... | collective-permute-start | bytes 786440 | tf_op jit(solution)/shard_map/ppermute | solution.py:676

commit v7 on v6

--- a/solution.py
+++ b/solution.py
@@ -396,6 +396,15 @@
     wide[1] = hidden
 
 
+def source_kernel(source, sources):
+    for at in range(STEPS):
+        for row in range(ROWS):
+            mid = source[at, :, seg(row)]
+            sides = (pltpu.roll(mid, 1, 1), mid, pltpu.roll(mid, LON - 1, 1))
+            for place, value in enumerate(sides):
+                sources[at, place * CH : (place + 1) * CH, seg(row)] = keep_owned(value)
+
+
 def ocean_weight_kernel(
     ids, gathered, own, other, head, columns, slopes, sixteen, wide, next_state, wire
 ):
@@ -422,11 +431,10 @@
     scale, ids, window, flux_own, flux_strip, ocean_wire, back, head_back, lift_back,
     inputs, source, gate_one, gate_two, last,
     wire,
-    head_grad, flags, weight_total, small_total, taps_even, taps_odd, sources_even, sources_odd, grad_total,
+    head_grad, flags, weight_total, small_total, taps_even, taps_odd, grad_total,
 ):
     half = ids[0] % 2
     all_taps = (taps_even, taps_odd)
-    all_sources = (sources_even, sources_odd)
     chosen = 1 - jnp.where(ids[0] // 2 == 0, 1, 0)
 
     head_grad[0:8, :] = window[0:8, :] * scale
@@ -447,11 +455,6 @@
 
     for at in reversed(range(STEPS)):
         taps = all_taps[at % 2]
-        sources = all_sources[at % 2]
-        for row in range(ROWS):
-            mid = source[at, :, seg(row)]
-            for place, value in enumerate((pltpu.roll(mid, 1, 1), mid, pltpu.roll(mid, LON - 1, 1))):
-                sources[place * CH : (place + 1) * CH, seg(row)] = keep_owned(value)
         grad = head_grad[...].astype(BF)
         slope_two = grad_total[...] * gate_two[at].astype(F32)
         build_back(taps, 1, split_rows(slope_two), flags)
@@ -468,7 +471,7 @@
         lift_weight = dot(inputs[at], grad_lifted, NT)
         head_weight = dot(keep_owned(grad), last[at], NT)
         small_total[...] += jnp.concatenate([lift_weight, head_weight], axis=1)
-        weight_total[...] += dot(taps[chosen], sources[...], NT)
+        weight_total[...] += dot(taps[chosen], source[at], NT)
 
     def product(slope, side):
         rows = weight_total[slope * CH : (slope + 1) * CH, :]
@@ -642,6 +645,7 @@
         ocean_lift_back, ocean_back, ocean_head_back,
     )
     flux_strip = lax.ppermute(flux_strip, BOTH, beside)
+    (sources,) = call(source_kernel, [((STEPS, 3 * CH, WIN), BF)])(source)
     next_state, ocean_wire = call(
         ocean_weight_kernel,
         [((8, CELLS), F32), ((160, LON), BF)],
@@ -658,14 +662,12 @@
             pltpu.VMEM((16, LON), F32),
             pltpu.VMEM((2, 7 * CH, WIN), BF),
             pltpu.VMEM((2, 7 * CH, WIN), BF),
-            pltpu.VMEM((3 * CH, WIN), BF),
-            pltpu.VMEM((3 * CH, WIN), BF),
             pltpu.VMEM((CH, WIN), F32),
         ],
         in_specs=[smem()] + [vmem()] * 12,
     )(
         ids, window, flux_grad, flux_strip, ocean_wire, back, head_back, lift_back,
-        inputs, source, gate_one, gate_two, last,
+        inputs, sources, gate_one, gate_two, last,
     )
 
     parts = lax.all_to_all(wire.reshape(sectors, rows, LON), "tile", 0, 0, tiled=True)

time: 86.2 us -> 86 us (level)
  no operation moved by 1% of the time
where the time goes in v7:
time: 86 us; the launch traced here: 85.7 us
  blocking collectives  42 us (49%)
  Pallas kernels  29.4 us (34%)
  starting transfers between devices  7.97 us (9%)
  waiting for transfers between devices  3.75 us (4%)
  local copies, waits for them, and re-layouts  1.92 us (2%)
    all_to_all x1, blocking collectives, shards(): sums = lax.all_to_all(sums, ('high', 'tile'), 0, 0, tiled=True)  16.3 us
    all_to_all x1, blocking collectives, shards(): lax.all_to_all(wire.reshape(sectors, rows, LON), 'tile', 0, 0, tiled=True)  16.3 us
    pallas_call x1, Pallas kernels, shards(): call(functools.partial(backward_kernel, scale), [((WIRE, LON), BF)], scra...  11.4 us
    all_gather x1, blocking collectives, shards(): gathered = lax.all_gather(packed, GROUP)  9.33 us
    pallas_call x1, Pallas kernels, shards(): call(forward_kernel, [((STEPS,) + shape, BF) for shape in history] + [((1...  7.43 us
    ppermute x1, starting transfers between devices, shards(): other_final = lax.ppermute(final, BOTH, partner)  5.23 us
    pallas_call x1, Pallas kernels, shards(): call(functools.partial(ocean_kernel, scale), [((8, WIN), F32), ((8, CELLS...  3.59 us
    unnamed x4, local copies, waits for them, and re-layouts  1.92 us
  transfers between devices with their start and end apart: 4, of which 3 were waited for; matrix products, arithmetic and copies ran while one was open for 0% of the time, Pallas kernels for 4%

profile of v7, /device:TPU:1, one launch (start us, length us, event | category | flops | bytes accessed | tf_op | source)
XLA Modules:
  0.0 85.7 jit_solution(10479678135664306418)
XLA Ops:
  0.6 1.6 %shard_map.153 = f32[32,384]{1,0:T(8,128)} custom-call(s32[1]{0:T(128)} %bitcast.ids, f32[8,384]{1,0:T(8,128)} %bitcast.18, f32[8,384]{1,0:T(8,128)} %bitcast.19, s32[9,1,384]{2,1,0:T(1,128)} %bitcast.17, s32[3,1,128]{2,1,0:T(1,128)} %sea.1, bf16[10,64]{1,0:T(8,128)(2,1)} %bitcast.20, bf16[12,64]{1,0:T(8,128)(2,1)} %atm_head.1, bf16[12,64]{1,0:T(8,128)(2,1)} %bitcast.21, ...), custom_call_target="tpu_custom_call" | custom-call | tf_op jit(solution)/shard_map/pallas_call | solution.py:569
  2.2 9.3 %all-gather = f32[128,384]{1,0:T(8,128)S(1)} all-gather(f32[32,384]{1,0:T(8,128)} %shard_map.153), channel_id=2, replica_groups=mesh['high'=2,'core'=2,'tile'=32] {'high','core'}, dimensions={0}, use_global_device_ids=true | all-gather | bytes 245760 | tf_op jit(solution)/shard_map/all_gather | solution.py:581
  11.5 0.3 shard_map.154
  11.9 1.1 %collective-permute-start = (f32[24,384]{1,0:T(8,128)S(1)}, f32[24,384]{1,0:T(8,128)S(1)}, u32[]{:S(2)}, u32[]{:S(2)}) collective-permute-start(f32[24,384]{1,0:T(8,128)S(1)} %get-tuple-element.50), channel_id=1, source_target_pairs={{0,63},{1,32},{2,33},{3,34},{4,35},{5,36},{6,37},{7,38},{8,39},{9,... | collective-permute-start | bytes 110600 | tf_op jit(solution)/shard_map/ppermute | solution.py:587
  12.9 1.7 %shard_map.155 = (bf16[9,384,384]{2,1,0:T(8,128)(2,1)S(1)}, bf16[3456,384]{1,0:T(8,128)(2,1)S(1)}, bf16[3,384,128]{2,1,0:T(8,128)(2,1)S(1)}) custom-call(f32[4,32,384]{2,1,0:T(8,128)S(1)} %bitcast.12), custom_call_target="tpu_custom_call" | custom-call | tf_op jit(solution)/shard_map/pallas_call | solution.py:609
  14.6 0.0 copy-start
  14.6 1.0 %copy-done = bf16[2,9,64,64]{3,2,1,0:T(8,128)(2,1)S(1)} copy-done((bf16[2,9,64,64]{3,2,1,0:T(8,128)(2,1)S(1)}, bf16[2,9,64,64]{3,2,1,0:T(8,128)(2,1)}, u32[]{:S(2)}) %copy-start) | copy-done | bytes 147480
  15.6 0.0 copy-start.1
  15.6 1.0 %copy-done.1 = bf16[2,9,64,64]{3,2,1,0:T(8,128)(2,1)S(1)} copy-done((bf16[2,9,64,64]{3,2,1,0:T(8,128)(2,1)S(1)}, bf16[2,9,64,64]{3,2,1,0:T(8,128)(2,1)}, u32[]{:S(2)}) %copy-start.1) | copy-done | bytes 147480
  16.6 0.7 shard_map.156
  17.3 0.0 collective-permute-done.strip
  17.3 7.4 %shard_map.157 = (bf16[8,16,1152]{2,1,0:T(8,128)(2,1)S(1)}, bf16[8,64,1152]{2,1,0:T(8,128)(2,1)S(1)}, bf16[8,64,1152]{2,1,0:T(8,128)(2,1)S(1)}, bf16[8,64,1152]{...) custom-call(s32[1]{0:T(128)} %bitcast.ids, ...), custom_call_target="tpu_custom_call" | custom-call | tf_op jit(solution)/shard_map/pallas_call | solution.py:614
  24.7 5.2 %collective-permute-start.1 = (f32[16,1152]{1,0:T(8,128)S(1)}, f32[16,1152]{1,0:T(8,128)S(1)}, u32[]{:S(2)}, u32[]{:S(2)}) collective-permute-start(f32[16,1152]{1,0:T(8,128)S(1)} %get-tuple-element.58.own), channel_id=1, source_target_pairs={{0,32},{1,33},{2,34},{3,35},{4,36},{5,37},{6,38},{7,39},{8,40},{9,... | collective-permute-start | bytes 221192 | tf_op jit(solution)/shard_map/ppermute | solution.py:630
  29.9 0.9 %collective-permute-done.1.other = f32[16,1152]{1,0:T(8,128)S(1)} collective-permute-done((f32[16,1152]{1,0:T(8,128)S(1)}, f32[16,1152]{1,0:T(8,128)S(1)}, u32[]{:S(2)}, u32[]{:S(2)}) %collective-permute-start.1) | collective-permute-done | bytes 73760 | tf_op jit(solution)/shard_map/ppermute | solution.py:630
  30.8 3.6 %shard_map.158 = (f32[8,1152]{1,0:T(8,128)S(1)}, f32[8,384]{1,0:T(8,128)S(1)}, bf16[2,576,384]{2,1,0:T(8,128)(2,1)S(1)}, bf16[2,64,384]{2,1,0:T(8,128)(2,1)S(1)}...) custom-call(s32[1]{0:T(128)} %bitcast.ids, f32[4,32,384]{2,1,0:T(8,128)S(1)} %bitcast.14, ...), custom_call_target="tpu_custom_call" | custom-call | tf_op jit(solution)/shard_map/pallas_call | solution.py:631
  34.4 0.0 collective-permute-start.2
  34.5 0.7 shard_map.160.source
  35.2 0.7 shard_map.159
  35.9 1.7 %collective-permute-done.2.flux_strip = f32[8,384]{1,0:T(8,128)S(1)} collective-permute-done((f32[8,384]{1,0:T(8,128)S(1)}, f32[8,384]{1,0:T(8,128)S(1)}, u32[]{:S(2)}, u32[]{:S(2)}) %collective-permute-start.2) | collective-permute-done | bytes 12320 | tf_op jit(solution)/shard_map/ppermute | solution.py:647
  37.6 11.4 %shard_map.161 = bf16[512,128]{1,0:T(8,128)(2,1)S(1)} custom-call(s32[1]{0:T(128)} %bitcast.ids, f32[16,1152]{1,0:T(8,128)S(1)} %get-tuple-element.73.window, f32[8,1152]{1,0:T(8,128)S(1)} %get-tuple-element.74.flux_own, f32[8,384]{1,0:T(8,128)S(1)} %collective-permute-done.2.flux_strip, bf16[160,128]{1,0:T(8,128)(2,1)S(1)} %get-tuple-element.76.ocean_wire, ...), custom_call_target="tpu_custom_call" | custom-call | tf_op jit(solution)/shard_map/pallas_call | solution.py:655
  49.0 16.3 %all_to_all.10.parts = bf16[32,16,128]{2,1,0:T(8,128)(2,1)S(1)} all-to-all(bf16[32,16,128]{2,1,0:T(8,128)(2,1)S(1)} %bitcast.16), channel_id=1, replica_groups=mesh['high'=2,'core'=2,'tile'=32] {'tile'}, dimensions={0} | all-to-all | bytes 262144 | tf_op jit(solution)/shard_map/all_to_all | solution.py:673
  65.3 0.1 shard_map.162
  65.4 16.3 %all_to_all.11.own = bf16[64,16,128]{2,1,0:T(8,128)(2,1)S(1)} all-to-all(bf16[64,16,128]{2,1,0:T(8,128)(2,1)S(1)} %shard_map.162), channel_id=1, replica_groups=mesh['high'=2,'core'=2,'tile'=32] {'high','tile'}, dimensions={0} | all-to-all | bytes 524288 | tf_op jit(solution)/shard_map/all_to_all | solution.py:677
  81.7 1.6 %collective-permute-start.3 = (bf16[64,16,128]{2,1,0:T(8,128)(2,1)S(1)}, bf16[64,16,128]{2,1,0:T(8,128)(2,1)S(1)}, u32[]{:S(2)}, u32[]{:S(2)}) collective-permute-start(bf16[64,16,128]{2,1,0:T(8,128)(2,1)S(1)} %all_to_all.11.own), channel_id=1, source_target_pairs={{0,32},{32,0},{1,33},{33,1},{2,34},{34,2},{3,35},{35,3},{4,36},{36... | collective-permute-start | bytes 786440 | tf_op jit(solution)/shard_map/ppermute | solution.py:678
  83.3 1.2 %collective-permute-done.3.other = bf16[64,16,128]{2,1,0:T(8,128)(2,1)S(1)} collective-permute-done((bf16[64,16,128]{2,1,0:T(8,128)(2,1)S(1)}, bf16[64,16,128]{2,1,0:T(8,128)(2,1)S(1)}, u32[]{:S(2)}, u32[]{:S(2)}) %collective-permute-start.3) | collective-permute-done | bytes 262176 | tf_op jit(solution)/shard_map/ppermute | solution.py:678
  84.5 1.2 %shard_map.163 = (f32[10,64]{1,0:T(8,128)}, f32[2,9,64,64]{3,2,1,0:T(8,128)}, f32[12,64]{1,0:T(8,128)}, f32[12,64]{1,0:T(8,128)}, f32[2,9,64,64]{3,2,1,0:T(8,128)}, /*index=5*/f32[8,64]{1,0:T(8,128)}) custom-call(s32[1]{0:T(128)} %bitcast.ids, bf16[64,16,128]{2,1,0:T(8,128)(2,1)S(1)} %all_to_all.11.own, bf16[64,16,128]{2,1,0:T(8,128)(2,1)S(1)} %collective-permute-done.3.other), custom_call_target="tpu_custom_call" | custom-call | tf_op jit(solution)/shard_map/pallas_call | solution.py:679
Async XLA Ops:
  11.9 5.4 %collective-permute-start = (f32[24,384]{1,0:T(8,128)S(1)}, f32[24,384]{1,0:T(8,128)S(1)}, u32[]{:S(2)}, u32[]{:S(2)}) collective-permute-start(f32[24,384]{1,0:T(8,128)S(1)} %get-tuple-element.50), channel_id=1, source_target_pairs={{0,63},{1,32},{2,33},{3,34},{4,35},{5,36},{6,37},{7,38},{8,39},{9,... | collective-permute-start | bytes 110600 | tf_op jit(solution)/shard_map/ppermute | solution.py:587
  14.6 1.0 %copy-start = (bf16[2,9,64,64]{3,2,1,0:T(8,128)(2,1)S(1)}, bf16[2,9,64,64]{3,2,1,0:T(8,128)(2,1)}, u32[]{:S(2)}) copy-start(bf16[2,9,64,64]{3,2,1,0:T(8,128)(2,1)} %atm_conv.1) | copy-start | bytes 442372
  15.6 1.0 %copy-start.1 = (bf16[2,9,64,64]{3,2,1,0:T(8,128)(2,1)S(1)}, bf16[2,9,64,64]{3,2,1,0:T(8,128)(2,1)}, u32[]{:S(2)}) copy-start(bf16[2,9,64,64]{3,2,1,0:T(8,128)(2,1)} %ocn_conv.1) | copy-start | bytes 442372
  24.7 6.1 %collective-permute-start.1 = (f32[16,1152]{1,0:T(8,128)S(1)}, f32[16,1152]{1,0:T(8,128)S(1)}, u32[]{:S(2)}, u32[]{:S(2)}) collective-permute-start(f32[16,1152]{1,0:T(8,128)S(1)} %get-tuple-element.58.own), channel_id=1, source_target_pairs={{0,32},{1,33},{2,34},{3,35},{4,36},{5,37},{6,38},{7,39},{8,40},{9,... | collective-permute-start | bytes 221192 | tf_op jit(solution)/shard_map/ppermute | solution.py:630
  34.4 3.1 %collective-permute-start.2 = (f32[8,384]{1,0:T(8,128)S(1)}, f32[8,384]{1,0:T(8,128)S(1)}, u32[]{:S(2)}, u32[]{:S(2)}) collective-permute-start(f32[8,384]{1,0:T(8,128)S(1)} %get-tuple-element.75), channel_id=1, source_target_pairs={{0,63},{1,32},{2,33},{3,34},{4,35},{5,36},{6,37},{7,38},{8,39},{9,... | collective-permute-start | bytes 36872 | tf_op jit(solution)/shard_map/ppermute | solution.py:647
  81.7 2.8 %collective-permute-start.3 = (bf16[64,16,128]{2,1,0:T(8,128)(2,1)S(1)}, bf16[64,16,128]{2,1,0:T(8,128)(2,1)S(1)}, u32[]{:S(2)}, u32[]{:S(2)}) collective-permute-start(bf16[64,16,128]{2,1,0:T(8,128)(2,1)S(1)} %all_to_all.11.own), channel_id=1, source_target_pairs={{0,32},{32,0},{1,33},{33,1},{2,34},{34,2},{3,35},{35,3},{4,36},{36... | collective-permute-start | bytes 786440 | tf_op jit(solution)/shard_map/ppermute | solution.py:678

commit v8 on v7

--- a/solution.py
+++ b/solution.py
@@ -308,7 +308,8 @@
         else:
             build_columns(columns, split_rows(hidden), flags)
             pre = pre_total[...] + dot(flat[2], columns[...])
-        pre_total[...] = pre
+        if at < STEPS - 1:
+            pre_total[...] = pre
         gate = sigmoid(pre)
         hidden = pre * gate
         gate_one[at] = (gate + hidden - hidden * gate).astype(BF)
@@ -320,9 +321,12 @@
         gate_two[at] = (gate + hidden - hidden * gate).astype(BF)
         hidden = hidden.astype(BF)
         last_out[at] = hidden
-        change = dot(head[...], hidden)
-        total[...] += change[0:16]
-        lifted_total[...] += change[16:]
+        if at < STEPS - 1:
+            change = dot(head[...], hidden)
+            total[...] += change[0:16]
+            lifted_total[...] += change[16:]
+        else:
+            total[...] += dot(head[0:16, :], hidden)
 
     for row in range(ROWS):
         shift = jnp.where(half == 0, LON - HALO, HALO)

time: 86 us -> 86.1 us (level)
  no operation moved by 1% of the time
where the time goes in v8:
time: 86.1 us; the launch traced here: 85.8 us
  blocking collectives  42.3 us (49%)
  Pallas kernels  29.4 us (34%)
  starting transfers between devices  7.69 us (9%)
  waiting for transfers between devices  3.75 us (4%)
  local copies, waits for them, and re-layouts  1.92 us (2%)
    all_to_all x1, blocking collectives, shards(): sums = lax.all_to_all(sums, ('high', 'tile'), 0, 0, tiled=True)  16.6 us
    all_to_all x1, blocking collectives, shards(): lax.all_to_all(wire.reshape(sectors, rows, LON), 'tile', 0, 0, tiled=True)  16.3 us
    pallas_call x1, Pallas kernels, shards(): call(functools.partial(backward_kernel, scale), [((WIRE, LON), BF)], scra...  11.4 us
    all_gather x1, blocking collectives, shards(): gathered = lax.all_gather(packed, GROUP)  9.33 us
    pallas_call x1, Pallas kernels, shards(): call(forward_kernel, [((STEPS,) + shape, BF) for shape in history] + [((1...  7.48 us
    ppermute x1, starting transfers between devices, shards(): other_final = lax.ppermute(final, BOTH, partner)  5.21 us
    pallas_call x1, Pallas kernels, shards(): call(functools.partial(ocean_kernel, scale), [((8, WIN), F32), ((8, CELLS...  3.59 us
    unnamed x4, local copies, waits for them, and re-layouts  1.92 us
  transfers between devices with their start and end apart: 4, of which 3 were waited for; matrix products, arithmetic and copies ran while one was open for 0% of the time, Pallas kernels for 4%

profile of v8, /device:TPU:1, one launch (start us, length us, event | category | flops | bytes accessed | tf_op | source)
XLA Modules:
  0.0 85.8 jit_solution(1742508822487743651)
XLA Ops:
  0.6 1.6 %shard_map.153 = f32[32,384]{1,0:T(8,128)} custom-call(s32[1]{0:T(128)} %bitcast.ids, f32[8,384]{1,0:T(8,128)} %bitcast.18, f32[8,384]{1,0:T(8,128)} %bitcast.19, s32[9,1,384]{2,1,0:T(1,128)} %bitcast.17, s32[3,1,128]{2,1,0:T(1,128)} %sea.1, bf16[10,64]{1,0:T(8,128)(2,1)} %bitcast.20, bf16[12,64]{1,0:T(8,128)(2,1)} %atm_head.1, bf16[12,64]{1,0:T(8,128)(2,1)} %bitcast.21, ...), custom_call_target="tpu_custom_call" | custom-call | tf_op jit(solution)/shard_map/pallas_call | solution.py:573
  2.2 9.3 %all-gather = f32[128,384]{1,0:T(8,128)S(1)} all-gather(f32[32,384]{1,0:T(8,128)} %shard_map.153), channel_id=2, replica_groups=mesh['high'=2,'core'=2,'tile'=32] {'high','core'}, dimensions={0}, use_global_device_ids=true | all-gather | bytes 245760 | tf_op jit(solution)/shard_map/all_gather | solution.py:585
  11.5 0.3 shard_map.154
  11.9 1.1 %collective-permute-start = (f32[24,384]{1,0:T(8,128)S(1)}, f32[24,384]{1,0:T(8,128)S(1)}, u32[]{:S(2)}, u32[]{:S(2)}) collective-permute-start(f32[24,384]{1,0:T(8,128)S(1)} %get-tuple-element.50), channel_id=1, source_target_pairs={{0,63},{1,32},{2,33},{3,34},{4,35},{5,36},{6,37},{7,38},{8,39},{9,... | collective-permute-start | bytes 110600 | tf_op jit(solution)/shard_map/ppermute | solution.py:591
  12.9 1.7 %shard_map.155 = (bf16[9,384,384]{2,1,0:T(8,128)(2,1)S(1)}, bf16[3456,384]{1,0:T(8,128)(2,1)S(1)}, bf16[3,384,128]{2,1,0:T(8,128)(2,1)S(1)}) custom-call(f32[4,32,384]{2,1,0:T(8,128)S(1)} %bitcast.12), custom_call_target="tpu_custom_call" | custom-call | tf_op jit(solution)/shard_map/pallas_call | solution.py:613
  14.6 0.0 copy-start
  14.6 1.0 %copy-done = bf16[2,9,64,64]{3,2,1,0:T(8,128)(2,1)S(1)} copy-done((bf16[2,9,64,64]{3,2,1,0:T(8,128)(2,1)S(1)}, bf16[2,9,64,64]{3,2,1,0:T(8,128)(2,1)}, u32[]{:S(2)}) %copy-start) | copy-done | bytes 147480
  15.6 0.0 copy-start.1
  15.6 1.0 %copy-done.1 = bf16[2,9,64,64]{3,2,1,0:T(8,128)(2,1)S(1)} copy-done((bf16[2,9,64,64]{3,2,1,0:T(8,128)(2,1)S(1)}, bf16[2,9,64,64]{3,2,1,0:T(8,128)(2,1)}, u32[]{:S(2)}) %copy-start.1) | copy-done | bytes 147480
  16.6 0.7 shard_map.156
  17.3 0.0 collective-permute-done.strip
  17.3 7.5 %shard_map.157 = (bf16[8,16,1152]{2,1,0:T(8,128)(2,1)S(1)}, bf16[8,64,1152]{2,1,0:T(8,128)(2,1)S(1)}, bf16[8,64,1152]{2,1,0:T(8,128)(2,1)S(1)}, bf16[8,64,1152]{...) custom-call(s32[1]{0:T(128)} %bitcast.ids, ...), custom_call_target="tpu_custom_call" | custom-call | tf_op jit(solution)/shard_map/pallas_call | solution.py:618
  24.7 5.2 %collective-permute-start.1 = (f32[16,1152]{1,0:T(8,128)S(1)}, f32[16,1152]{1,0:T(8,128)S(1)}, u32[]{:S(2)}, u32[]{:S(2)}) collective-permute-start(f32[16,1152]{1,0:T(8,128)S(1)} %get-tuple-element.58.own), channel_id=1, source_target_pairs={{0,32},{1,33},{2,34},{3,35},{4,36},{5,37},{6,38},{7,39},{8,40},{9,... | collective-permute-start | bytes 221192 | tf_op jit(solution)/shard_map/ppermute | solution.py:634
  30.0 0.9 %collective-permute-done.1.other = f32[16,1152]{1,0:T(8,128)S(1)} collective-permute-done((f32[16,1152]{1,0:T(8,128)S(1)}, f32[16,1152]{1,0:T(8,128)S(1)}, u32[]{:S(2)}, u32[]{:S(2)}) %collective-permute-start.1) | collective-permute-done | bytes 73760 | tf_op jit(solution)/shard_map/ppermute | solution.py:634
  30.9 3.6 %shard_map.158 = (f32[8,1152]{1,0:T(8,128)S(1)}, f32[8,384]{1,0:T(8,128)S(1)}, bf16[2,576,384]{2,1,0:T(8,128)(2,1)S(1)}, bf16[2,64,384]{2,1,0:T(8,128)(2,1)S(1)}...) custom-call(s32[1]{0:T(128)} %bitcast.ids, f32[4,32,384]{2,1,0:T(8,128)S(1)} %bitcast.14, ...), custom_call_target="tpu_custom_call" | custom-call | tf_op jit(solution)/shard_map/pallas_call | solution.py:635
  34.5 0.0 collective-permute-start.2
  34.5 0.7 shard_map.160.source
  35.2 0.7 shard_map.159
  35.9 1.7 %collective-permute-done.2.flux_strip = f32[8,384]{1,0:T(8,128)S(1)} collective-permute-done((f32[8,384]{1,0:T(8,128)S(1)}, f32[8,384]{1,0:T(8,128)S(1)}, u32[]{:S(2)}, u32[]{:S(2)}) %collective-permute-start.2) | collective-permute-done | bytes 12320 | tf_op jit(solution)/shard_map/ppermute | solution.py:651
  37.6 11.4 %shard_map.161 = bf16[512,128]{1,0:T(8,128)(2,1)S(1)} custom-call(s32[1]{0:T(128)} %bitcast.ids, f32[16,1152]{1,0:T(8,128)S(1)} %get-tuple-element.73.window, f32[8,1152]{1,0:T(8,128)S(1)} %get-tuple-element.74.flux_own, f32[8,384]{1,0:T(8,128)S(1)} %collective-permute-done.2.flux_strip, bf16[160,128]{1,0:T(8,128)(2,1)S(1)} %get-tuple-element.76.ocean_wire, ...), custom_call_target="tpu_custom_call" | custom-call | tf_op jit(solution)/shard_map/pallas_call | solution.py:659
  49.0 16.3 %all_to_all.10.parts = bf16[32,16,128]{2,1,0:T(8,128)(2,1)S(1)} all-to-all(bf16[32,16,128]{2,1,0:T(8,128)(2,1)S(1)} %bitcast.16), channel_id=1, replica_groups=mesh['high'=2,'core'=2,'tile'=32] {'tile'}, dimensions={0} | all-to-all | bytes 262144 | tf_op jit(solution)/shard_map/all_to_all | solution.py:677
  65.3 0.1 shard_map.162
  65.4 16.6 %all_to_all.11.own = bf16[64,16,128]{2,1,0:T(8,128)(2,1)S(1)} all-to-all(bf16[64,16,128]{2,1,0:T(8,128)(2,1)S(1)} %shard_map.162), channel_id=1, replica_groups=mesh['high'=2,'core'=2,'tile'=32] {'high','tile'}, dimensions={0} | all-to-all | bytes 524288 | tf_op jit(solution)/shard_map/all_to_all | solution.py:681
  82.0 1.4 %collective-permute-start.3 = (bf16[64,16,128]{2,1,0:T(8,128)(2,1)S(1)}, bf16[64,16,128]{2,1,0:T(8,128)(2,1)S(1)}, u32[]{:S(2)}, u32[]{:S(2)}) collective-permute-start(bf16[64,16,128]{2,1,0:T(8,128)(2,1)S(1)} %all_to_all.11.own), channel_id=1, source_target_pairs={{0,32},{32,0},{1,33},{33,1},{2,34},{34,2},{3,35},{35,3},{4,36},{36... | collective-permute-start | bytes 786440 | tf_op jit(solution)/shard_map/ppermute | solution.py:682
  83.4 1.2 %collective-permute-done.3.other = bf16[64,16,128]{2,1,0:T(8,128)(2,1)S(1)} collective-permute-done((bf16[64,16,128]{2,1,0:T(8,128)(2,1)S(1)}, bf16[64,16,128]{2,1,0:T(8,128)(2,1)S(1)}, u32[]{:S(2)}, u32[]{:S(2)}) %collective-permute-start.3) | collective-permute-done | bytes 262176 | tf_op jit(solution)/shard_map/ppermute | solution.py:682
  84.6 1.2 %shard_map.163 = (f32[10,64]{1,0:T(8,128)}, f32[2,9,64,64]{3,2,1,0:T(8,128)}, f32[12,64]{1,0:T(8,128)}, f32[12,64]{1,0:T(8,128)}, f32[2,9,64,64]{3,2,1,0:T(8,128)}, /*index=5*/f32[8,64]{1,0:T(8,128)}) custom-call(s32[1]{0:T(128)} %bitcast.ids, bf16[64,16,128]{2,1,0:T(8,128)(2,1)S(1)} %all_to_all.11.own, bf16[64,16,128]{2,1,0:T(8,128)(2,1)S(1)} %collective-permute-done.3.other), custom_call_target="tpu_custom_call" | custom-call | tf_op jit(solution)/shard_map/pallas_call | solution.py:683
Async XLA Ops:
  11.9 5.4 %collective-permute-start = (f32[24,384]{1,0:T(8,128)S(1)}, f32[24,384]{1,0:T(8,128)S(1)}, u32[]{:S(2)}, u32[]{:S(2)}) collective-permute-start(f32[24,384]{1,0:T(8,128)S(1)} %get-tuple-element.50), channel_id=1, source_target_pairs={{0,63},{1,32},{2,33},{3,34},{4,35},{5,36},{6,37},{7,38},{8,39},{9,... | collective-permute-start | bytes 110600 | tf_op jit(solution)/shard_map/ppermute | solution.py:591
  14.6 1.0 %copy-start = (bf16[2,9,64,64]{3,2,1,0:T(8,128)(2,1)S(1)}, bf16[2,9,64,64]{3,2,1,0:T(8,128)(2,1)}, u32[]{:S(2)}) copy-start(bf16[2,9,64,64]{3,2,1,0:T(8,128)(2,1)} %atm_conv.1) | copy-start | bytes 442372
  15.6 1.0 %copy-start.1 = (bf16[2,9,64,64]{3,2,1,0:T(8,128)(2,1)S(1)}, bf16[2,9,64,64]{3,2,1,0:T(8,128)(2,1)}, u32[]{:S(2)}) copy-start(bf16[2,9,64,64]{3,2,1,0:T(8,128)(2,1)} %ocn_conv.1) | copy-start | bytes 442372
  24.7 6.1 %collective-permute-start.1 = (f32[16,1152]{1,0:T(8,128)S(1)}, f32[16,1152]{1,0:T(8,128)S(1)}, u32[]{:S(2)}, u32[]{:S(2)}) collective-permute-start(f32[16,1152]{1,0:T(8,128)S(1)} %get-tuple-element.58.own), channel_id=1, source_target_pairs={{0,32},{1,33},{2,34},{3,35},{4,36},{5,37},{6,38},{7,39},{8,40},{9,... | collective-permute-start | bytes 221192 | tf_op jit(solution)/shard_map/ppermute | solution.py:634
  34.5 3.1 %collective-permute-start.2 = (f32[8,384]{1,0:T(8,128)S(1)}, f32[8,384]{1,0:T(8,128)S(1)}, u32[]{:S(2)}, u32[]{:S(2)}) collective-permute-start(f32[8,384]{1,0:T(8,128)S(1)} %get-tuple-element.75), channel_id=1, source_target_pairs={{0,63},{1,32},{2,33},{3,34},{4,35},{5,36},{6,37},{7,38},{8,39},{9,... | collective-permute-start | bytes 36872 | tf_op jit(solution)/shard_map/ppermute | solution.py:651
  82.0 2.6 %collective-permute-start.3 = (bf16[64,16,128]{2,1,0:T(8,128)(2,1)S(1)}, bf16[64,16,128]{2,1,0:T(8,128)(2,1)S(1)}, u32[]{:S(2)}, u32[]{:S(2)}) collective-permute-start(bf16[64,16,128]{2,1,0:T(8,128)(2,1)S(1)} %all_to_all.11.own), channel_id=1, source_target_pairs={{0,32},{32,0},{1,33},{33,1},{2,34},{34,2},{3,35},{35,3},{4,36},{36... | collective-permute-start | bytes 786440 | tf_op jit(solution)/shard_map/ppermute | solution.py:682
